TPU v7x, 32 devices: a whole 2x2x4 slice. The times are simulated.
32 devices in a mesh: ctx: 8 (over z, x), dp: 4 (over y, core).
Axes of the slice: x: 2, y: 2, z: 4, core: 2. Of those that a mesh axis runs over, the one named last changes fastest.
Arguments:
- query: bfloat16 [4, 1024, 1024], P('dp', 'ctx')
- key: bfloat16 [4, 1024, 1024], P('dp', 'ctx')
- value: bfloat16 [4, 1024, 1024], P('dp', 'ctx'), may hold values from -5 to 5
- dout: bfloat16 [4, 1024, 1024], P('dp', 'ctx'), may hold values from -5 to 5
- glob_keys: bfloat16 [4, 64, 1024], replicated, may hold values from -5 to 5
- glob_values: bfloat16 [4, 64, 1024], replicated, may hold values from -5 to 5
- glob_ids: int32 [4, 2], P('dp'), may hold values from 0 to 3, all different within a row
- rand_blocks: int32 [8, 16, 3], replicated, may hold values from 0 to 15, as said below
Outputs:
- d_query: bfloat16 [4, 1024, 1024], P('dp', 'ctx')
- d_key: bfloat16 [4, 1024, 1024], P('dp', 'ctx')
- d_value: bfloat16 [4, 1024, 1024], P('dp', 'ctx')
- d_global: float32 [2, 4, 64, 1024], replicated
Inputs may be any that keep to these rules, and one draw needn't show every extreme that they name: With P = 8 and o_r = (r + 1) * P // 4, rand_blocks[h, i, r] lies in the span of blocks 2 * q to 2 * (q + 1) - 1, where q = (i // 2 + o_r) mod P.
All inputs are finite; a program needn't handle non-finite values.
Results may differ from a plain program's by a relative error of at most 0.015.
Values may be sent and summed in bfloat16 or wider, within the bound.
No kernel may reach another device: no remote copies, remote signals or barrier semaphores. Data moves between devices by JAX's collectives and lax.ppermute only.
A program may use at most 64 MiB of HBM per device.

v0:
```python
import math

import jax
import jax.numpy as jnp
from jax import lax
from jax.sharding import PartitionSpec as P

BLK = 64


def passed_along(shard, axis, by):
    length = lax.axis_size(axis)
    return lax.ppermute(shard, axis, [(i, (i + by) % length) for i in range(length)])


def padded(cells, sides, width):
    for axis, dim in sides:
        count = lax.axis_size(axis)
        ends = count - 1
        head = lax.slice_in_dim(cells, 0, width, axis=dim)
        tail = lax.slice_in_dim(cells, cells.shape[dim] - width, cells.shape[dim], axis=dim)
        cells = jnp.concatenate(
            [
                lax.ppermute(tail, axis, [(i, (i + 1) % count) for i in range(ends)]),
                cells,
                lax.ppermute(head, axis, [((i + 1) % count, i) for i in range(ends)]),
            ],
            axis=dim,
        )
    return cells


def passed_along_2(value, axis, steps):
    count = lax.axis_size(axis)
    leading, last = (max(0, -steps), min(count, count - steps))
    return lax.ppermute(value, axis, [(source, source + steps) for source in range(leading, last)])


def attend(
    q_head,
    o_grad,
    k_head,
    v_head,
    gk_head,
    gv_head,
    key_index,
    key_valid,
    scatter_count,
    rand_count,
):
    q_blocks = q_head.shape[0]
    head_size = q_head.shape[2]
    scaling = 1.0 / math.sqrt(head_size)
    local_lists = key_index.shape[1]
    keys_all = jnp.concatenate(
        [
            jnp.take(k_head, key_index, axis=0),
            jnp.broadcast_to(gk_head[None], (q_blocks,) + gk_head.shape),
        ],
        axis=1,
    ).reshape(q_blocks, -1, head_size)
    values_all = jnp.concatenate(
        [
            jnp.take(v_head, key_index, axis=0),
            jnp.broadcast_to(gv_head[None], (q_blocks,) + gv_head.shape),
        ],
        axis=1,
    ).reshape(q_blocks, -1, head_size)
    keep_mask = jnp.repeat(
        jnp.concatenate([key_valid, jnp.ones((q_blocks, 2), dtype=bool)], axis=1), BLK, axis=1
    )
    scores = (
        jnp.einsum("nqd,nkd->nqk", q_head, keys_all, preferred_element_type=jnp.float32) * scaling
    )
    scores = jnp.where(keep_mask[:, None, :], scores, -1e30)
    row_max = jnp.max(scores, axis=-1, keepdims=True)
    exp_scores = jnp.exp(scores - row_max)
    weights = exp_scores / jnp.sum(exp_scores, axis=-1, keepdims=True)
    weights_b = weights.astype(jnp.bfloat16)
    attn_out = jnp.einsum("nqk,nkd->nqd", weights_b, values_all, preferred_element_type=jnp.float32)
    row_dot = jnp.sum(o_grad.astype(jnp.float32) * attn_out, axis=-1, keepdims=True)
    prob_grad = jnp.einsum("nqd,nkd->nqk", o_grad, values_all, preferred_element_type=jnp.float32)
    score_grad = (weights * (prob_grad - row_dot) * scaling).astype(jnp.bfloat16)
    q_grad = jnp.einsum("nqk,nkd->nqd", score_grad, keys_all, preferred_element_type=jnp.float32)
    k_grad = jnp.einsum(
        "nqk,nqd->nkd", score_grad, q_head, preferred_element_type=jnp.float32
    ).reshape(q_blocks, local_lists + 2, BLK, head_size)
    v_grad = jnp.einsum(
        "nqk,nqd->nkd", weights_b, o_grad, preferred_element_type=jnp.float32
    ).reshape(q_blocks, local_lists + 2, BLK, head_size)
    flat_index = key_index.reshape(-1)
    k_local = (
        jnp.zeros(k_head.shape, jnp.float32)
        .at[flat_index]
        .add(k_grad[:, :scatter_count].reshape(-1, BLK, head_size))
    )
    v_local = (
        jnp.zeros(v_head.shape, jnp.float32)
        .at[flat_index]
        .add(v_grad[:, :scatter_count].reshape(-1, BLK, head_size))
    )
    grad_tiles = score_grad.reshape(q_blocks, BLK, local_lists + 2, BLK)[
        :, :, 3 : 3 + rand_count
    ].transpose(0, 2, 1, 3)
    prob_tiles = weights_b.reshape(q_blocks, BLK, local_lists + 2, BLK)[
        :, :, 3 : 3 + rand_count
    ].transpose(0, 2, 1, 3)
    return (
        q_grad,
        k_local,
        v_local,
        k_grad[:, local_lists:],
        v_grad[:, local_lists:],
        grad_tiles,
        prob_tiles,
    )


def by_heads(row_array, head_count):
    block_total = row_array.shape[0] // BLK
    return row_array.reshape(block_total, BLK, head_count, -1).transpose(2, 0, 1, 3)


def from_heads(head_array):
    head_count = head_array.shape[0]
    head_size = head_array.shape[3]
    return head_array.transpose(1, 2, 0, 3).reshape(-1, head_count * head_size)


def fetch_far(key_value, offset):
    return passed_along(key_value, "ctx", -offset)


def return_far(partials, offset):
    return passed_along(partials, "ctx", offset)


def on_device(query, key, value, dout, glob_keys, glob_values, glob_ids, rand_blocks):
    row_count = query.shape[1]
    head_count = rand_blocks.shape[0]
    rand_count = rand_blocks.shape[2]
    head_size = query.shape[2] // head_count
    per_device = row_count // BLK
    span_count = lax.axis_size("ctx")
    device_pos = lax.axis_index("ctx")
    block_count = per_device * span_count
    offsets = [(slot + 1) * span_count // (rand_count + 1) for slot in range(rand_count)]
    key_value = jnp.stack([key[0], value[0]])
    extended = padded(key_value, (("ctx", 1),), row_count)
    far_spans = [fetch_far(key_value, offset) for offset in offsets]
    k_rows = jnp.concatenate([extended[0]] + [span[0] for span in far_spans], axis=0)
    v_rows = jnp.concatenate([extended[1]] + [span[1] for span in far_spans], axis=0)
    first_block = device_pos * per_device
    key_base = first_block - per_device
    query_ids = first_block + jnp.arange(per_device, dtype=jnp.int32)
    window = query_ids[:, None] + jnp.arange(-1, 2, dtype=jnp.int32)[None, :]
    key_valid = jnp.concatenate(
        [(window >= 0) & (window < block_count), jnp.ones((per_device, rand_count), dtype=bool)],
        axis=1,
    )
    window_local = jnp.clip(window - key_base, 0, 3 * per_device - 1)
    rand_rows = lax.dynamic_slice_in_dim(rand_blocks, first_block, per_device, 1)
    offset_table = jnp.array(offsets, dtype=jnp.int32)
    far_starts = (device_pos + offset_table) % span_count * per_device
    slot_base = (3 + jnp.arange(rand_count, dtype=jnp.int32)) * per_device
    rand_local = rand_rows - far_starts[None, None, :] + slot_base[None, None, :]
    all_lists = jnp.concatenate(
        [jnp.broadcast_to(window_local[None], (head_count,) + window_local.shape), rand_local],
        axis=2,
    )
    key_index = jnp.clip(all_lists, 0, (3 + rand_count) * per_device - 1)
    chosen = glob_ids[0]
    gk_heads = by_heads(jnp.take(glob_keys, chosen, axis=0).reshape(2 * BLK, -1), head_count)
    gv_heads = by_heads(jnp.take(glob_values, chosen, axis=0).reshape(2 * BLK, -1), head_count)
    scatter_count = 3 + rand_count

    def per_head(pieces):
        q_head, o_grad, k_head, v_head, gk_head, gv_head, index_head = pieces
        return attend(
            q_head,
            o_grad,
            k_head,
            v_head,
            gk_head,
            gv_head,
            index_head,
            key_valid,
            scatter_count,
            rand_count,
        )

    results = lax.map(
        per_head,
        (
            by_heads(query[0], head_count),
            by_heads(dout[0], head_count),
            by_heads(k_rows, head_count),
            by_heads(v_rows, head_count),
            gk_heads,
            gv_heads,
            key_index,
        ),
    )
    q_grad = results[0]
    kv_grads = jnp.stack([results[1], results[2]])
    lower_part = kv_grads[:, :, :per_device]
    upper_part = kv_grads[:, :, 2 * per_device : 3 * per_device]
    from_below = passed_along_2(upper_part.astype(jnp.bfloat16), "ctx", 1).astype(upper_part.dtype)
    from_above = passed_along_2(lower_part.astype(jnp.bfloat16), "ctx", -1).astype(lower_part.dtype)
    own_grads = kv_grads[:, :, per_device : 2 * per_device] + from_below + from_above
    for slot in range(rand_count):
        start = (3 + slot) * per_device
        own_grads = own_grads + return_far(
            kv_grads[:, :, start : start + per_device], offsets[slot]
        )
    global_part = jnp.stack([jnp.sum(results[3], axis=1), jnp.sum(results[4], axis=1)])
    global_part = global_part.transpose(0, 2, 3, 1, 4).reshape(2, 2, BLK, head_count * head_size)
    one_hot = (chosen[:, None] == jnp.arange(glob_keys.shape[0], dtype=jnp.int32)[None, :]).astype(
        jnp.float32
    )
    table_term = jnp.einsum("sg,ksbd->kgbd", one_hot, global_part, precision=lax.Precision.HIGHEST)
    table_grad = lax.psum(table_term, ("ctx", "dp"))
    d_query = from_heads(q_grad).astype(jnp.bfloat16)[None]
    d_key = from_heads(own_grads[0]).astype(jnp.bfloat16)[None]
    d_value = from_heads(own_grads[1]).astype(jnp.bfloat16)[None]
    return (d_query, d_key, d_value, table_grad)


def solution(mesh):
    placed = (
        P("dp", "ctx", None),
        P("dp", "ctx", None),
        P("dp", "ctx", None),
        P("dp", "ctx", None),
        P(),
        P(),
        P("dp", None),
        P(),
    )
    return jax.shard_map(
        on_device,
        mesh=mesh,
        in_specs=placed,
        out_specs=(P("dp", "ctx", None), P("dp", "ctx", None), P("dp", "ctx", None), P()),
        check_vma=False,
    )
```

profile of v0, /device:TPU:0, one launch (start us, length us, event | category | flops | bytes accessed | tf_op | source)
XLA Modules:
  0.0 430.5 jit_solution(12351242924697786723)
XLA Ops:
  9.3 3.1 collective-permute-start.4
  12.3 2.6 collective-permute-start.3
  14.9 1.3 collective-permute-start.2
  17.6 5.3 %collective-permute-start = (bf16[2,128,1024]{2,1,0:T(8,128)(2,1)S(1)}, bf16[2,128,1024]{2,1,0:T(8,128)(2,1)}, u32[]{:S(2)}, u32[]{:S(2)}) collective-permute-start(bf16[2,128,1024]{2,1,0:T(8,128)(2,1)S(1)} %constant_dynamic-update-slice_fusion), channel_id=1, source_target_pairs={{0,4},{4,8},{8,12},{12,16},{16,20},{20,24},{24,28},{1,5},{5,9},{9,... | collective-permute-start | bytes 1572872 | tf_op jit(solution)/shard_map/ppermute | solution.py:24
  26.4 1.6 gather_fusion.2
  34.6 14.5 %collective-permute-done.3 = bf16[2,128,1024]{2,1,0:T(8,128)(2,1)} collective-permute-done((bf16[2,128,1024]{2,1,0:T(8,128)(2,1)S(1)}, bf16[2,128,1024]{2,1,0:T(8,128)(2,1)}, u32[]{:S(2)}, u32[]{:S(2)}) %collective-permute-start.3) | collective-permute-done | bytes 524320 | tf_op jit(solution)/shard_map/ppermute | solution.py:13
  50.3 3.7 maximum_bitcast_fusion
  54.6 1.6 copy.31
  56.7 1.6 copy.34
  58.3 113.2 %while.19 = (s32[]{:T(128)}, bf16[8,2,64,128]{3,2,1,0:T(8,128)(2,1)}, f32[8,12,64,128]{3,2,1,0:T(8,128)}, f32[8,12,64,128]{3,2,1,0:T(8,128)}, f32[8,2,2,64,128]{...) while((s32[]{:T(128)}, ...), condition=%wide.region_6.9_spmd.clone, body=%wide.region_0.8_spmd.clone.sunk | while | flops 102353728 | bytes 15382599 | solution.py:192
  68.0 1.3 scatter_fusion
  110.5 1.3 scatter_fusion
  111.8 1.3 scatter_fusion.1
  171.5 1.3 reduce_sum.37
  172.8 1.3 reduce_sum.36
  175.4 3.7 convolution_bitcast_fusion.1
  179.2 3.3 fusion.38
  182.5 14.2 %collective-permute-start.7 = (f32[2,8,2,64,128]{4,3,2,1,0:T(8,128)}, f32[2,8,2,64,128]{4,3,2,1,0:T(8,128)}, u32[]{:S(2)}, u32[]{:S(2)}) collective-permute-start(f32[2,8,2,64,128]{4,3,2,1,0:T(8,128)} %get-tuple-element.203), channel_id=1, source_target_pairs={{0,8},{4,12},{8,16},{12,20},{16,24},{20,28},{24,0},{28,4},{1,9},{5... | collective-permute-start | bytes 3145736 | tf_op jit(solution)/shard_map/ppermute | solution.py:13
  196.7 12.2 %collective-permute-start.8 = (f32[2,8,2,64,128]{4,3,2,1,0:T(8,128)S(1)}, f32[2,8,2,64,128]{4,3,2,1,0:T(8,128)}, u32[]{:S(2)}, u32[]{:S(2)}) collective-permute-start(f32[2,8,2,64,128]{4,3,2,1,0:T(8,128)S(1)} %get-tuple-element.204), channel_id=1, source_target_pairs={{0,16},{4,20},{8,24},{12,28},{16,0},{20,4},{24,8},{28,12},{1,17},{... | collective-permute-start | bytes 3145736 | tf_op jit(solution)/shard_map/ppermute | solution.py:13
  208.9 2.9 collective-permute-start.9
  213.3 2.6 collective-permute-start.5
  219.1 195.3 %all-reduce.2.cloned.1.call-done = f32[2,4,64,1024]{3,1,2,0:T(4,128)} async-done(((f32[2,4,64,1024]{3,1,2,0:T(4,128)}), f32[2,4,64,1024]{3,1,2,0:T(4,128)}) %all-reduce.2.cloned.1.call-update) | async-done | bytes 2097168 | tf_op jit(solution)/shard_map/psum | solution.py:222
  414.4 4.3 copy.40
  418.8 2.9 fusion.41
  (398 shorter events, 131.5 us)
Async XLA Ops:
  7.2 18.7 %copy-start = (bf16[4,64,1024]{2,1,0:T(8,128)(2,1)S(1)}, bf16[4,64,1024]{2,1,0:T(8,128)(2,1)}, u32[]{:S(2)}) copy-start(bf16[4,64,1024]{2,1,0:T(8,128)(2,1)} %param.20) | copy-start | bytes 1572868
  7.2 21.1 %copy-start.4 = (bf16[1,128,1024]{2,1,0:T(8,128)(2,1)S(1)}, bf16[1,128,1024]{2,1,0:T(8,128)(2,1)}, u32[]{:S(2)}) copy-start(bf16[1,128,1024]{2,1,0:T(8,128)(2,1)} %param.15) | copy-start | bytes 786436
  7.2 21.2 %copy-start.5 = (bf16[1,128,1024]{2,1,0:T(8,128)(2,1)S(1)}, bf16[1,128,1024]{2,1,0:T(8,128)(2,1)}, u32[]{:S(2)}) copy-start(bf16[1,128,1024]{2,1,0:T(8,128)(2,1)} %param.18) | copy-start | bytes 786436
  7.2 407.2 %all-reduce.2.cloned.1.call-start = ((), (), s32[]{:S(2)}) async-start(), calls=%async_computation | async-start | bytes 4194304 | tf_op jit(solution)/shard_map/psum | solution.py:222
  9.3 24.2 %collective-permute-start.4 = (bf16[2,128,1024]{2,1,0:T(8,128)(2,1)S(1)}, bf16[2,128,1024]{2,1,0:T(8,128)(2,1)}, u32[]{:S(2)}, u32[]{:S(2)}) collective-permute-start(bf16[2,128,1024]{2,1,0:T(8,128)(2,1)S(1)} %constant_dynamic-update-slice_fusion), channel_id=1, source_target_pairs={{0,8},{4,12},{8,16},{12,20},{16,24},{20,28},{24,0},{28,4},{1,9},{5... | collective-permute-start | bytes 1572872 | tf_op jit(solution)/shard_map/ppermute | solution.py:13
  12.3 36.7 %collective-permute-start.3 = (bf16[2,128,1024]{2,1,0:T(8,128)(2,1)S(1)}, bf16[2,128,1024]{2,1,0:T(8,128)(2,1)}, u32[]{:S(2)}, u32[]{:S(2)}) collective-permute-start(bf16[2,128,1024]{2,1,0:T(8,128)(2,1)S(1)} %constant_dynamic-update-slice_fusion), channel_id=1, source_target_pairs={{0,16},{4,20},{8,24},{12,28},{16,0},{20,4},{24,8},{28,12},{1,17},{... | collective-permute-start | bytes 1572872 | tf_op jit(solution)/shard_map/ppermute | solution.py:13
  14.9 35.3 %collective-permute-start.2 = (bf16[2,128,1024]{2,1,0:T(8,128)(2,1)S(1)}, bf16[2,128,1024]{2,1,0:T(8,128)(2,1)S(1)}, u32[]{:S(2)}, u32[]{:S(2)}) collective-permute-start(bf16[2,128,1024]{2,1,0:T(8,128)(2,1)S(1)} %constant_dynamic-update-slice_fusion), channel_id=1, source_target_pairs={{0,24},{4,28},{8,0},{12,4},{16,8},{20,12},{24,16},{28,20},{1,25},{... | collective-permute-start | bytes 1572872 | tf_op jit(solution)/shard_map/ppermute | solution.py:13
  16.3 14.8 %collective-permute-start.1 = (bf16[2,128,1024]{2,1,0:T(8,128)(2,1)S(1)}, bf16[2,128,1024]{2,1,0:T(8,128)(2,1)}, u32[]{:S(2)}, u32[]{:S(2)}) collective-permute-start(bf16[2,128,1024]{2,1,0:T(8,128)(2,1)S(1)} %constant_dynamic-update-slice_fusion), channel_id=1, source_target_pairs={{4,0},{8,4},{12,8},{16,12},{20,16},{24,20},{28,24},{5,1},{9,5},{13... | collective-permute-start | bytes 1572872 | tf_op jit(solution)/shard_map/ppermute | solution.py:26
  17.6 14.6 %collective-permute-start = (bf16[2,128,1024]{2,1,0:T(8,128)(2,1)S(1)}, bf16[2,128,1024]{2,1,0:T(8,128)(2,1)}, u32[]{:S(2)}, u32[]{:S(2)}) collective-permute-start(bf16[2,128,1024]{2,1,0:T(8,128)(2,1)S(1)} %constant_dynamic-update-slice_fusion), channel_id=1, source_target_pairs={{0,4},{4,8},{8,12},{12,16},{16,20},{20,24},{24,28},{1,5},{5,9},{9,... | collective-permute-start | bytes 1572872 | tf_op jit(solution)/shard_map/ppermute | solution.py:24
  174.2 1.3 copy-start.6
  179.2 32.6 %copy-start.1 = (f32[8,12,64,128]{3,2,1,0:T(8,128)S(1)}, f32[8,12,64,128]{3,2,1,0:T(8,128)}, u32[]{:S(2)}) copy-start(f32[8,12,64,128]{3,2,1,0:T(8,128)} %get-tuple-element.84) | copy-start | bytes 9437188
  179.2 32.6 %copy-start.3 = (f32[8,12,64,128]{3,2,1,0:T(8,128)S(1)}, f32[8,12,64,128]{3,2,1,0:T(8,128)}, u32[]{:S(2)}) copy-start(f32[8,12,64,128]{3,2,1,0:T(8,128)} %get-tuple-element.83) | copy-start | bytes 9437188
  182.5 236.2 %collective-permute-start.7 = (f32[2,8,2,64,128]{4,3,2,1,0:T(8,128)}, f32[2,8,2,64,128]{4,3,2,1,0:T(8,128)}, u32[]{:S(2)}, u32[]{:S(2)}) collective-permute-start(f32[2,8,2,64,128]{4,3,2,1,0:T(8,128)} %get-tuple-element.203), channel_id=1, source_target_pairs={{0,8},{4,12},{8,16},{12,20},{16,24},{20,28},{24,0},{28,4},{1,9},{5... | collective-permute-start | bytes 3145736 | tf_op jit(solution)/shard_map/ppermute | solution.py:13
  196.7 222.1 %collective-permute-start.8 = (f32[2,8,2,64,128]{4,3,2,1,0:T(8,128)S(1)}, f32[2,8,2,64,128]{4,3,2,1,0:T(8,128)}, u32[]{:S(2)}, u32[]{:S(2)}) collective-permute-start(f32[2,8,2,64,128]{4,3,2,1,0:T(8,128)S(1)} %get-tuple-element.204), channel_id=1, source_target_pairs={{0,16},{4,20},{8,24},{12,28},{16,0},{20,4},{24,8},{28,12},{1,17},{... | collective-permute-start | bytes 3145736 | tf_op jit(solution)/shard_map/ppermute | solution.py:13
  208.9 209.9 %collective-permute-start.9 = (f32[2,8,2,64,128]{4,3,2,1,0:T(8,128)S(1)}, f32[2,8,2,64,128]{4,3,2,1,0:T(8,128)}, u32[]{:S(2)}, u32[]{:S(2)}) collective-permute-start(f32[2,8,2,64,128]{4,3,2,1,0:T(8,128)S(1)} %get-tuple-element.205), channel_id=1, source_target_pairs={{0,24},{4,28},{8,0},{12,4},{16,8},{20,12},{24,16},{28,20},{1,25},{... | collective-permute-start | bytes 3145736 | tf_op jit(solution)/shard_map/ppermute | solution.py:13
  213.3 205.4 %collective-permute-start.5 = (bf16[2,8,2,64,128]{4,3,2,1,0:T(8,128)(2,1)}, bf16[2,8,2,64,128]{4,3,2,1,0:T(8,128)(2,1)}, u32[]{:S(2)}, u32[]{:S(2)}) collective-permute-start(bf16[2,8,2,64,128]{4,3,2,1,0:T(8,128)(2,1)} %get-tuple-element.206), channel_id=1, source_target_pairs={{0,4},{4,8},{8,12},{12,16},{16,20},{20,24},{24,28},{1,5},{5,9},{9,... | collective-permute-start | bytes 1572872 | tf_op jit(solution)/shard_map/ppermute | solution.py:36
  215.9 202.9 %collective-permute-start.6 = (bf16[2,8,2,64,128]{4,3,2,1,0:T(8,128)(2,1)S(1)}, bf16[2,8,2,64,128]{4,3,2,1,0:T(8,128)(2,1)}, u32[]{:S(2)}, u32[]{:S(2)}) collective-permute-start(bf16[2,8,2,64,128]{4,3,2,1,0:T(8,128)(2,1)S(1)} %get-tuple-element.207), channel_id=1, source_target_pairs={{4,0},{8,4},{12,8},{16,12},{20,16},{24,20},{28,24},{5,1},{9,5},{13... | collective-permute-start | bytes 1572872 | tf_op jit(solution)/shard_map/ppermute | solution.py:36
  414.4 4.3 %copy-start.2 = (f32[8,12,64,128]{3,2,1,0:T(8,128)S(1)}, f32[8,12,64,128]{3,2,1,0:T(8,128)}, u32[]{:S(2)}) copy-start(f32[8,12,64,128]{3,2,1,0:T(8,128)} %get-tuple-element.84) | copy-start | bytes 9437188
Sparse Core Ops, SparseCore 0:
  179.3 235.0 all-reduce.1
where the time goes:
time: 433 us; the launch traced here: 431 us
  waiting for transfers between devices  211 us (49%)
  local copies, waits for them, and re-layouts  66.3 us (15%)
  other arithmetic  49.1 us (11%)
  starting transfers between devices  46.8 us (11%)
  matrix products  41.2 us (10%)
  between operations  14.4 us (3%)
    psum x1, waiting for transfers between devices, on_device(): table_grad = lax.psum(table_term, ('ctx', 'dp'))  195 us
    ppermute x6, starting transfers between devices, passed_along(): lax.ppermute(shard, axis, [(i, (i + by) % length) for i in range(length)])  36.3 us
    squeeze x16, local copies, waits for them, and re-layouts, on_device(): lax.map(per_head, (by_heads(query[0], head_count), by_heads(dout[0], head...  15.1 us
    ppermute x6, waiting for transfers between devices, passed_along(): lax.ppermute(shard, axis, [(i, (i + by) % length) for i in range(length)])  14.5 us
    dynamic_update_slice x16, local copies, waits for them, and re-layouts, on_device(): lax.map(per_head, (by_heads(query[0], head_count), by_heads(dout[0], head...  13.6 us
    scatter-add x8, other arithmetic, attend(): k_local = jnp.zeros(k_head.shape, jnp.float32).at[flat_index].add(k_grad[...  10.6 us
    scatter-add x8, other arithmetic, attend(): v_local = jnp.zeros(v_head.shape, jnp.float32).at[flat_index].add(v_grad[...  10.6 us
    unnamed x29, local copies, waits for them, and re-layouts  10.6 us
  transfers between devices with their start and end apart: 11, of which 4 were waited for; matrix products, arithmetic and copies ran while one was open for 5% of the time, Pallas kernels for 0%

commit v1 on v0

--- a/solution.py
+++ b/solution.py
@@ -1,8 +1,11 @@
+import functools
 import math
 
 import jax
 import jax.numpy as jnp
 from jax import lax
+from jax.experimental import pallas as pl
+from jax.experimental.pallas import tpu as pltpu
 from jax.sharding import PartitionSpec as P
 
 BLK = 64
@@ -135,7 +138,7 @@
     return passed_along(partials, "ctx", offset)
 
 
-def on_device(query, key, value, dout, glob_keys, glob_values, glob_ids, rand_blocks):
+def on_ring(query, key, value, dout, glob_keys, glob_values, glob_ids, rand_blocks):
     row_count = query.shape[1]
     head_count = rand_blocks.shape[0]
     rand_count = rand_blocks.shape[2]
@@ -226,6 +229,304 @@
     return (d_query, d_key, d_value, table_grad)
 
 
+VMEM_BYTES = 48 * 1024 * 1024
+MASKED = -1e30
+
+
+def dot(left, right, left_dim, right_dim):
+    dims = (((left_dim,), (right_dim,)), ((), ()))
+    return lax.dot_general(left, right, dims, preferred_element_type=jnp.float32)
+
+
+def pack_kernel(q_ref, k_ref, v_ref, o_ref, out_ref):
+    head_size = out_ref.shape[3]
+    for head in range(out_ref.shape[0]):
+        columns = slice(head * head_size, (head + 1) * head_size)
+        for place, ref in enumerate((q_ref, k_ref, v_ref, o_ref)):
+            out_ref[head, place] = ref[0, :, columns]
+
+
+def pack(query, key, value, dout, head_count):
+    _, rows, width = query.shape
+    return pl.pallas_call(
+        pack_kernel,
+        out_shape=jax.ShapeDtypeStruct((head_count, 4, rows, width // head_count), query.dtype),
+        compiler_params=pltpu.CompilerParams(vmem_limit_bytes=VMEM_BYTES),
+        cost_estimate=pl.CostEstimate(flops=0, bytes_accessed=16 * rows * width, transcendentals=0),
+        name="pack_heads",
+    )(query, key, value, dout)
+
+
+def head_kernel(
+    place_ref,
+    rand_ref,
+    x_ref,
+    gk0_ref,
+    gk1_ref,
+    gv0_ref,
+    gv1_ref,
+    send_ref,
+    table_ref,
+    k_all,
+    v_all,
+    dk_all,
+    dv_all,
+    dgk,
+    dgv,
+):
+    spans, _, rows, head_size = x_ref.shape
+    rand_count = rand_ref.shape[0] // (2 * spans)
+    scaling = 1.0 / math.sqrt(head_size)
+    top = BLK + spans * rows
+    for pool in (k_all, v_all, dk_all, dv_all):
+        pool[:BLK] = jnp.zeros((BLK, head_size), pool.dtype)
+        pool[top:] = jnp.zeros((BLK, head_size), pool.dtype)
+    for pool in (dk_all, dv_all):
+        pool[BLK:top] = jnp.zeros((top - BLK, head_size), pool.dtype)
+    for span in range(spans):
+        at = BLK + span * rows
+        k_all[at : at + rows] = x_ref[span, 1]
+        v_all[at : at + rows] = x_ref[span, 2]
+    gk = [gk0_ref[0], gk1_ref[0]]
+    gv = [gv0_ref[0], gv1_ref[0]]
+    shared = 4 * BLK
+    own = (1 + rand_count) * BLK
+    first = lax.broadcasted_iota(jnp.int32, (1, rows), 1) < BLK
+    empty = jnp.zeros((BLK, head_size), x_ref.dtype)
+
+    def split(block):
+        return jnp.concatenate(
+            [
+                jnp.concatenate([block[:BLK], empty], axis=0),
+                jnp.concatenate([empty, block[BLK:]], axis=0),
+            ],
+            axis=1,
+        )
+
+    for span in range(spans):
+        at = span * rows
+        q = x_ref[span, 0]
+        o = x_ref[span, 3]
+        q_split = split(q)
+        o_split = split(o)
+        places = [
+            [
+                pl.multiple_of((rand_ref[(2 * span + half) * rand_count + slot] + 1) * BLK, BLK)
+                for slot in range(rand_count)
+            ]
+            for half in range(2)
+        ]
+
+        def gathered(pool, table):
+            window = pool[at : at + 4 * BLK]
+            lists = [
+                jnp.concatenate([edge] + [pool[pl.ds(p, BLK)] for p in places[half]], axis=0)
+                for half, edge in enumerate((window[:BLK], window[3 * BLK :]))
+            ]
+            both = jnp.concatenate([window[BLK : 3 * BLK]] + table, axis=0)
+            return jnp.concatenate(lists, axis=1), both
+
+        k_own, k_both = gathered(k_all, gk)
+        v_own, v_both = gathered(v_all, gv)
+        s_own = dot(k_own, q_split, 1, 1) * scaling
+        s_both = dot(k_both, q, 1, 1) * scaling
+        if span == 0 or span == spans - 1:
+            row = lax.broadcasted_iota(jnp.int32, (own, 1), 0) < BLK
+            outside = row & (first if span == 0 else jnp.logical_not(first))
+            s_own = jnp.where(outside, MASKED, s_own)
+        top_score = jnp.maximum(
+            jnp.max(s_own, axis=0, keepdims=True), jnp.max(s_both, axis=0, keepdims=True)
+        )
+        e_own = jnp.exp(s_own - top_score)
+        e_both = jnp.exp(s_both - top_score)
+        total = jnp.sum(e_own, axis=0, keepdims=True) + jnp.sum(e_both, axis=0, keepdims=True)
+        inverse = 1.0 / total
+        p_own = e_own * inverse
+        p_both = e_both * inverse
+        pb_own = p_own.astype(jnp.bfloat16)
+        pb_both = p_both.astype(jnp.bfloat16)
+        g_own = dot(v_own, o_split, 1, 1)
+        g_both = dot(v_both, o, 1, 1)
+        row_dot = jnp.sum(pb_own.astype(jnp.float32) * g_own, axis=0, keepdims=True) + jnp.sum(
+            pb_both.astype(jnp.float32) * g_both, axis=0, keepdims=True
+        )
+        ds_own = (p_own * (g_own - row_dot) * scaling).astype(jnp.bfloat16)
+        ds_both = (p_both * (g_both - row_dot) * scaling).astype(jnp.bfloat16)
+        wide = dot(ds_own, k_own, 0, 0)
+        dq = jnp.concatenate([wide[:BLK, :head_size], wide[BLK:, head_size:]], axis=0)
+        dq = dq + dot(ds_both, k_both, 0, 0)
+        send_ref[span, 0] = dq.astype(jnp.bfloat16)
+        for weights_own, weights_both, x_split, x, pool, table in (
+            (ds_own, ds_both, q_split, q, dk_all, dgk),
+            (pb_own, pb_both, o_split, o, dv_all, dgv),
+        ):
+            d_own = dot(weights_own, x_split, 1, 0)
+            d_both = dot(weights_both, x, 1, 0)
+            pool[at + BLK : at + 3 * BLK] += d_both[: 2 * BLK]
+            if span == 0:
+                table[...] = d_both[2 * BLK :]
+            else:
+                table[...] += d_both[2 * BLK :]
+            pool[at : at + BLK] += d_own[:BLK, :head_size]
+            pool[at + 3 * BLK : at + 4 * BLK] += d_own[:BLK, head_size:]
+            for half in range(2):
+                columns = slice(half * head_size, (half + 1) * head_size)
+                for slot, p in enumerate(places[half]):
+                    pool[pl.ds(p, BLK)] += d_own[(1 + slot) * BLK : (2 + slot) * BLK, columns]
+    for span in range(spans):
+        at = BLK + span * rows
+        send_ref[span, 1] = dk_all[at : at + rows].astype(jnp.bfloat16)
+        send_ref[span, 2] = dv_all[at : at + rows].astype(jnp.bfloat16)
+    table_ref[...] = jnp.zeros(table_ref.shape, table_ref.dtype)
+    for slot in range(2):
+        for kind, table in enumerate((dgk, dgv)):
+            table_ref[kind, place_ref[1 + slot]] = table[
+                slot * BLK : (slot + 1) * BLK
+            ].astype(table_ref.dtype)
+
+
+def attend_head(x, glob_keys, glob_values, place, rand_head):
+    spans, _, rows, head_size = x.shape
+    table_size = glob_keys.shape[0]
+    padded_rows = spans * rows + 2 * BLK
+    block = (1, BLK, head_size)
+    chosen = [
+        pl.BlockSpec(block, lambda i, place, rand: (place[1], 0, place[0])),
+        pl.BlockSpec(block, lambda i, place, rand: (place[2], 0, place[0])),
+    ]
+    whole = lambda *shape: pl.BlockSpec(shape, lambda i, place, rand: (0,) * len(shape))
+    keys_each = spans * rows * 8 * BLK
+    return pl.pallas_call(
+        head_kernel,
+        grid_spec=pltpu.PrefetchScalarGridSpec(
+            num_scalar_prefetch=2,
+            grid=(1,),
+            in_specs=[whole(*x.shape)] + chosen + chosen,
+            out_specs=[
+                whole(spans, 3, rows, head_size),
+                whole(2, table_size, BLK, head_size),
+            ],
+            scratch_shapes=[
+                pltpu.VMEM((padded_rows, head_size), jnp.bfloat16),
+                pltpu.VMEM((padded_rows, head_size), jnp.bfloat16),
+                pltpu.VMEM((padded_rows, head_size), jnp.float32),
+                pltpu.VMEM((padded_rows, head_size), jnp.float32),
+                pltpu.VMEM((2 * BLK, head_size), jnp.float32),
+                pltpu.VMEM((2 * BLK, head_size), jnp.float32),
+            ],
+        ),
+        out_shape=[
+            jax.ShapeDtypeStruct((spans, 3, rows, head_size), jnp.bfloat16),
+            jax.ShapeDtypeStruct((2, table_size, BLK, head_size), jnp.bfloat16),
+        ],
+        compiler_params=pltpu.CompilerParams(vmem_limit_bytes=VMEM_BYTES),
+        cost_estimate=pl.CostEstimate(
+            flops=10 * keys_each * head_size,
+            bytes_accessed=16 * spans * rows * head_size,
+            transcendentals=keys_each,
+        ),
+        name="attend_head",
+    )(place, rand_head, x, glob_keys, glob_keys, glob_values, glob_values)
+
+
+def unpack_kernel(x_ref, dq_ref, dk_ref, dv_ref):
+    head_size = x_ref.shape[3]
+    for head in range(x_ref.shape[0]):
+        columns = slice(head * head_size, (head + 1) * head_size)
+        for place, ref in enumerate((dq_ref, dk_ref, dv_ref)):
+            ref[0, :, columns] = x_ref[head, place]
+
+
+def unpack(x):
+    heads, _, rows, head_size = x.shape
+    shape = jax.ShapeDtypeStruct((1, rows, heads * head_size), x.dtype)
+    return pl.pallas_call(
+        unpack_kernel,
+        grid=(1,),
+        in_specs=[pl.BlockSpec((heads, 3, rows, head_size), lambda i: (0, 0, 0, 0))],
+        out_specs=[pl.BlockSpec(shape.shape, lambda i: (0, 0, 0))] * 3,
+        out_shape=[shape] * 3,
+        compiler_params=pltpu.CompilerParams(vmem_limit_bytes=VMEM_BYTES),
+        cost_estimate=pl.CostEstimate(
+            flops=0, bytes_accessed=12 * rows * heads * head_size, transcendentals=0
+        ),
+        name="unpack_heads",
+    )(x)
+
+
+def table_kernel(place_ref, *refs):
+    parts, out_ref = refs[:-1], refs[-1]
+    head_size = parts[0].shape[2]
+    for flip, ref in enumerate(parts):
+        at = place_ref[0] ^ flip
+        for head in range(ref.shape[0]):
+            columns = slice(head * head_size, (head + 1) * head_size)
+            out_ref[at, :, columns] = ref[head].astype(out_ref.dtype)
+
+
+def whole_table(me, parts):
+    heads, rows, head_size = parts[0].shape
+    shape = (len(parts), rows, heads * head_size)
+    part = pl.BlockSpec(parts[0].shape, lambda i, me: (0, 0, 0))
+    return pl.pallas_call(
+        table_kernel,
+        grid_spec=pltpu.PrefetchScalarGridSpec(
+            num_scalar_prefetch=1,
+            grid=(1,),
+            in_specs=[part] * len(parts),
+            out_specs=pl.BlockSpec(shape, lambda i, me: (0, 0, 0)),
+        ),
+        out_shape=jax.ShapeDtypeStruct(shape, jnp.float32),
+        compiler_params=pltpu.CompilerParams(vmem_limit_bytes=VMEM_BYTES),
+        name="whole_table",
+    )(me, *parts)
+
+
+def flipped(array, axis, bits):
+    length = lax.axis_size(axis)
+    return lax.ppermute(array, axis, [(i, i ^ bits) for i in range(length)])
+
+
+def on_heads(query, key, value, dout, glob_keys, glob_values, glob_ids, rand_blocks):
+    head_count, block_count, _ = rand_blocks.shape
+    rows = query.shape[1]
+    head_size = query.shape[2] // head_count
+    table_size = glob_keys.shape[0]
+    dp_count = lax.axis_size("dp")
+    head = lax.axis_index("ctx")
+    place = jnp.concatenate([head[None].astype(jnp.int32), glob_ids[0]])
+    rand_head = lax.dynamic_index_in_dim(rand_blocks, head, 0, keepdims=False).reshape(-1)
+    rand_head = jnp.clip(rand_head, 0, block_count - 1)
+    packed = pack(query, key, value, dout, head_count)
+    arrived = lax.all_to_all(packed, "ctx", 0, 0)
+    grads, table = attend_head(arrived, glob_keys, glob_values, place, rand_head)
+    shares = table.reshape(dp_count, -1, head_size)
+    shares = lax.all_to_all(shares, "dp", 0, 0)
+    share = jnp.sum(shares.astype(jnp.float32), axis=0).astype(jnp.bfloat16)
+    share = jnp.broadcast_to(share.reshape(1, -1, rows, head_size), (head_count, 1, rows, head_size))
+    back = lax.all_to_all(jnp.concatenate([grads, share], axis=1), "ctx", 0, 0)
+    d_query, d_key, d_value = unpack(back)
+    quarter = back[:, 3]
+    beside = flipped(quarter, "dp", 1)
+    across = flipped(quarter, "dp", 2)
+    corner = flipped(across, "dp", 1)
+    me = lax.axis_index("dp").astype(jnp.int32)[None]
+    d_table = whole_table(me, [quarter, beside, across, corner])
+    return (d_query, d_key, d_value, d_table.reshape((2,) + glob_keys.shape))
+
+
+def on_device(query, key, value, dout, glob_keys, glob_values, glob_ids, rand_blocks):
+    head_count = rand_blocks.shape[0]
+    rows = query.shape[1]
+    one_head_each = lax.axis_size("ctx") == head_count and rows == 2 * BLK
+    shared_table = 2 * glob_keys.shape[0] * BLK == lax.axis_size("dp") * rows
+    if one_head_each and shared_table and lax.axis_size("dp") == 4:
+        plan = on_heads
+    else:
+        plan = on_ring
+    return plan(query, key, value, dout, glob_keys, glob_values, glob_ids, rand_blocks)
+
+
 def solution(mesh):
     placed = (
         P("dp", "ctx", None),

time: 433 us -> 90.4 us (0.21)
  waiting for transfers between devices: 211 us -> 32.1 us
  local copies, waits for them, and re-layouts: 66.3 us -> 4.11 us
  other arithmetic: 49.1 us -> 0.2 us
  matrix products: 41.2 us -> 0 us
  starting transfers between devices: 46.8 us -> 8.09 us
  blocking collectives: 0 us -> 36.1 us
  between operations: 14.4 us -> 0.73 us
  Pallas kernels: 0 us -> 8.77 us
    psum x1 -> x0, waiting for transfers between devices: 195 us -> none  [on_device(): table_grad = lax.psum(table_term, ('ctx', 'dp'))]
    ppermute x10 -> x3, starting transfers between devices: 46.8 us -> 0.84 us  [flipped(): return lax.ppermute(array, axis, [(i, i ^ bits) for i in range(length)])]
    dot_general x49 -> x0, matrix products: 41.2 us -> none  [the longest x8 9.79 us: attend(): jnp.einsum('nqk,nkd->nqd', weights_b, values_all, preferred_element_type=...]
    all_to_all x0 -> x2, blocking collectives: none -> 36.1 us  [the longest x1 28.8 us: on_heads(): back = lax.all_to_all(jnp.concatenate([grads, share], axis=1), 'ctx', 0, 0)]
    all_to_all x0 -> x1, waiting for transfers between devices: none -> 25.5 us  [on_heads(): arrived = lax.all_to_all(packed, 'ctx', 0, 0)]
    scatter-add x16 -> x0, other arithmetic: 21.2 us -> none  [the longest x8 10.6 us: attend(): k_local = jnp.zeros(k_head.shape, jnp.float32).at[flat_index].add(k_grad[...]
    squeeze x20 -> x1, local copies, waits for them, and re-layouts: 17.4 us -> 0.02 us  [on_heads(): quarter = back[:, 3]]
    dynamic_update_slice x16 -> x0, local copies, waits for them, and re-layouts: 13.6 us -> none  [on_device(): lax.map(per_head, (by_heads(query[0], head_count), by_heads(dout[0], head...]
  transfers between devices with their start and end apart: 11 -> 4, of which waited for: 4 -> 3; matrix products, arithmetic and copies ran while one was open for 5% -> 0% of each run, Pallas kernels for 0% -> 1%
where the time goes in v1:
time: 90.4 us; the launch traced here: 90 us
  blocking collectives  36.1 us (40%)
  waiting for transfers between devices  32.1 us (36%)
  Pallas kernels  8.77 us (10%)
  starting transfers between devices  8.09 us (9%)
  local copies, waits for them, and re-layouts  4.11 us (5%)
    all_to_all x1, blocking collectives, on_heads(): back = lax.all_to_all(jnp.concatenate([grads, share], axis=1), 'ctx', 0, 0)  28.8 us
    all_to_all x1, waiting for transfers between devices, on_heads(): arrived = lax.all_to_all(packed, 'ctx', 0, 0)  25.5 us
    all_to_all x1, starting transfers between devices, on_heads(): arrived = lax.all_to_all(packed, 'ctx', 0, 0)  7.25 us
    all_to_all x1, blocking collectives, on_heads(): shares = lax.all_to_all(shares, 'dp', 0, 0)  7.23 us
    ppermute x3, waiting for transfers between devices, flipped(): return lax.ppermute(array, axis, [(i, i ^ bits) for i in range(length)])  6.59 us
    pallas_call x1, Pallas kernels, attend_head(): pl.pallas_call(head_kernel, grid_spec=pltpu.PrefetchScalarGridSpec(num_sc...  5.03 us
    unnamed x16, local copies, waits for them, and re-layouts  3.87 us
  transfers between devices with their start and end apart: 4, of which 3 were waited for; matrix products, arithmetic and copies ran while one was open for 0% of the time, Pallas kernels for 1%

profile of v1, /device:TPU:0, one launch (start us, length us, event | category | flops | bytes accessed | tf_op | source)
XLA Modules:
  0.0 90.0 jit_solution(14104760930953778413)
XLA Ops:
  0.6 0.0 copy-start
  0.6 0.0 copy-start.2
  0.7 1.0 %copy-done.3 = bf16[1,128,1024]{2,1,0:T(8,128)(2,1)S(1)} copy-done((bf16[1,128,1024]{2,1,0:T(8,128)(2,1)S(1)}, bf16[1,128,1024]{2,1,0:T(8,128)(2,1)}, u32[]{:S(2)}) %copy-start.3) | copy-done | bytes 262168
  1.7 0.9 %copy-done.4 = bf16[1,128,1024]{2,1,0:T(8,128)(2,1)S(1)} copy-done((bf16[1,128,1024]{2,1,0:T(8,128)(2,1)S(1)}, bf16[1,128,1024]{2,1,0:T(8,128)(2,1)}, u32[]{:S(2)}) %copy-start.4) | copy-done | bytes 262168
  2.6 0.9 %copy-done.5 = bf16[1,128,1024]{2,1,0:T(8,128)(2,1)S(1)} copy-done((bf16[1,128,1024]{2,1,0:T(8,128)(2,1)S(1)}, bf16[1,128,1024]{2,1,0:T(8,128)(2,1)}, u32[]{:S(2)}) %copy-start.5) | copy-done | bytes 262168
  3.6 0.9 %copy-done.6 = bf16[1,128,1024]{2,1,0:T(8,128)(2,1)S(1)} copy-done((bf16[1,128,1024]{2,1,0:T(8,128)(2,1)S(1)}, bf16[1,128,1024]{2,1,0:T(8,128)(2,1)}, u32[]{:S(2)}) %copy-start.6) | copy-done | bytes 262168
  4.5 1.2 %pack_heads.1 = bf16[8,4,128,128]{3,2,1,0:T(8,128)(2,1)} custom-call(bf16[1,128,1024]{2,1,0:T(8,128)(2,1)S(1)} %copy-done.3, bf16[1,128,1024]{2,1,0:T(8,128)(2,1)S(1)} %copy-done.4, bf16[1,128,1024]{2,1,0:T(8,128)(2,1)S(1)} %copy-done.5, bf16[1,128,1024]{2,1,0:T(8,128)(2,1)S(1)} %copy-done.6), custom_call_target="tpu_custom_call" | custom-call | bytes 2097152 | tf_op jit(solution)/shard_map/pack_heads/pallas_call | solution.py:251
  5.7 7.3 %all-to-all-start = ((bf16[8,4,128,128]{3,2,1,0:T(8,128)(2,1)}), bf16[8,4,128,128]{3,2,1,0:T(8,128)(2,1)S(1)}, u32[]{:S(2)}, u32[]{:S(2)}) async-start(bf16[8,4,128,128]{3,2,1,0:T(8,128)(2,1)} %pack_heads.1), calls=%async_computation | async-start | bytes 2097152 | tf_op jit(solution)/shard_map/all_to_all | solution.py:501
  13.0 0.1 copy.21
  13.1 0.1 min.12.rand_ref
  13.2 0.1 pad_add_fusion.place_ref
  13.2 25.5 %all-to-all-done.x_ref = bf16[8,4,128,128]{3,2,1,0:T(8,128)(2,1)S(1)} async-done(((bf16[8,4,128,128]{3,2,1,0:T(8,128)(2,1)}), bf16[8,4,128,128]{3,2,1,0:T(8,128)(2,1)S(1)}, u32[]{:S(2)}, u32[]{:S(2)}) %all-to-all-start) | async-done | bytes 1048608 | tf_op jit(solution)/shard_map/all_to_all | solution.py:501
  38.7 5.0 %attend_head.1 = (bf16[8,3,128,128]{3,2,1,0:T(8,128)(2,1)S(1)}, bf16[2,4,64,128]{3,2,1,0:T(8,128)(2,1)S(1)}) custom-call(s32[3]{0:T(128)S(1)} %pad_add_fusion.place_ref, s32[48]{0:T(128)S(1)} %min.12.rand_ref, bf16[8,4,128,128]{3,2,1,0:T(8,128)(2,1)S(1)} %all-to-all-done.x_ref, bf16[4,64,1024]{2,1,0:T(8,128)(2,1)S(1)} %copy-done.1, ...), custom_call_target="tpu_custom_call" | custom-call | flops 671088640 | bytes 2097152 | tf_op jit(solution)/shard_map/attend_head/pallas_call | solution.py:399
  43.8 7.2 %all_to_all.15 = bf16[4,128,128]{2,1,0:T(8,128)(2,1)S(1)} all-to-all(bf16[4,128,128]{2,1,0:T(8,128)(2,1)S(1)} %bitcast.9), channel_id=1, replica_groups=mesh['ctx'=8,'dp'=4] {'dp'}, dimensions={0} | all-to-all | bytes 262144 | tf_op jit(solution)/shard_map/all_to_all | solution.py:504
  51.0 0.1 pad_maximum_fusion
  51.1 28.8 %all_to_all.16.x_ref = bf16[8,4,128,128]{3,2,1,0:T(8,128)(2,1)S(1)} all-to-all(bf16[8,4,128,128]{3,2,1,0:T(8,128)(2,1)S(1)} %pad_maximum_fusion), channel_id=1, replica_groups=mesh['ctx'=8,'dp'=4] {'ctx'}, dimensions={0} | all-to-all | bytes 2097152 | tf_op jit(solution)/shard_map/all_to_all | solution.py:507
  80.0 0.8 collective-permute-start.1
  80.8 0.0 collective-permute-start
  80.9 6.1 %collective-permute-done.1.refs_2_ = bf16[8,128,128]{2,1,0:T(8,128)(2,1)S(1)} collective-permute-done((bf16[8,128,128]{2,1,0:T(8,128)(2,1)S(1)}, bf16[8,128,128]{2,1,0:T(8,128)(2,1)S(1)}, u32[]{:S(2)}, u32[]{:S(2)}) %collective-permute-start.1) | collective-permute-done | bytes 262176 | tf_op jit(solution)/shard_map/ppermute | solution.py:487
  87.0 0.0 collective-permute-start.2
  87.0 1.1 %unpack_heads.1 = (bf16[1,128,1024]{2,1,0:T(8,128)(2,1)}, bf16[1,128,1024]{2,1,0:T(8,128)(2,1)}, bf16[1,128,1024]{2,1,0:T(8,128)(2,1)}) custom-call(bf16[8,4,128,128]{3,2,1,0:T(8,128)(2,1)S(1)} %all_to_all.16.x_ref), custom_call_target="tpu_custom_call" | custom-call | bytes 1572864 | tf_op jit(solution)/shard_map/unpack_heads/pallas_call | solution.py:443
  88.0 0.0 collective-permute-done.refs_1_
  88.0 0.5 collective-permute-done.2.refs_3_
  88.5 1.5 %whole_table.1 = f32[4,128,1024]{2,1,0:T(8,128)} custom-call(s32[1]{0:T(128)} %bitcast.3.place_ref, bf16[8,128,128]{2,1,0:T(8,128)(2,1)S(1)} %slice_bitcast_fusion.refs_0_, bf16[8,128,128]{2,1,0:T(8,128)(2,1)S(1)} %collective-permute-done.refs_1_, bf16[8,128,128]{2,1,0:T(8,128)(2,1)S(1)} %collective-permute-done.1.refs_2_, ...), custom_call_target="tpu_custom_call" | custom-call | tf_op jit(solution)/shard_map/whole_table/pallas_call | solution.py:471
  (15 shorter events, 0.1 us)
Async XLA Ops:
  0.6 12.3 %copy-start = (s32[8,16,3]{1,0,2:T(8,128)S(1)}, s32[8,16,3]{1,0,2:T(8,128)}, u32[]{:S(2)}) copy-start(s32[8,16,3]{1,0,2:T(8,128)} %param.15) | copy-start | bytes 4612
  0.6 38.1 %copy-start.2 = (bf16[4,64,1024]{2,1,0:T(8,128)(2,1)S(1)}, bf16[4,64,1024]{2,1,0:T(8,128)(2,1)}, u32[]{:S(2)}) copy-start(bf16[4,64,1024]{2,1,0:T(8,128)(2,1)} %gv1_ref.1) | copy-start | bytes 1572868
  0.7 1.0 %copy-start.3 = (bf16[1,128,1024]{2,1,0:T(8,128)(2,1)S(1)}, bf16[1,128,1024]{2,1,0:T(8,128)(2,1)}, u32[]{:S(2)}) copy-start(bf16[1,128,1024]{2,1,0:T(8,128)(2,1)} %q_ref.1) | copy-start | bytes 786436
  1.7 0.9 %copy-start.4 = (bf16[1,128,1024]{2,1,0:T(8,128)(2,1)S(1)}, bf16[1,128,1024]{2,1,0:T(8,128)(2,1)}, u32[]{:S(2)}) copy-start(bf16[1,128,1024]{2,1,0:T(8,128)(2,1)} %k_ref.1) | copy-start | bytes 786436
  2.6 0.9 %copy-start.5 = (bf16[1,128,1024]{2,1,0:T(8,128)(2,1)S(1)}, bf16[1,128,1024]{2,1,0:T(8,128)(2,1)}, u32[]{:S(2)}) copy-start(bf16[1,128,1024]{2,1,0:T(8,128)(2,1)} %v_ref.1) | copy-start | bytes 786436
  3.6 0.9 %copy-start.6 = (bf16[1,128,1024]{2,1,0:T(8,128)(2,1)S(1)}, bf16[1,128,1024]{2,1,0:T(8,128)(2,1)}, u32[]{:S(2)}) copy-start(bf16[1,128,1024]{2,1,0:T(8,128)(2,1)} %o_ref.1) | copy-start | bytes 786436
  4.5 8.6 %copy-start.7 = (s32[1,2]{1,0:T(1,128)S(1)}, s32[1,2]{1,0:T(1,128)}, u32[]{:S(2)}) copy-start(s32[1,2]{1,0:T(1,128)} %param.14) | copy-start | bytes 28
  4.5 34.2 %copy-start.1 = (bf16[4,64,1024]{2,1,0:T(8,128)(2,1)S(1)}, bf16[4,64,1024]{2,1,0:T(8,128)(2,1)}, u32[]{:S(2)}) copy-start(bf16[4,64,1024]{2,1,0:T(8,128)(2,1)} %gk1_ref.1) | copy-start | bytes 1572868
  5.7 33.0 %all-to-all-start = ((bf16[8,4,128,128]{3,2,1,0:T(8,128)(2,1)}), bf16[8,4,128,128]{3,2,1,0:T(8,128)(2,1)S(1)}, u32[]{:S(2)}, u32[]{:S(2)}) async-start(bf16[8,4,128,128]{3,2,1,0:T(8,128)(2,1)} %pack_heads.1), calls=%async_computation | async-start | bytes 2097152 | tf_op jit(solution)/shard_map/all_to_all | solution.py:501
  80.0 6.9 %collective-permute-start.1 = (bf16[8,128,128]{2,1,0:T(8,128)(2,1)S(1)}, bf16[8,128,128]{2,1,0:T(8,128)(2,1)S(1)}, u32[]{:S(2)}, u32[]{:S(2)}) collective-permute-start(bf16[8,128,128]{2,1,0:T(8,128)(2,1)S(1)} %slice_bitcast_fusion.refs_0_), channel_id=1, source_target_pairs={{0,2},{1,3},{2,0},{3,1},{4,6},{5,7},{6,4},{7,5},{8,10},{9,11},{10,... | collective-permute-start | bytes 786440 | tf_op jit(solution)/shard_map/ppermute | solution.py:487
  80.8 7.2 %collective-permute-start = (bf16[8,128,128]{2,1,0:T(8,128)(2,1)S(1)}, bf16[8,128,128]{2,1,0:T(8,128)(2,1)S(1)}, u32[]{:S(2)}, u32[]{:S(2)}) collective-permute-start(bf16[8,128,128]{2,1,0:T(8,128)(2,1)S(1)} %slice_bitcast_fusion.refs_0_), channel_id=1, source_target_pairs={{0,1},{1,0},{2,3},{3,2},{4,5},{5,4},{6,7},{7,6},{8,9},{9,8},{10,11... | collective-permute-start | bytes 786440 | tf_op jit(solution)/shard_map/ppermute | solution.py:487
  87.0 1.5 %collective-permute-start.2 = (bf16[8,128,128]{2,1,0:T(8,128)(2,1)S(1)}, bf16[8,128,128]{2,1,0:T(8,128)(2,1)S(1)}, u32[]{:S(2)}, u32[]{:S(2)}) collective-permute-start(bf16[8,128,128]{2,1,0:T(8,128)(2,1)S(1)} %collective-permute-done.1.refs_2_), channel_id=1, source_target_pairs={{0,1},{1,0},{2,3},{3,2},{4,5},{5,4},{6,7},{7,6},{8,9},{9,8},{10,11... | collective-permute-start | bytes 786440 | tf_op jit(solution)/shard_map/ppermute | solution.py:487

commit v2 on v1

--- a/solution.py
+++ b/solution.py
@@ -229,8 +229,12 @@
     return (d_query, d_key, d_value, table_grad)
 
 
-VMEM_BYTES = 48 * 1024 * 1024
+VMEM_BYTES = 24 * 1024 * 1024
+SMALL_VMEM_BYTES = 4 * 1024 * 1024
+LARGE_VMEM_BYTES = 60 * 1024 * 1024
 MASKED = -1e30
+ORDER = (0, 2, 4, 5, 3, 6, 7, 1)
+HEADS_ORDER = (0, 2, 4, 6, 1, 3, 5, 7)
 
 
 def dot(left, right, left_dim, right_dim):
@@ -238,61 +242,116 @@
     return lax.dot_general(left, right, dims, preferred_element_type=jnp.float32)
 
 
-def pack_kernel(q_ref, k_ref, v_ref, o_ref, out_ref):
-    head_size = out_ref.shape[3]
-    for head in range(out_ref.shape[0]):
-        columns = slice(head * head_size, (head + 1) * head_size)
-        for place, ref in enumerate((q_ref, k_ref, v_ref, o_ref)):
-            out_ref[head, place] = ref[0, :, columns]
+def in_vmem(count):
+    return [pl.BlockSpec(memory_space=pltpu.VMEM)] * count
+
+
+def pack_kernel(count, *refs):
+    ins, outs = refs[:4], refs[4 : 4 + count]
+    held, made, in_sems, out_sems = refs[4 + count :]
+    head_size = made.shape[3]
+    me = lax.axis_index("ctx")
+    loads = [
+        pltpu.make_async_copy(ref.at[0], held.at[place], in_sems.at[place])
+        for place, ref in enumerate(ins)
+    ]
+    for load in loads:
+        load.start()
+    for load in loads:
+        load.wait()
+    stores = []
+    for flip in ORDER:
+        at = pl.multiple_of((me ^ flip) * head_size, head_size)
+        made[flip] = held[:, :, pl.ds(at, head_size)]
+        store = pltpu.make_async_copy(made.at[flip], outs[flip], out_sems.at[flip])
+        store.start()
+        stores.append(store)
+    for store in stores:
+        store.wait()
 
 
 def pack(query, key, value, dout, head_count):
     _, rows, width = query.shape
+    chunk = (4, rows, width // head_count)
+    in_hbm = pl.BlockSpec(memory_space=pltpu.HBM)
     return pl.pallas_call(
-        pack_kernel,
-        out_shape=jax.ShapeDtypeStruct((head_count, 4, rows, width // head_count), query.dtype),
-        compiler_params=pltpu.CompilerParams(vmem_limit_bytes=VMEM_BYTES),
+        functools.partial(pack_kernel, head_count),
+        in_specs=[in_hbm] * 4,
+        out_specs=[in_hbm] * head_count,
+        out_shape=[jax.ShapeDtypeStruct(chunk, query.dtype)] * head_count,
+        scratch_shapes=[
+            pltpu.VMEM((4, rows, width), query.dtype),
+            pltpu.VMEM((head_count,) + chunk, query.dtype),
+            pltpu.SemaphoreType.DMA((4,)),
+            pltpu.SemaphoreType.DMA((head_count,)),
+        ],
+        compiler_params=pltpu.CompilerParams(vmem_limit_bytes=LARGE_VMEM_BYTES),
         cost_estimate=pl.CostEstimate(flops=0, bytes_accessed=16 * rows * width, transcendentals=0),
         name="pack_heads",
     )(query, key, value, dout)
 
 
-def head_kernel(
-    place_ref,
-    rand_ref,
-    x_ref,
-    gk0_ref,
-    gk1_ref,
-    gv0_ref,
-    gv1_ref,
-    send_ref,
-    table_ref,
-    k_all,
-    v_all,
-    dk_all,
-    dv_all,
-    dgk,
-    dgv,
-):
-    spans, _, rows, head_size = x_ref.shape
+def choose_kernel(place_ref, gk_ref, gv_ref, out_ref, sems):
+    head_size = out_ref.shape[2]
+    columns = pl.ds(pl.multiple_of(place_ref[0] * head_size, head_size), head_size)
+    copies = [
+        pltpu.make_async_copy(
+            ref.at[place_ref[2 + slot], :, columns],
+            out_ref.at[2 * kind + slot],
+            sems.at[2 * kind + slot],
+        )
+        for kind, ref in enumerate((gk_ref, gv_ref))
+        for slot in range(2)
+    ]
+    for copy in copies:
+        copy.start()
+    for copy in copies:
+        copy.wait()
+
+
+def choose(place, glob_keys, glob_values, head_size):
+    return pl.pallas_call(
+        choose_kernel,
+        in_specs=[pl.BlockSpec(memory_space=pltpu.SMEM)]
+        + [pl.BlockSpec(memory_space=pltpu.HBM)] * 2,
+        out_specs=pl.BlockSpec(memory_space=pltpu.VMEM),
+        out_shape=jax.ShapeDtypeStruct((4, BLK, head_size), glob_keys.dtype),
+        scratch_shapes=[pltpu.SemaphoreType.DMA((4,))],
+        compiler_params=pltpu.CompilerParams(vmem_limit_bytes=SMALL_VMEM_BYTES),
+        cost_estimate=pl.CostEstimate(
+            flops=0, bytes_accessed=16 * BLK * head_size, transcendentals=0
+        ),
+        name="choose_blocks",
+    )(place, glob_keys, glob_values)
+
+
+def head_kernel(spans, shares, place_ref, rand_ref, *refs):
+    x_refs, g_ref, send_ref = refs[:spans], refs[spans], refs[spans + 1]
+    share_refs = refs[spans + 2 : spans + 2 + shares]
+    q_all, k_all, v_all, o_all, dk_all, dv_all, dgk, dgv, table = refs[
+        spans + 2 + shares :
+    ]
+    _, rows, head_size = x_refs[0].shape
     rand_count = rand_ref.shape[0] // (2 * spans)
     scaling = 1.0 / math.sqrt(head_size)
+    me = place_ref[0]
     top = BLK + spans * rows
     for pool in (k_all, v_all, dk_all, dv_all):
         pool[:BLK] = jnp.zeros((BLK, head_size), pool.dtype)
         pool[top:] = jnp.zeros((BLK, head_size), pool.dtype)
     for pool in (dk_all, dv_all):
         pool[BLK:top] = jnp.zeros((top - BLK, head_size), pool.dtype)
-    for span in range(spans):
-        at = BLK + span * rows
-        k_all[at : at + rows] = x_ref[span, 1]
-        v_all[at : at + rows] = x_ref[span, 2]
-    gk = [gk0_ref[0], gk1_ref[0]]
-    gv = [gv0_ref[0], gv1_ref[0]]
-    shared = 4 * BLK
+    starts = [pl.multiple_of((me ^ flip) * rows, rows) for flip in ORDER]
+    for at, ref in zip(starts, x_refs):
+        q_all[pl.ds(at, rows)] = ref[0]
+        k_all[pl.ds(pl.multiple_of(at + BLK, BLK), rows)] = ref[1]
+        v_all[pl.ds(pl.multiple_of(at + BLK, BLK), rows)] = ref[2]
+        o_all[pl.ds(at, rows)] = ref[3]
+    gk = [g_ref[0], g_ref[1]]
+    gv = [g_ref[2], g_ref[3]]
     own = (1 + rand_count) * BLK
     first = lax.broadcasted_iota(jnp.int32, (1, rows), 1) < BLK
-    empty = jnp.zeros((BLK, head_size), x_ref.dtype)
+    empty = jnp.zeros((BLK, head_size), jnp.bfloat16)
 
     def split(block):
         return jnp.concatenate(
@@ -305,8 +364,8 @@
 
     for span in range(spans):
         at = span * rows
-        q = x_ref[span, 0]
-        o = x_ref[span, 3]
+        q = q_all[at : at + rows]
+        o = o_all[at : at + rows]
         q_split = split(q)
         o_split = split(o)
         places = [
@@ -317,13 +376,13 @@
             for half in range(2)
         ]
 
-        def gathered(pool, table):
+        def gathered(pool, table_blocks):
             window = pool[at : at + 4 * BLK]
             lists = [
                 jnp.concatenate([edge] + [pool[pl.ds(p, BLK)] for p in places[half]], axis=0)
                 for half, edge in enumerate((window[:BLK], window[3 * BLK :]))
             ]
-            both = jnp.concatenate([window[BLK : 3 * BLK]] + table, axis=0)
+            both = jnp.concatenate([window[BLK : 3 * BLK]] + table_blocks, axis=0)
             return jnp.concatenate(lists, axis=1), both
 
         k_own, k_both = gathered(k_all, gk)
@@ -354,9 +413,8 @@
         ds_both = (p_both * (g_both - row_dot) * scaling).astype(jnp.bfloat16)
         wide = dot(ds_own, k_own, 0, 0)
         dq = jnp.concatenate([wide[:BLK, :head_size], wide[BLK:, head_size:]], axis=0)
-        dq = dq + dot(ds_both, k_both, 0, 0)
-        send_ref[span, 0] = dq.astype(jnp.bfloat16)
-        for weights_own, weights_both, x_split, x, pool, table in (
+        send_ref[span, 0] = (dq + dot(ds_both, k_both, 0, 0)).astype(jnp.bfloat16)
+        for weights_own, weights_both, x_split, x, pool, shared in (
             (ds_own, ds_both, q_split, q, dk_all, dgk),
             (pb_own, pb_both, o_split, o, dv_all, dgv),
         ):
@@ -364,9 +422,9 @@
             d_both = dot(weights_both, x, 1, 0)
             pool[at + BLK : at + 3 * BLK] += d_both[: 2 * BLK]
             if span == 0:
-                table[...] = d_both[2 * BLK :]
+                shared[...] = d_both[2 * BLK :]
             else:
-                table[...] += d_both[2 * BLK :]
+                shared[...] += d_both[2 * BLK :]
             pool[at : at + BLK] += d_own[:BLK, :head_size]
             pool[at + 3 * BLK : at + 4 * BLK] += d_own[:BLK, head_size:]
             for half in range(2):
@@ -377,47 +435,40 @@
         at = BLK + span * rows
         send_ref[span, 1] = dk_all[at : at + rows].astype(jnp.bfloat16)
         send_ref[span, 2] = dv_all[at : at + rows].astype(jnp.bfloat16)
-    table_ref[...] = jnp.zeros(table_ref.shape, table_ref.dtype)
+    table[...] = jnp.zeros(table.shape, table.dtype)
+    kinds = table.shape[0] // 2
     for slot in range(2):
-        for kind, table in enumerate((dgk, dgv)):
-            table_ref[kind, place_ref[1 + slot]] = table[
-                slot * BLK : (slot + 1) * BLK
-            ].astype(table_ref.dtype)
-
-
-def attend_head(x, glob_keys, glob_values, place, rand_head):
-    spans, _, rows, head_size = x.shape
-    table_size = glob_keys.shape[0]
+        for kind, shared in enumerate((dgk, dgv)):
+            block = shared[slot * BLK : (slot + 1) * BLK]
+            table[kind * kinds + place_ref[2 + slot]] = block
+    for flip, ref in enumerate(share_refs):
+        count = table.shape[0] // shares
+        start = (place_ref[1] ^ flip) * count
+        ref[...] = table[pl.ds(start, count)].astype(ref.dtype)
+
+
+def attend_head(chunks, chosen, place, rand_head, table_size, shares):
+    spans = len(chunks)
+    _, rows, head_size = chunks[0].shape
     padded_rows = spans * rows + 2 * BLK
-    block = (1, BLK, head_size)
-    chosen = [
-        pl.BlockSpec(block, lambda i, place, rand: (place[1], 0, place[0])),
-        pl.BlockSpec(block, lambda i, place, rand: (place[2], 0, place[0])),
-    ]
-    whole = lambda *shape: pl.BlockSpec(shape, lambda i, place, rand: (0,) * len(shape))
     keys_each = spans * rows * 8 * BLK
-    return pl.pallas_call(
-        head_kernel,
-        grid_spec=pltpu.PrefetchScalarGridSpec(
-            num_scalar_prefetch=2,
-            grid=(1,),
-            in_specs=[whole(*x.shape)] + chosen + chosen,
-            out_specs=[
-                whole(spans, 3, rows, head_size),
-                whole(2, table_size, BLK, head_size),
-            ],
-            scratch_shapes=[
-                pltpu.VMEM((padded_rows, head_size), jnp.bfloat16),
-                pltpu.VMEM((padded_rows, head_size), jnp.bfloat16),
-                pltpu.VMEM((padded_rows, head_size), jnp.float32),
-                pltpu.VMEM((padded_rows, head_size), jnp.float32),
-                pltpu.VMEM((2 * BLK, head_size), jnp.float32),
-                pltpu.VMEM((2 * BLK, head_size), jnp.float32),
-            ],
-        ),
-        out_shape=[
-            jax.ShapeDtypeStruct((spans, 3, rows, head_size), jnp.bfloat16),
-            jax.ShapeDtypeStruct((2, table_size, BLK, head_size), jnp.bfloat16),
+    share = jax.ShapeDtypeStruct((2 * table_size // shares, BLK, head_size), jnp.bfloat16)
+    outs = [jax.ShapeDtypeStruct((spans, 3, rows, head_size), jnp.bfloat16)] + [share] * shares
+    results = pl.pallas_call(
+        functools.partial(head_kernel, spans, shares),
+        in_specs=[pl.BlockSpec(memory_space=pltpu.SMEM)] * 2 + in_vmem(spans + 1),
+        out_specs=in_vmem(len(outs)),
+        out_shape=outs,
+        scratch_shapes=[
+            pltpu.VMEM((spans * rows, head_size), jnp.bfloat16),
+            pltpu.VMEM((padded_rows, head_size), jnp.bfloat16),
+            pltpu.VMEM((padded_rows, head_size), jnp.bfloat16),
+            pltpu.VMEM((spans * rows, head_size), jnp.bfloat16),
+            pltpu.VMEM((padded_rows, head_size), jnp.float32),
+            pltpu.VMEM((padded_rows, head_size), jnp.float32),
+            pltpu.VMEM((2 * BLK, head_size), jnp.float32),
+            pltpu.VMEM((2 * BLK, head_size), jnp.float32),
+            pltpu.VMEM((2 * table_size, BLK, head_size), jnp.float32),
         ],
         compiler_params=pltpu.CompilerParams(vmem_limit_bytes=VMEM_BYTES),
         cost_estimate=pl.CostEstimate(
@@ -426,7 +477,8 @@
             transcendentals=keys_each,
         ),
         name="attend_head",
-    )(place, rand_head, x, glob_keys, glob_keys, glob_values, glob_values)
+    )(place, rand_head, *chunks, chosen)
+    return results[0], results[1:]
 
 
 def unpack_kernel(x_ref, dq_ref, dk_ref, dv_ref):
@@ -454,73 +506,71 @@
     )(x)
 
 
-def table_kernel(place_ref, *refs):
+def table_kernel(*refs):
     parts, out_ref = refs[:-1], refs[-1]
-    head_size = parts[0].shape[2]
-    for flip, ref in enumerate(parts):
-        at = place_ref[0] ^ flip
-        for head in range(ref.shape[0]):
-            columns = slice(head * head_size, (head + 1) * head_size)
-            out_ref[at, :, columns] = ref[head].astype(out_ref.dtype)
-
-
-def whole_table(me, parts):
-    heads, rows, head_size = parts[0].shape
-    shape = (len(parts), rows, heads * head_size)
-    part = pl.BlockSpec(parts[0].shape, lambda i, me: (0, 0, 0))
+    _, count, _, head_size = parts[0].shape
+    head = lax.axis_index("ctx")
+    share = lax.axis_index("dp")
+    for bits, ref in enumerate(parts):
+        for place, flip in enumerate(HEADS_ORDER):
+            columns = pl.ds(pl.multiple_of((head ^ flip) * head_size, head_size), head_size)
+            for block in range(count):
+                out_ref[(share ^ bits) * count + block, :, columns] = ref[place, block].astype(
+                    out_ref.dtype
+                )
+
+
+def whole_table(parts):
+    heads, blocks, rows, head_size = parts[0].shape
+    shape = (len(parts) * blocks, rows, heads * head_size)
     return pl.pallas_call(
         table_kernel,
-        grid_spec=pltpu.PrefetchScalarGridSpec(
-            num_scalar_prefetch=1,
-            grid=(1,),
-            in_specs=[part] * len(parts),
-            out_specs=pl.BlockSpec(shape, lambda i, me: (0, 0, 0)),
-        ),
+        grid=(1,),
+        in_specs=[pl.BlockSpec(parts[0].shape, lambda i: (0, 0, 0, 0))] * len(parts),
+        out_specs=pl.BlockSpec(shape, lambda i: (0, 0, 0)),
         out_shape=jax.ShapeDtypeStruct(shape, jnp.float32),
         compiler_params=pltpu.CompilerParams(vmem_limit_bytes=VMEM_BYTES),
         name="whole_table",
-    )(me, *parts)
+    )(*parts)
 
 
 def flipped(array, axis, bits):
-    length = lax.axis_size(axis)
-    return lax.ppermute(array, axis, [(i, i ^ bits) for i in range(length)])
+    if bits == 0:
+        return array
+    return lax.ppermute(array, axis, [(i, i ^ bits) for i in range(lax.axis_size(axis))])
 
 
 def on_heads(query, key, value, dout, glob_keys, glob_values, glob_ids, rand_blocks):
     head_count, block_count, _ = rand_blocks.shape
-    rows = query.shape[1]
     head_size = query.shape[2] // head_count
     table_size = glob_keys.shape[0]
-    dp_count = lax.axis_size("dp")
-    head = lax.axis_index("ctx")
-    place = jnp.concatenate([head[None].astype(jnp.int32), glob_ids[0]])
+    shares = lax.axis_size("dp")
+    head = lax.axis_index("ctx").astype(jnp.int32)
+    sequence = lax.axis_index("dp").astype(jnp.int32)
+    packed = pack(query, key, value, dout, head_count)
+    chunks = [flipped(packed[flip], "ctx", flip) for flip in ORDER]
+    place = jnp.concatenate([head[None], sequence[None], glob_ids[0]])
     rand_head = lax.dynamic_index_in_dim(rand_blocks, head, 0, keepdims=False).reshape(-1)
     rand_head = jnp.clip(rand_head, 0, block_count - 1)
-    packed = pack(query, key, value, dout, head_count)
-    arrived = lax.all_to_all(packed, "ctx", 0, 0)
-    grads, table = attend_head(arrived, glob_keys, glob_values, place, rand_head)
-    shares = table.reshape(dp_count, -1, head_size)
-    shares = lax.all_to_all(shares, "dp", 0, 0)
-    share = jnp.sum(shares.astype(jnp.float32), axis=0).astype(jnp.bfloat16)
-    share = jnp.broadcast_to(share.reshape(1, -1, rows, head_size), (head_count, 1, rows, head_size))
-    back = lax.all_to_all(jnp.concatenate([grads, share], axis=1), "ctx", 0, 0)
+    chosen = choose(place, glob_keys, glob_values, head_size)
+    grads, terms = attend_head(chunks, chosen, place, rand_head, table_size, shares)
+    terms = [flipped(terms[bits], "dp", bits) for bits in range(shares)]
+    share = sum(term.astype(jnp.float32) for term in terms).astype(jnp.bfloat16)
+    column = jnp.stack([flipped(share, "ctx", flip) for flip in HEADS_ORDER[:4]])
+    quarter = jnp.concatenate([column, flipped(column, "ctx", 1)])
+    across = flipped(quarter, "dp", 2)
+    beside = flipped(quarter, "dp", 1)
+    corner = flipped(across, "dp", 1)
+    d_table = whole_table([quarter, beside, across, corner])
+    back = lax.all_to_all(grads, "ctx", 0, 0)
     d_query, d_key, d_value = unpack(back)
-    quarter = back[:, 3]
-    beside = flipped(quarter, "dp", 1)
-    across = flipped(quarter, "dp", 2)
-    corner = flipped(across, "dp", 1)
-    me = lax.axis_index("dp").astype(jnp.int32)[None]
-    d_table = whole_table(me, [quarter, beside, across, corner])
     return (d_query, d_key, d_value, d_table.reshape((2,) + glob_keys.shape))
 
 
 def on_device(query, key, value, dout, glob_keys, glob_values, glob_ids, rand_blocks):
     head_count = rand_blocks.shape[0]
-    rows = query.shape[1]
-    one_head_each = lax.axis_size("ctx") == head_count and rows == 2 * BLK
-    shared_table = 2 * glob_keys.shape[0] * BLK == lax.axis_size("dp") * rows
-    if one_head_each and shared_table and lax.axis_size("dp") == 4:
+    one_head_each = lax.axis_size("ctx") == head_count == 8 and query.shape[1] == 2 * BLK
+    if one_head_each and lax.axis_size("dp") == 4 and glob_keys.shape[0] % 2 == 0:
         plan = on_heads
     else:
         plan = on_ring

time: 90.4 us -> 73.6 us (0.81)
  blocking collectives: 36.1 us -> 0 us
  starting transfers between devices: 8.09 us -> 32.3 us
  waiting for transfers between devices: 32.1 us -> 24 us
  Pallas kernels: 8.77 us -> 11.5 us
    all_to_all x2 -> x0, blocking collectives: 36.1 us -> none  [the longest x1 28.8 us: on_heads(): back = lax.all_to_all(jnp.concatenate([grads, share], axis=1), 'ctx', 0, 0)]
    ppermute x3 -> x17, starting transfers between devices: 0.84 us -> 28.1 us  [flipped(): lax.ppermute(array, axis, [(i, i ^ bits) for i in range(lax.axis_size(axi...]
    all_to_all x1, waiting for transfers between devices: 25.5 us -> 0.01 us  [on_heads(): back = lax.all_to_all(grads, 'ctx', 0, 0)]
    ppermute x3 -> x17, waiting for transfers between devices: 6.59 us -> 24 us  [flipped(): lax.ppermute(array, axis, [(i, i ^ bits) for i in range(lax.axis_size(axi...]
    all_to_all x1, starting transfers between devices: 7.25 us -> 4.2 us  [on_heads(): back = lax.all_to_all(grads, 'ctx', 0, 0)]
    pallas_call x3 -> x4, Pallas kernels: 7.72 us -> 10.4 us  [the longest x1 5.97 us: attend_head(): pl.pallas_call(functools.partial(head_kernel, spans, shares), in_specs=[p...]
    unnamed x16 -> x11, local copies, waits for them, and re-layouts: 3.87 us -> 3.02 us
  transfers between devices with their start and end apart: 4 -> 18, of which waited for: 3 -> 7; matrix products, arithmetic and copies ran while one was open for 0% -> 1% of each run, Pallas kernels for 1% -> 3%
where the time goes in v2:
time: 73.6 us; the launch traced here: 72.6 us
  starting transfers between devices  32.3 us (44%)
  waiting for transfers between devices  24 us (33%)
  Pallas kernels  11.5 us (16%)
  local copies, waits for them, and re-layouts  3.22 us (4%)
  other arithmetic  0.78 us (1%)
  between operations  0.75 us (1%)
    ppermute x17, starting transfers between devices, flipped(): lax.ppermute(array, axis, [(i, i ^ bits) for i in range(lax.axis_size(axi...  28.1 us
    ppermute x17, waiting for transfers between devices, flipped(): lax.ppermute(array, axis, [(i, i ^ bits) for i in range(lax.axis_size(axi...  24 us
    pallas_call x1, Pallas kernels, attend_head(): pl.pallas_call(functools.partial(head_kernel, spans, shares), in_specs=[p...  5.97 us
    all_to_all x1, starting transfers between devices, on_heads(): back = lax.all_to_all(grads, 'ctx', 0, 0)  4.2 us
    unnamed x11, local copies, waits for them, and re-layouts  3.02 us
    pallas_call x1, Pallas kernels, pack(): pl.pallas_call(functools.partial(pack_kernel, head_count), in_specs=[in_h...  2.29 us
    pallas_call x1, Pallas kernels, whole_table(): pl.pallas_call(table_kernel, grid=(1,), in_specs=[pl.BlockSpec(parts[0].s...  1.56 us
  transfers between devices with their start and end apart: 18, of which 7 were waited for; matrix products, arithmetic and copies ran while one was open for 1% of the time, Pallas kernels for 3%

profile of v2, /device:TPU:0, one launch (start us, length us, event | category | flops | bytes accessed | tf_op | source)
XLA Modules:
  0.0 72.6 jit_solution(1971910105401289291)
XLA Ops:
  0.6 2.3 %pack_heads.1 = (bf16[4,128,128]{2,1,0:T(8,128)(2,1)}, bf16[4,128,128]{2,1,0:T(8,128)(2,1)}, bf16[4,128,128]{2,1,0:T(8,128)(2,1)}, bf16[4,128,128]{2,1,0:T(8,128...) custom-call(bf16[1,128,1024]{2,1,0:T(8,128)(2,1)} %refs_0_.1, ...), custom_call_target="tpu_custom_call" | custom-call | bytes 2097152 | tf_op jit(solution)/shard_map/pack_heads/pallas_call | solution.py:277
  2.9 3.1 %collective-permute-start = (bf16[4,128,128]{2,1,0:T(8,128)(2,1)}, bf16[4,128,128]{2,1,0:T(8,128)(2,1)S(1)}, u32[]{:S(2)}, u32[]{:S(2)}) collective-permute-start(bf16[4,128,128]{2,1,0:T(8,128)(2,1)} %get-tuple-element.21), channel_id=1, source_target_pairs={{0,8},{4,12},{8,0},{12,4},{16,24},{20,28},{24,16},{28,20},{1,9},{5... | collective-permute-start | bytes 393224 | tf_op jit(solution)/shard_map/ppermute | solution.py:540
  6.0 2.6 %collective-permute-start.1 = (bf16[4,128,128]{2,1,0:T(8,128)(2,1)}, bf16[4,128,128]{2,1,0:T(8,128)(2,1)S(1)}, u32[]{:S(2)}, u32[]{:S(2)}) collective-permute-start(bf16[4,128,128]{2,1,0:T(8,128)(2,1)} %get-tuple-element.22), channel_id=1, source_target_pairs={{0,16},{4,20},{8,24},{12,28},{16,0},{20,4},{24,8},{28,12},{1,17},{... | collective-permute-start | bytes 393224 | tf_op jit(solution)/shard_map/ppermute | solution.py:540
  8.6 1.3 %collective-permute-start.2 = (bf16[4,128,128]{2,1,0:T(8,128)(2,1)}, bf16[4,128,128]{2,1,0:T(8,128)(2,1)S(1)}, u32[]{:S(2)}, u32[]{:S(2)}) collective-permute-start(bf16[4,128,128]{2,1,0:T(8,128)(2,1)} %get-tuple-element.23), channel_id=1, source_target_pairs={{0,20},{4,16},{8,28},{12,24},{16,4},{20,0},{24,12},{28,8},{1,21},{... | collective-permute-start | bytes 393224 | tf_op jit(solution)/shard_map/ppermute | solution.py:540
  10.0 3.9 %collective-permute-start.4 = (bf16[4,128,128]{2,1,0:T(8,128)(2,1)}, bf16[4,128,128]{2,1,0:T(8,128)(2,1)S(1)}, u32[]{:S(2)}, u32[]{:S(2)}) collective-permute-start(bf16[4,128,128]{2,1,0:T(8,128)(2,1)} %get-tuple-element.25), channel_id=1, source_target_pairs={{0,24},{4,28},{8,16},{12,20},{16,8},{20,12},{24,0},{28,4},{1,25},{... | collective-permute-start | bytes 393224 | tf_op jit(solution)/shard_map/ppermute | solution.py:540
  13.9 2.9 %collective-permute-start.5 = (bf16[4,128,128]{2,1,0:T(8,128)(2,1)}, bf16[4,128,128]{2,1,0:T(8,128)(2,1)S(1)}, u32[]{:S(2)}, u32[]{:S(2)}) collective-permute-start(bf16[4,128,128]{2,1,0:T(8,128)(2,1)} %get-tuple-element.26), channel_id=1, source_target_pairs={{0,28},{4,24},{8,20},{12,16},{16,12},{20,8},{24,4},{28,0},{1,29},{... | collective-permute-start | bytes 393224 | tf_op jit(solution)/shard_map/ppermute | solution.py:540
  17.6 2.6 %collective-permute-start.6 = (bf16[4,128,128]{2,1,0:T(8,128)(2,1)}, bf16[4,128,128]{2,1,0:T(8,128)(2,1)S(1)}, u32[]{:S(2)}, u32[]{:S(2)}) collective-permute-start(bf16[4,128,128]{2,1,0:T(8,128)(2,1)} %get-tuple-element.27), channel_id=1, source_target_pairs={{0,4},{4,0},{8,12},{12,8},{16,20},{20,16},{24,28},{28,24},{1,5},{5... | collective-permute-start | bytes 393224 | tf_op jit(solution)/shard_map/ppermute | solution.py:540
  21.2 1.0 %copy-done.1 = bf16[4,64,1024]{2,1,0:T(8,128)(2,1)S(1)} copy-done((bf16[4,64,1024]{2,1,0:T(8,128)(2,1)S(1)}, bf16[4,64,1024]{2,1,0:T(8,128)(2,1)}, u32[]{:S(2)}) %copy-start.1) | copy-done | bytes 524312
  22.2 1.0 %copy-done.2 = bf16[4,64,1024]{2,1,0:T(8,128)(2,1)S(1)} copy-done((bf16[4,64,1024]{2,1,0:T(8,128)(2,1)S(1)}, bf16[4,64,1024]{2,1,0:T(8,128)(2,1)}, u32[]{:S(2)}) %copy-start.2) | copy-done | bytes 524312
  23.9 4.2 %collective-permute-done.2.refs_3_ = bf16[4,128,128]{2,1,0:T(8,128)(2,1)S(1)} collective-permute-done((bf16[4,128,128]{2,1,0:T(8,128)(2,1)}, bf16[4,128,128]{2,1,0:T(8,128)(2,1)S(1)}, u32[]{:S(2)}, u32[]{:S(2)}) %collective-permute-start.2) | collective-permute-done | bytes 131104 | tf_op jit(solution)/shard_map/ppermute | solution.py:540
  28.1 0.9 %copy-done.3 = bf16[4,128,128]{2,1,0:T(8,128)(2,1)S(1)} copy-done((bf16[4,128,128]{2,1,0:T(8,128)(2,1)S(1)}, bf16[4,128,128]{2,1,0:T(8,128)(2,1)}, u32[]{:S(2)}) %copy-start.3) | copy-done | bytes 131096
  29.0 6.0 %attend_head.1 = (bf16[8,3,128,128]{3,2,1,0:T(8,128)(2,1)}, bf16[2,64,128]{2,1,0:T(8,128)(2,1)S(1)}, bf16[2,64,128]{2,1,0:T(8,128)(2,1)S(1)}, bf16[2,64,128]{2,1,0:T(8,128)(2,1)S(1)}, bf16[2,64,128]{2,1,0:T(8,128)(2,1)S(1)}) custom-call(s32[4]{0:T(128)S(1)} %pad_add_fusion.place_ref, s32[48]{0:T(128)S(1)} %min.12.rand_ref, ...), custom_call_target="tpu_custom_call" | custom-call | flops 671088640 | bytes 2097152 | tf_op jit(solution)/shard_map/attend_head/pallas_call | solution.py:457
  35.0 1.5 %collective-permute-start.8 = (bf16[2,64,128]{2,1,0:T(8,128)(2,1)S(1)}, bf16[2,64,128]{2,1,0:T(8,128)(2,1)S(1)}, u32[]{:S(2)}, u32[]{:S(2)}) collective-permute-start(bf16[2,64,128]{2,1,0:T(8,128)(2,1)S(1)} %get-tuple-element.34), channel_id=1, source_target_pairs={{0,2},{1,3},{2,0},{3,1},{4,6},{5,7},{6,4},{7,5},{8,10},{9,11},{10,... | collective-permute-start | bytes 98312 | tf_op jit(solution)/shard_map/ppermute | solution.py:540
  36.9 2.1 %collective-permute-done.8 = bf16[2,64,128]{2,1,0:T(8,128)(2,1)S(1)} collective-permute-done((bf16[2,64,128]{2,1,0:T(8,128)(2,1)S(1)}, bf16[2,64,128]{2,1,0:T(8,128)(2,1)S(1)}, u32[]{:S(2)}, u32[]{:S(2)}) %collective-permute-start.8) | collective-permute-done | bytes 32800 | tf_op jit(solution)/shard_map/ppermute | solution.py:540
  38.9 1.0 %collective-permute-done.9 = bf16[2,64,128]{2,1,0:T(8,128)(2,1)S(1)} collective-permute-done((bf16[2,64,128]{2,1,0:T(8,128)(2,1)S(1)}, bf16[2,64,128]{2,1,0:T(8,128)(2,1)S(1)}, u32[]{:S(2)}, u32[]{:S(2)}) %collective-permute-start.9) | collective-permute-done | bytes 32800 | tf_op jit(solution)/shard_map/ppermute | solution.py:540
  39.9 2.8 %collective-permute-start.12 = (bf16[2,64,128]{2,1,0:T(8,128)(2,1)S(1)}, bf16[2,64,128]{2,1,0:T(8,128)(2,1)S(1)}, u32[]{:S(2)}, u32[]{:S(2)}) collective-permute-start(bf16[2,64,128]{2,1,0:T(8,128)(2,1)S(1)} %get-tuple-element.37), channel_id=1, source_target_pairs={{0,24},{4,28},{8,16},{12,20},{16,8},{20,12},{24,0},{28,4},{1,25},{... | collective-permute-start | bytes 98312 | tf_op jit(solution)/shard_map/ppermute | solution.py:540
  42.7 3.9 %collective-permute-start.11 = (bf16[2,64,128]{2,1,0:T(8,128)(2,1)S(1)}, bf16[2,64,128]{2,1,0:T(8,128)(2,1)S(1)}, u32[]{:S(2)}, u32[]{:S(2)}) collective-permute-start(bf16[2,64,128]{2,1,0:T(8,128)(2,1)S(1)} %get-tuple-element.37), channel_id=1, source_target_pairs={{0,16},{4,20},{8,24},{12,28},{16,0},{20,4},{24,8},{28,12},{1,17},{... | collective-permute-start | bytes 98312 | tf_op jit(solution)/shard_map/ppermute | solution.py:540
  46.7 4.2 %all-to-all-start = ((bf16[8,3,128,128]{3,2,1,0:T(8,128)(2,1)}), bf16[8,3,128,128]{3,2,1,0:T(8,128)(2,1)S(1)}, u32[]{:S(2)}, u32[]{:S(2)}) async-start(bf16[8,3,128,128]{3,2,1,0:T(8,128)(2,1)} %get-tuple-element.28), calls=%async_computation | async-start | bytes 1572864 | tf_op jit(solution)/shard_map/all_to_all | solution.py:565
  51.0 2.1 %collective-permute-start.13 = (bf16[4,2,64,128]{3,2,1,0:T(8,128)(2,1)S(1)}, bf16[4,2,64,128]{3,2,1,0:T(8,128)(2,1)S(1)}, u32[]{:S(2)}, u32[]{:S(2)}) collective-permute-start(bf16[4,2,64,128]{3,2,1,0:T(8,128)(2,1)S(1)} %pad_maximum_fusion), channel_id=1, source_target_pairs={{0,4},{4,0},{8,12},{12,8},{16,20},{20,16},{24,28},{28,24},{1,5},{5... | collective-permute-start | bytes 393224 | tf_op jit(solution)/shard_map/ppermute | solution.py:540
  53.1 8.9 %collective-permute-done.13 = bf16[4,2,64,128]{3,2,1,0:T(8,128)(2,1)S(1)} collective-permute-done((bf16[4,2,64,128]{3,2,1,0:T(8,128)(2,1)S(1)}, bf16[4,2,64,128]{3,2,1,0:T(8,128)(2,1)S(1)}, u32[]{:S(2)}, u32[]{:S(2)}) %collective-permute-start.13) | collective-permute-done | bytes 131104 | tf_op jit(solution)/shard_map/ppermute | solution.py:540
  62.8 5.6 %collective-permute-done.15.refs_2_ = bf16[8,2,64,128]{3,2,1,0:T(8,128)(2,1)S(1)} collective-permute-done((bf16[8,2,64,128]{3,2,1,0:T(8,128)(2,1)S(1)}, bf16[8,2,64,128]{3,2,1,0:T(8,128)(2,1)S(1)}, u32[]{:S(2)}, u32[]{:S(2)}) %collective-permute-start.15) | collective-permute-done | bytes 262176 | tf_op jit(solution)/shard_map/ppermute | solution.py:540
  68.4 1.5 %collective-permute-done.16.refs_3_ = bf16[8,2,64,128]{3,2,1,0:T(8,128)(2,1)S(1)} collective-permute-done((bf16[8,2,64,128]{3,2,1,0:T(8,128)(2,1)S(1)}, bf16[8,2,64,128]{3,2,1,0:T(8,128)(2,1)S(1)}, u32[]{:S(2)}, u32[]{:S(2)}) %collective-permute-start.16) | collective-permute-done | bytes 262176 | tf_op jit(solution)/shard_map/ppermute | solution.py:540
  70.0 1.6 %whole_table.1 = f32[8,64,1024]{2,1,0:T(8,128)} custom-call(bf16[8,2,64,128]{3,2,1,0:T(8,128)(2,1)S(1)} %constant_dynamic-update-slice_fusion.refs_0_, bf16[8,2,64,128]{3,2,1,0:T(8,128)(2,1)S(1)} %collective-permute-done.14.refs_1_, bf16[8,2,64,128]{3,2,1,0:T(8,128)(2,1)S(1)} %collective-permute-done.15.refs_2_, ...), custom_call_target="tpu_custom_call" | custom-call | tf_op jit(solution)/shard_map/whole_table/pallas_call | solution.py:526
  71.5 1.1 %unpack_heads.1 = (bf16[1,128,1024]{2,1,0:T(8,128)(2,1)}, bf16[1,128,1024]{2,1,0:T(8,128)(2,1)}, bf16[1,128,1024]{2,1,0:T(8,128)(2,1)}) custom-call(bf16[8,3,128,128]{3,2,1,0:T(8,128)(2,1)S(1)} %all-to-all-done.x_ref), custom_call_target="tpu_custom_call" | custom-call | bytes 1572864 | tf_op jit(solution)/shard_map/unpack_heads/pallas_call | solution.py:495
  (36 shorter events, 3.9 us)
Async XLA Ops:
  0.6 13.3 %copy-start = (s32[8,16,3]{1,0,2:T(8,128)S(1)}, s32[8,16,3]{1,0,2:T(8,128)}, u32[]{:S(2)}) copy-start(s32[8,16,3]{1,0,2:T(8,128)} %param.15) | copy-start | bytes 4612
  2.9 11.0 %collective-permute-start = (bf16[4,128,128]{2,1,0:T(8,128)(2,1)}, bf16[4,128,128]{2,1,0:T(8,128)(2,1)S(1)}, u32[]{:S(2)}, u32[]{:S(2)}) collective-permute-start(bf16[4,128,128]{2,1,0:T(8,128)(2,1)} %get-tuple-element.21), channel_id=1, source_target_pairs={{0,8},{4,12},{8,0},{12,4},{16,24},{20,28},{24,16},{28,20},{1,9},{5... | collective-permute-start | bytes 393224 | tf_op jit(solution)/shard_map/ppermute | solution.py:540
  6.0 11.6 %collective-permute-start.1 = (bf16[4,128,128]{2,1,0:T(8,128)(2,1)}, bf16[4,128,128]{2,1,0:T(8,128)(2,1)S(1)}, u32[]{:S(2)}, u32[]{:S(2)}) collective-permute-start(bf16[4,128,128]{2,1,0:T(8,128)(2,1)} %get-tuple-element.22), channel_id=1, source_target_pairs={{0,16},{4,20},{8,24},{12,28},{16,0},{20,4},{24,8},{28,12},{1,17},{... | collective-permute-start | bytes 393224 | tf_op jit(solution)/shard_map/ppermute | solution.py:540
  8.6 19.5 %collective-permute-start.2 = (bf16[4,128,128]{2,1,0:T(8,128)(2,1)}, bf16[4,128,128]{2,1,0:T(8,128)(2,1)S(1)}, u32[]{:S(2)}, u32[]{:S(2)}) collective-permute-start(bf16[4,128,128]{2,1,0:T(8,128)(2,1)} %get-tuple-element.23), channel_id=1, source_target_pairs={{0,20},{4,16},{8,28},{12,24},{16,4},{20,0},{24,12},{28,8},{1,21},{... | collective-permute-start | bytes 393224 | tf_op jit(solution)/shard_map/ppermute | solution.py:540
  9.9 18.2 %collective-permute-start.3 = (bf16[4,128,128]{2,1,0:T(8,128)(2,1)}, bf16[4,128,128]{2,1,0:T(8,128)(2,1)S(1)}, u32[]{:S(2)}, u32[]{:S(2)}) collective-permute-start(bf16[4,128,128]{2,1,0:T(8,128)(2,1)} %get-tuple-element.24), channel_id=1, source_target_pairs={{0,12},{4,8},{8,4},{12,0},{16,28},{20,24},{24,20},{28,16},{1,13},{... | collective-permute-start | bytes 393224 | tf_op jit(solution)/shard_map/ppermute | solution.py:540
  10.0 18.1 %collective-permute-start.4 = (bf16[4,128,128]{2,1,0:T(8,128)(2,1)}, bf16[4,128,128]{2,1,0:T(8,128)(2,1)S(1)}, u32[]{:S(2)}, u32[]{:S(2)}) collective-permute-start(bf16[4,128,128]{2,1,0:T(8,128)(2,1)} %get-tuple-element.25), channel_id=1, source_target_pairs={{0,24},{4,28},{8,16},{12,20},{16,8},{20,12},{24,0},{28,4},{1,25},{... | collective-permute-start | bytes 393224 | tf_op jit(solution)/shard_map/ppermute | solution.py:540
  13.9 14.2 %collective-permute-start.5 = (bf16[4,128,128]{2,1,0:T(8,128)(2,1)}, bf16[4,128,128]{2,1,0:T(8,128)(2,1)S(1)}, u32[]{:S(2)}, u32[]{:S(2)}) collective-permute-start(bf16[4,128,128]{2,1,0:T(8,128)(2,1)} %get-tuple-element.26), channel_id=1, source_target_pairs={{0,28},{4,24},{8,20},{12,16},{16,12},{20,8},{24,4},{28,0},{1,29},{... | collective-permute-start | bytes 393224 | tf_op jit(solution)/shard_map/ppermute | solution.py:540
  17.6 10.5 %collective-permute-start.6 = (bf16[4,128,128]{2,1,0:T(8,128)(2,1)}, bf16[4,128,128]{2,1,0:T(8,128)(2,1)S(1)}, u32[]{:S(2)}, u32[]{:S(2)}) collective-permute-start(bf16[4,128,128]{2,1,0:T(8,128)(2,1)} %get-tuple-element.27), channel_id=1, source_target_pairs={{0,4},{4,0},{8,12},{12,8},{16,20},{20,16},{24,28},{28,24},{1,5},{5... | collective-permute-start | bytes 393224 | tf_op jit(solution)/shard_map/ppermute | solution.py:540
  21.2 1.0 %copy-start.1 = (bf16[4,64,1024]{2,1,0:T(8,128)(2,1)S(1)}, bf16[4,64,1024]{2,1,0:T(8,128)(2,1)}, u32[]{:S(2)}) copy-start(bf16[4,64,1024]{2,1,0:T(8,128)(2,1)} %gk_ref.1) | copy-start | bytes 1572868
  22.2 1.0 %copy-start.2 = (bf16[4,64,1024]{2,1,0:T(8,128)(2,1)S(1)}, bf16[4,64,1024]{2,1,0:T(8,128)(2,1)}, u32[]{:S(2)}) copy-start(bf16[4,64,1024]{2,1,0:T(8,128)(2,1)} %gv_ref.1) | copy-start | bytes 1572868
  28.1 0.9 %copy-start.3 = (bf16[4,128,128]{2,1,0:T(8,128)(2,1)S(1)}, bf16[4,128,128]{2,1,0:T(8,128)(2,1)}, u32[]{:S(2)}) copy-start(bf16[4,128,128]{2,1,0:T(8,128)(2,1)} %get-tuple-element.20.refs_0_) | copy-start | bytes 393220
  35.0 1.9 %collective-permute-start.7 = (bf16[2,64,128]{2,1,0:T(8,128)(2,1)S(1)}, bf16[2,64,128]{2,1,0:T(8,128)(2,1)S(1)}, u32[]{:S(2)}, u32[]{:S(2)}) collective-permute-start(bf16[2,64,128]{2,1,0:T(8,128)(2,1)S(1)} %get-tuple-element.33), channel_id=1, source_target_pairs={{0,1},{1,0},{2,3},{3,2},{4,5},{5,4},{6,7},{7,6},{8,9},{9,8},{10,11... | collective-permute-start | bytes 98312 | tf_op jit(solution)/shard_map/ppermute | solution.py:540
  35.0 3.9 %collective-permute-start.8 = (bf16[2,64,128]{2,1,0:T(8,128)(2,1)S(1)}, bf16[2,64,128]{2,1,0:T(8,128)(2,1)S(1)}, u32[]{:S(2)}, u32[]{:S(2)}) collective-permute-start(bf16[2,64,128]{2,1,0:T(8,128)(2,1)S(1)} %get-tuple-element.34), channel_id=1, source_target_pairs={{0,2},{1,3},{2,0},{3,1},{4,6},{5,7},{6,4},{7,5},{8,10},{9,11},{10,... | collective-permute-start | bytes 98312 | tf_op jit(solution)/shard_map/ppermute | solution.py:540
  36.5 3.3 %collective-permute-start.9 = (bf16[2,64,128]{2,1,0:T(8,128)(2,1)S(1)}, bf16[2,64,128]{2,1,0:T(8,128)(2,1)S(1)}, u32[]{:S(2)}, u32[]{:S(2)}) collective-permute-start(bf16[2,64,128]{2,1,0:T(8,128)(2,1)S(1)} %get-tuple-element.35), channel_id=1, source_target_pairs={{0,3},{1,2},{2,1},{3,0},{4,7},{5,6},{6,5},{7,4},{8,11},{9,10},{10,... | collective-permute-start | bytes 98312 | tf_op jit(solution)/shard_map/ppermute | solution.py:540
  39.9 11.0 %collective-permute-start.12 = (bf16[2,64,128]{2,1,0:T(8,128)(2,1)S(1)}, bf16[2,64,128]{2,1,0:T(8,128)(2,1)S(1)}, u32[]{:S(2)}, u32[]{:S(2)}) collective-permute-start(bf16[2,64,128]{2,1,0:T(8,128)(2,1)S(1)} %get-tuple-element.37), channel_id=1, source_target_pairs={{0,24},{4,28},{8,16},{12,20},{16,8},{20,12},{24,0},{28,4},{1,25},{... | collective-permute-start | bytes 98312 | tf_op jit(solution)/shard_map/ppermute | solution.py:540
  42.7 8.2 %collective-permute-start.11 = (bf16[2,64,128]{2,1,0:T(8,128)(2,1)S(1)}, bf16[2,64,128]{2,1,0:T(8,128)(2,1)S(1)}, u32[]{:S(2)}, u32[]{:S(2)}) collective-permute-start(bf16[2,64,128]{2,1,0:T(8,128)(2,1)S(1)} %get-tuple-element.37), channel_id=1, source_target_pairs={{0,16},{4,20},{8,24},{12,28},{16,0},{20,4},{24,8},{28,12},{1,17},{... | collective-permute-start | bytes 98312 | tf_op jit(solution)/shard_map/ppermute | solution.py:540
  46.6 4.4 %collective-permute-start.10 = (bf16[2,64,128]{2,1,0:T(8,128)(2,1)S(1)}, bf16[2,64,128]{2,1,0:T(8,128)(2,1)S(1)}, u32[]{:S(2)}, u32[]{:S(2)}) collective-permute-start(bf16[2,64,128]{2,1,0:T(8,128)(2,1)S(1)} %get-tuple-element.37), channel_id=1, source_target_pairs={{0,8},{4,12},{8,0},{12,4},{16,24},{20,28},{24,16},{28,20},{1,9},{5... | collective-permute-start | bytes 98312 | tf_op jit(solution)/shard_map/ppermute | solution.py:540
  46.7 24.8 %all-to-all-start = ((bf16[8,3,128,128]{3,2,1,0:T(8,128)(2,1)}), bf16[8,3,128,128]{3,2,1,0:T(8,128)(2,1)S(1)}, u32[]{:S(2)}, u32[]{:S(2)}) async-start(bf16[8,3,128,128]{3,2,1,0:T(8,128)(2,1)} %get-tuple-element.28), calls=%async_computation | async-start | bytes 1572864 | tf_op jit(solution)/shard_map/all_to_all | solution.py:565
  51.0 11.0 %collective-permute-start.13 = (bf16[4,2,64,128]{3,2,1,0:T(8,128)(2,1)S(1)}, bf16[4,2,64,128]{3,2,1,0:T(8,128)(2,1)S(1)}, u32[]{:S(2)}, u32[]{:S(2)}) collective-permute-start(bf16[4,2,64,128]{3,2,1,0:T(8,128)(2,1)S(1)} %pad_maximum_fusion), channel_id=1, source_target_pairs={{0,4},{4,0},{8,12},{12,8},{16,20},{20,16},{24,28},{28,24},{1,5},{5... | collective-permute-start | bytes 393224 | tf_op jit(solution)/shard_map/ppermute | solution.py:540
  62.0 6.4 %collective-permute-start.15 = (bf16[8,2,64,128]{3,2,1,0:T(8,128)(2,1)S(1)}, bf16[8,2,64,128]{3,2,1,0:T(8,128)(2,1)S(1)}, u32[]{:S(2)}, u32[]{:S(2)}) collective-permute-start(bf16[8,2,64,128]{3,2,1,0:T(8,128)(2,1)S(1)} %constant_dynamic-update-slice_fusion.refs_0_), channel_id=1, source_target_pairs={{0,2},{1,3},{2,0},{3,1},{4,6},{5,7},{6,4},{7,5},{8,10},{9,11},{10,... | collective-permute-start | bytes 786440 | tf_op jit(solution)/shard_map/ppermute | solution.py:540
  62.8 5.6 %collective-permute-start.14 = (bf16[8,2,64,128]{3,2,1,0:T(8,128)(2,1)S(1)}, bf16[8,2,64,128]{3,2,1,0:T(8,128)(2,1)S(1)}, u32[]{:S(2)}, u32[]{:S(2)}) collective-permute-start(bf16[8,2,64,128]{3,2,1,0:T(8,128)(2,1)S(1)} %constant_dynamic-update-slice_fusion.refs_0_), channel_id=1, source_target_pairs={{0,1},{1,0},{2,3},{3,2},{4,5},{5,4},{6,7},{7,6},{8,9},{9,8},{10,11... | collective-permute-start | bytes 786440 | tf_op jit(solution)/shard_map/ppermute | solution.py:540
  68.4 1.5 %collective-permute-start.16 = (bf16[8,2,64,128]{3,2,1,0:T(8,128)(2,1)S(1)}, bf16[8,2,64,128]{3,2,1,0:T(8,128)(2,1)S(1)}, u32[]{:S(2)}, u32[]{:S(2)}) collective-permute-start(bf16[8,2,64,128]{3,2,1,0:T(8,128)(2,1)S(1)} %collective-permute-done.15.refs_2_), channel_id=1, source_target_pairs={{0,1},{1,0},{2,3},{3,2},{4,5},{5,4},{6,7},{7,6},{8,9},{9,8},{10,11... | collective-permute-start | bytes 786440 | tf_op jit(solution)/shard_map/ppermute | solution.py:540

commit v3 on v2

--- a/solution.py
+++ b/solution.py
@@ -233,7 +233,7 @@
 SMALL_VMEM_BYTES = 4 * 1024 * 1024
 LARGE_VMEM_BYTES = 60 * 1024 * 1024
 MASKED = -1e30
-ORDER = (0, 2, 4, 5, 3, 6, 7, 1)
+ORDER = (0, 4, 2, 5, 3, 6, 7, 1)
 HEADS_ORDER = (0, 2, 4, 6, 1, 3, 5, 7)
 
 
@@ -291,7 +291,7 @@
     )(query, key, value, dout)
 
 
-def choose_kernel(place_ref, gk_ref, gv_ref, out_ref, sems):
+def choose_kernel(place_ref, gk_ref, gv_ref, own_ref, out_ref, held_ref, sems):
     head_size = out_ref.shape[2]
     columns = pl.ds(pl.multiple_of(place_ref[0] * head_size, head_size), head_size)
     copies = [
@@ -303,44 +303,77 @@
         for kind, ref in enumerate((gk_ref, gv_ref))
         for slot in range(2)
     ]
+    copies.append(pltpu.make_async_copy(own_ref, held_ref, sems.at[4]))
     for copy in copies:
         copy.start()
     for copy in copies:
         copy.wait()
 
 
-def choose(place, glob_keys, glob_values, head_size):
+def choose(place, glob_keys, glob_values, own):
+    head_size = own.shape[2]
     return pl.pallas_call(
         choose_kernel,
         in_specs=[pl.BlockSpec(memory_space=pltpu.SMEM)]
-        + [pl.BlockSpec(memory_space=pltpu.HBM)] * 2,
-        out_specs=pl.BlockSpec(memory_space=pltpu.VMEM),
-        out_shape=jax.ShapeDtypeStruct((4, BLK, head_size), glob_keys.dtype),
-        scratch_shapes=[pltpu.SemaphoreType.DMA((4,))],
+        + [pl.BlockSpec(memory_space=pltpu.HBM)] * 3,
+        out_specs=in_vmem(2),
+        out_shape=[
+            jax.ShapeDtypeStruct((4, BLK, head_size), glob_keys.dtype),
+            jax.ShapeDtypeStruct(own.shape, own.dtype),
+        ],
+        scratch_shapes=[pltpu.SemaphoreType.DMA((5,))],
         compiler_params=pltpu.CompilerParams(vmem_limit_bytes=SMALL_VMEM_BYTES),
         cost_estimate=pl.CostEstimate(
             flops=0, bytes_accessed=16 * BLK * head_size, transcendentals=0
         ),
         name="choose_blocks",
-    )(place, glob_keys, glob_values)
-
-
-def head_kernel(spans, shares, place_ref, rand_ref, *refs):
-    x_refs, g_ref, send_ref = refs[:spans], refs[spans], refs[spans + 1]
-    share_refs = refs[spans + 2 : spans + 2 + shares]
-    q_all, k_all, v_all, o_all, dk_all, dv_all, dgk, dgv, table = refs[
-        spans + 2 + shares :
+    )(place, glob_keys, glob_values, own)
+
+
+def split_rows(block):
+    empty = jnp.zeros((BLK, block.shape[1]), block.dtype)
+    return jnp.concatenate(
+        [
+            jnp.concatenate([block[:BLK], empty], axis=0),
+            jnp.concatenate([empty, block[BLK:]], axis=0),
+        ],
+        axis=1,
+    )
+
+
+def list_places(rand_ref, span, rand_count):
+    return [
+        [
+            pl.multiple_of((rand_ref[(2 * span + half) * rand_count + slot] + 1) * BLK, BLK)
+            for slot in range(rand_count)
+        ]
+        for half in range(2)
     ]
+
+
+def gathered(pool, at, places, table_blocks):
+    window = pool[at : at + 4 * BLK]
+    lists = [
+        jnp.concatenate([edge] + [pool[pl.ds(p, BLK)] for p in places[half]], axis=0)
+        for half, edge in enumerate((window[:BLK], window[3 * BLK :]))
+    ]
+    both = jnp.concatenate([window[BLK : 3 * BLK]] + table_blocks, axis=0)
+    return jnp.concatenate(lists, axis=1), both
+
+
+def score_kernel(spans, shares, place_ref, rand_ref, *refs):
+    x_refs, g_ref = refs[:spans], refs[spans]
+    q_all, k_all, o_all, p_all, ds_all = refs[spans + 1 : spans + 6]
+    share_refs = refs[spans + 6 : spans + 6 + shares]
+    v_all, dgk, dgv, table = refs[spans + 6 + shares :]
     _, rows, head_size = x_refs[0].shape
     rand_count = rand_ref.shape[0] // (2 * spans)
     scaling = 1.0 / math.sqrt(head_size)
     me = place_ref[0]
     top = BLK + spans * rows
-    for pool in (k_all, v_all, dk_all, dv_all):
+    for pool in (k_all, v_all):
         pool[:BLK] = jnp.zeros((BLK, head_size), pool.dtype)
         pool[top:] = jnp.zeros((BLK, head_size), pool.dtype)
-    for pool in (dk_all, dv_all):
-        pool[BLK:top] = jnp.zeros((top - BLK, head_size), pool.dtype)
     starts = [pl.multiple_of((me ^ flip) * rows, rows) for flip in ORDER]
     for at, ref in zip(starts, x_refs):
         q_all[pl.ds(at, rows)] = ref[0]
@@ -351,43 +384,14 @@
     gv = [g_ref[2], g_ref[3]]
     own = (1 + rand_count) * BLK
     first = lax.broadcasted_iota(jnp.int32, (1, rows), 1) < BLK
-    empty = jnp.zeros((BLK, head_size), jnp.bfloat16)
-
-    def split(block):
-        return jnp.concatenate(
-            [
-                jnp.concatenate([block[:BLK], empty], axis=0),
-                jnp.concatenate([empty, block[BLK:]], axis=0),
-            ],
-            axis=1,
-        )
-
     for span in range(spans):
         at = span * rows
         q = q_all[at : at + rows]
         o = o_all[at : at + rows]
-        q_split = split(q)
-        o_split = split(o)
-        places = [
-            [
-                pl.multiple_of((rand_ref[(2 * span + half) * rand_count + slot] + 1) * BLK, BLK)
-                for slot in range(rand_count)
-            ]
-            for half in range(2)
-        ]
-
-        def gathered(pool, table_blocks):
-            window = pool[at : at + 4 * BLK]
-            lists = [
-                jnp.concatenate([edge] + [pool[pl.ds(p, BLK)] for p in places[half]], axis=0)
-                for half, edge in enumerate((window[:BLK], window[3 * BLK :]))
-            ]
-            both = jnp.concatenate([window[BLK : 3 * BLK]] + table_blocks, axis=0)
-            return jnp.concatenate(lists, axis=1), both
-
-        k_own, k_both = gathered(k_all, gk)
-        v_own, v_both = gathered(v_all, gv)
-        s_own = dot(k_own, q_split, 1, 1) * scaling
+        places = list_places(rand_ref, span, rand_count)
+        k_own, k_both = gathered(k_all, at, places, gk)
+        v_own, v_both = gathered(v_all, at, places, gv)
+        s_own = dot(k_own, split_rows(q), 1, 1) * scaling
         s_both = dot(k_both, q, 1, 1) * scaling
         if span == 0 or span == spans - 1:
             row = lax.broadcasted_iota(jnp.int32, (own, 1), 0) < BLK
@@ -404,37 +408,23 @@
         p_both = e_both * inverse
         pb_own = p_own.astype(jnp.bfloat16)
         pb_both = p_both.astype(jnp.bfloat16)
-        g_own = dot(v_own, o_split, 1, 1)
+        g_own = dot(v_own, split_rows(o), 1, 1)
         g_both = dot(v_both, o, 1, 1)
         row_dot = jnp.sum(pb_own.astype(jnp.float32) * g_own, axis=0, keepdims=True) + jnp.sum(
             pb_both.astype(jnp.float32) * g_both, axis=0, keepdims=True
         )
         ds_own = (p_own * (g_own - row_dot) * scaling).astype(jnp.bfloat16)
         ds_both = (p_both * (g_both - row_dot) * scaling).astype(jnp.bfloat16)
-        wide = dot(ds_own, k_own, 0, 0)
-        dq = jnp.concatenate([wide[:BLK, :head_size], wide[BLK:, head_size:]], axis=0)
-        send_ref[span, 0] = (dq + dot(ds_both, k_both, 0, 0)).astype(jnp.bfloat16)
-        for weights_own, weights_both, x_split, x, pool, shared in (
-            (ds_own, ds_both, q_split, q, dk_all, dgk),
-            (pb_own, pb_both, o_split, o, dv_all, dgv),
-        ):
-            d_own = dot(weights_own, x_split, 1, 0)
-            d_both = dot(weights_both, x, 1, 0)
-            pool[at + BLK : at + 3 * BLK] += d_both[: 2 * BLK]
+        p_all[span, :own] = pb_own
+        p_all[span, own:] = pb_both
+        ds_all[span, :own] = ds_own
+        ds_all[span, own:] = ds_both
+        for weights, x, shared in ((ds_both, q, dgk), (pb_both, o, dgv)):
+            term = dot(weights[2 * BLK :], x, 1, 0)
             if span == 0:
-                shared[...] = d_both[2 * BLK :]
+                shared[...] = term
             else:
-                shared[...] += d_both[2 * BLK :]
-            pool[at : at + BLK] += d_own[:BLK, :head_size]
-            pool[at + 3 * BLK : at + 4 * BLK] += d_own[:BLK, head_size:]
-            for half in range(2):
-                columns = slice(half * head_size, (half + 1) * head_size)
-                for slot, p in enumerate(places[half]):
-                    pool[pl.ds(p, BLK)] += d_own[(1 + slot) * BLK : (2 + slot) * BLK, columns]
-    for span in range(spans):
-        at = BLK + span * rows
-        send_ref[span, 1] = dk_all[at : at + rows].astype(jnp.bfloat16)
-        send_ref[span, 2] = dv_all[at : at + rows].astype(jnp.bfloat16)
+                shared[...] += term
     table[...] = jnp.zeros(table.shape, table.dtype)
     kinds = table.shape[0] // 2
     for slot in range(2):
@@ -447,60 +437,115 @@
         ref[...] = table[pl.ds(start, count)].astype(ref.dtype)
 
 
-def attend_head(chunks, chosen, place, rand_head, table_size, shares):
+def scores(chunks, chosen, place, rand_head, table_size, shares):
     spans = len(chunks)
     _, rows, head_size = chunks[0].shape
+    keys = 8 * BLK
     padded_rows = spans * rows + 2 * BLK
-    keys_each = spans * rows * 8 * BLK
-    share = jax.ShapeDtypeStruct((2 * table_size // shares, BLK, head_size), jnp.bfloat16)
-    outs = [jax.ShapeDtypeStruct((spans, 3, rows, head_size), jnp.bfloat16)] + [share] * shares
+    keys_each = spans * rows * keys
+    half = lambda *shape: jax.ShapeDtypeStruct(shape, jnp.bfloat16)
+    outs = [
+        half(spans * rows, head_size),
+        half(padded_rows, head_size),
+        half(spans * rows, head_size),
+        half(spans, keys, rows),
+        half(spans, keys, rows),
+    ] + [half(2 * table_size // shares, BLK, head_size)] * shares
     results = pl.pallas_call(
-        functools.partial(head_kernel, spans, shares),
+        functools.partial(score_kernel, spans, shares),
         in_specs=[pl.BlockSpec(memory_space=pltpu.SMEM)] * 2 + in_vmem(spans + 1),
         out_specs=in_vmem(len(outs)),
         out_shape=outs,
         scratch_shapes=[
-            pltpu.VMEM((spans * rows, head_size), jnp.bfloat16),
             pltpu.VMEM((padded_rows, head_size), jnp.bfloat16),
-            pltpu.VMEM((padded_rows, head_size), jnp.bfloat16),
-            pltpu.VMEM((spans * rows, head_size), jnp.bfloat16),
-            pltpu.VMEM((padded_rows, head_size), jnp.float32),
-            pltpu.VMEM((padded_rows, head_size), jnp.float32),
             pltpu.VMEM((2 * BLK, head_size), jnp.float32),
             pltpu.VMEM((2 * BLK, head_size), jnp.float32),
             pltpu.VMEM((2 * table_size, BLK, head_size), jnp.float32),
         ],
         compiler_params=pltpu.CompilerParams(vmem_limit_bytes=VMEM_BYTES),
         cost_estimate=pl.CostEstimate(
-            flops=10 * keys_each * head_size,
-            bytes_accessed=16 * spans * rows * head_size,
+            flops=4 * keys_each * head_size,
+            bytes_accessed=8 * spans * rows * head_size,
             transcendentals=keys_each,
         ),
-        name="attend_head",
+        name="scores",
     )(place, rand_head, *chunks, chosen)
-    return results[0], results[1:]
-
-
-def unpack_kernel(x_ref, dq_ref, dk_ref, dv_ref):
-    head_size = x_ref.shape[3]
-    for head in range(x_ref.shape[0]):
+    return results[:5], results[5:]
+
+
+def grad_kernel(rand_ref, g_ref, q_all, k_all, o_all, p_all, ds_all, send_ref, dk_all, dv_all):
+    spans, _, rows, head_size = send_ref.shape
+    rand_count = rand_ref.shape[0] // (2 * spans)
+    own = (1 + rand_count) * BLK
+    for pool in (dk_all, dv_all):
+        pool[...] = jnp.zeros(pool.shape, pool.dtype)
+    gk = [g_ref[0], g_ref[1]]
+    for span in range(spans):
+        at = span * rows
+        q = q_all[at : at + rows]
+        o = o_all[at : at + rows]
+        places = list_places(rand_ref, span, rand_count)
+        k_own, k_both = gathered(k_all, at, places, gk)
+        wide = dot(ds_all[span, :own], k_own, 0, 0)
+        dq = jnp.concatenate([wide[:BLK, :head_size], wide[BLK:, head_size:]], axis=0)
+        dq = dq + dot(ds_all[span, own:], k_both, 0, 0)
+        send_ref[span, 0] = dq.astype(send_ref.dtype)
+        for weights, x, pool in ((ds_all, q, dk_all), (p_all, o, dv_all)):
+            d_own = dot(weights[span, :own], split_rows(x), 1, 0)
+            d_both = dot(weights[span, own : own + 2 * BLK], x, 1, 0)
+            pool[at + BLK : at + 3 * BLK] += d_both
+            pool[at : at + BLK] += d_own[:BLK, :head_size]
+            pool[at + 3 * BLK : at + 4 * BLK] += d_own[:BLK, head_size:]
+            for half in range(2):
+                columns = slice(half * head_size, (half + 1) * head_size)
+                for slot, p in enumerate(places[half]):
+                    pool[pl.ds(p, BLK)] += d_own[(1 + slot) * BLK : (2 + slot) * BLK, columns]
+    for span in range(spans):
+        at = BLK + span * rows
+        send_ref[span, 1] = dk_all[at : at + rows].astype(send_ref.dtype)
+        send_ref[span, 2] = dv_all[at : at + rows].astype(send_ref.dtype)
+
+
+def grads(rand_head, chosen, held):
+    spans, keys, rows = held[3].shape
+    padded_rows, head_size = held[1].shape
+    keys_each = spans * keys * rows
+    return pl.pallas_call(
+        grad_kernel,
+        in_specs=[pl.BlockSpec(memory_space=pltpu.SMEM)] + in_vmem(1 + len(held)),
+        out_specs=pl.BlockSpec(memory_space=pltpu.VMEM),
+        out_shape=jax.ShapeDtypeStruct((spans, 3, rows, head_size), jnp.bfloat16),
+        scratch_shapes=[pltpu.VMEM((padded_rows, head_size), jnp.float32)] * 2,
+        compiler_params=pltpu.CompilerParams(vmem_limit_bytes=VMEM_BYTES),
+        cost_estimate=pl.CostEstimate(
+            flops=6 * keys_each * head_size,
+            bytes_accessed=8 * spans * rows * head_size,
+            transcendentals=0,
+        ),
+        name="grads",
+    )(rand_head, chosen, *held)
+
+
+def unpack_kernel(x_ref, *out_refs):
+    heads, _, _, head_size = x_ref.shape
+    for head in range(heads):
         columns = slice(head * head_size, (head + 1) * head_size)
-        for place, ref in enumerate((dq_ref, dk_ref, dv_ref)):
+        for place, ref in enumerate(out_refs):
             ref[0, :, columns] = x_ref[head, place]
 
 
 def unpack(x):
-    heads, _, rows, head_size = x.shape
+    heads, count, rows, head_size = x.shape
     shape = jax.ShapeDtypeStruct((1, rows, heads * head_size), x.dtype)
     return pl.pallas_call(
         unpack_kernel,
         grid=(1,),
-        in_specs=[pl.BlockSpec((heads, 3, rows, head_size), lambda i: (0, 0, 0, 0))],
-        out_specs=[pl.BlockSpec(shape.shape, lambda i: (0, 0, 0))] * 3,
-        out_shape=[shape] * 3,
+        in_specs=[pl.BlockSpec(x.shape, lambda i: (0, 0, 0, 0))],
+        out_specs=[pl.BlockSpec(shape.shape, lambda i: (0, 0, 0))] * count,
+        out_shape=[shape] * count,
         compiler_params=pltpu.CompilerParams(vmem_limit_bytes=VMEM_BYTES),
         cost_estimate=pl.CostEstimate(
-            flops=0, bytes_accessed=12 * rows * heads * head_size, transcendentals=0
+            flops=0, bytes_accessed=4 * count * rows * heads * head_size, transcendentals=0
         ),
         name="unpack_heads",
     )(x)
@@ -552,9 +597,12 @@
     place = jnp.concatenate([head[None], sequence[None], glob_ids[0]])
     rand_head = lax.dynamic_index_in_dim(rand_blocks, head, 0, keepdims=False).reshape(-1)
     rand_head = jnp.clip(rand_head, 0, block_count - 1)
-    chosen = choose(place, glob_keys, glob_values, head_size)
-    grads, terms = attend_head(chunks, chosen, place, rand_head, table_size, shares)
+    chosen, chunks[0] = choose(place, glob_keys, glob_values, packed[0])
+    held, terms = scores(chunks, chosen, place, rand_head, table_size, shares)
+    sent = grads(rand_head, chosen, held)
     terms = [flipped(terms[bits], "dp", bits) for bits in range(shares)]
+    *terms, sent = lax.optimization_barrier((*terms, sent))
+    back = lax.all_to_all(sent, "ctx", 0, 0)
     share = sum(term.astype(jnp.float32) for term in terms).astype(jnp.bfloat16)
     column = jnp.stack([flipped(share, "ctx", flip) for flip in HEADS_ORDER[:4]])
     quarter = jnp.concatenate([column, flipped(column, "ctx", 1)])
@@ -562,7 +610,6 @@
     beside = flipped(quarter, "dp", 1)
     corner = flipped(across, "dp", 1)
     d_table = whole_table([quarter, beside, across, corner])
-    back = lax.all_to_all(grads, "ctx", 0, 0)
     d_query, d_key, d_value = unpack(back)
     return (d_query, d_key, d_value, d_table.reshape((2,) + glob_keys.shape))
 

time: 73.6 us -> 70.5 us (0.958)
  waiting for transfers between devices: 24 us -> 19.8 us
  Pallas kernels: 11.5 us -> 12.5 us
    ppermute x17, waiting for transfers between devices: 24 us -> 19.8 us  [flipped(): lax.ppermute(array, axis, [(i, i ^ bits) for i in range(lax.axis_size(axi...]
    pallas_call x2 -> x3, Pallas kernels: 7.06 us -> 7.82 us  [the longest x1 4.04 us: scores(): pl.pallas_call(functools.partial(score_kernel, spans, shares), in_specs=[...]
  transfers between devices with their start and end apart: 18 -> 18, of which waited for: 7 -> 7; matrix products, arithmetic and copies ran while one was open for 1% -> 1% of each run, Pallas kernels for 3% -> 7%
where the time goes in v3:
time: 70.5 us; the launch traced here: 69.5 us
  starting transfers between devices  32.5 us (46%)
  waiting for transfers between devices  19.8 us (28%)
  Pallas kernels  12.5 us (18%)
  local copies, waits for them, and re-layouts  3.22 us (5%)
  other arithmetic  0.78 us (1%)
  between operations  0.76 us (1%)
    ppermute x17, starting transfers between devices, flipped(): lax.ppermute(array, axis, [(i, i ^ bits) for i in range(lax.axis_size(axi...  28.3 us
    ppermute x17, waiting for transfers between devices, flipped(): lax.ppermute(array, axis, [(i, i ^ bits) for i in range(lax.axis_size(axi...  19.8 us
    all_to_all x1, starting transfers between devices, on_heads(): back = lax.all_to_all(sent, 'ctx', 0, 0)  4.2 us
    pallas_call x1, Pallas kernels, scores(): pl.pallas_call(functools.partial(score_kernel, spans, shares), in_specs=[...  4.04 us
    unnamed x11, local copies, waits for them, and re-layouts  3.03 us
    pallas_call x1, Pallas kernels, grads(): pl.pallas_call(grad_kernel, in_specs=[pl.BlockSpec(memory_space=pltpu.SME...  2.69 us
    pallas_call x1, Pallas kernels, pack(): pl.pallas_call(functools.partial(pack_kernel, head_count), in_specs=[in_h...  2.29 us
    pallas_call x1, Pallas kernels, whole_table(): pl.pallas_call(table_kernel, grid=(1,), in_specs=[pl.BlockSpec(parts[0].s...  1.56 us
  transfers between devices with their start and end apart: 18, of which 7 were waited for; matrix products, arithmetic and copies ran while one was open for 1% of the time, Pallas kernels for 7%

profile of v3, /device:TPU:0, one launch (start us, length us, event | category | flops | bytes accessed | tf_op | source)
XLA Modules:
  0.0 69.5 jit_solution(8153666745352330753)
XLA Ops:
  0.6 2.3 %pack_heads.1 = (bf16[4,128,128]{2,1,0:T(8,128)(2,1)}, bf16[4,128,128]{2,1,0:T(8,128)(2,1)}, bf16[4,128,128]{2,1,0:T(8,128)(2,1)}, bf16[4,128,128]{2,1,0:T(8,128...) custom-call(bf16[1,128,1024]{2,1,0:T(8,128)(2,1)} %refs_0_.1, ...), custom_call_target="tpu_custom_call" | custom-call | bytes 2097152 | tf_op jit(solution)/shard_map/pack_heads/pallas_call | solution.py:277
  2.9 4.1 %collective-permute-start = (bf16[4,128,128]{2,1,0:T(8,128)(2,1)}, bf16[4,128,128]{2,1,0:T(8,128)(2,1)S(1)}, u32[]{:S(2)}, u32[]{:S(2)}) collective-permute-start(bf16[4,128,128]{2,1,0:T(8,128)(2,1)} %get-tuple-element.33), channel_id=1, source_target_pairs={{0,16},{4,20},{8,24},{12,28},{16,0},{20,4},{24,8},{28,12},{1,17},{... | collective-permute-start | bytes 393224 | tf_op jit(solution)/shard_map/ppermute | solution.py:585
  7.0 1.6 %collective-permute-start.1 = (bf16[4,128,128]{2,1,0:T(8,128)(2,1)}, bf16[4,128,128]{2,1,0:T(8,128)(2,1)S(1)}, u32[]{:S(2)}, u32[]{:S(2)}) collective-permute-start(bf16[4,128,128]{2,1,0:T(8,128)(2,1)} %get-tuple-element.34), channel_id=1, source_target_pairs={{0,8},{4,12},{8,0},{12,4},{16,24},{20,28},{24,16},{28,20},{1,9},{5... | collective-permute-start | bytes 393224 | tf_op jit(solution)/shard_map/ppermute | solution.py:585
  8.6 1.3 %collective-permute-start.2 = (bf16[4,128,128]{2,1,0:T(8,128)(2,1)}, bf16[4,128,128]{2,1,0:T(8,128)(2,1)S(1)}, u32[]{:S(2)}, u32[]{:S(2)}) collective-permute-start(bf16[4,128,128]{2,1,0:T(8,128)(2,1)} %get-tuple-element.35), channel_id=1, source_target_pairs={{0,20},{4,16},{8,28},{12,24},{16,4},{20,0},{24,12},{28,8},{1,21},{... | collective-permute-start | bytes 393224 | tf_op jit(solution)/shard_map/ppermute | solution.py:585
  10.0 3.9 %collective-permute-start.4 = (bf16[4,128,128]{2,1,0:T(8,128)(2,1)}, bf16[4,128,128]{2,1,0:T(8,128)(2,1)S(1)}, u32[]{:S(2)}, u32[]{:S(2)}) collective-permute-start(bf16[4,128,128]{2,1,0:T(8,128)(2,1)} %get-tuple-element.37), channel_id=1, source_target_pairs={{0,24},{4,28},{8,16},{12,20},{16,8},{20,12},{24,0},{28,4},{1,25},{... | collective-permute-start | bytes 393224 | tf_op jit(solution)/shard_map/ppermute | solution.py:585
  13.9 1.1 %collective-permute-done.refs_1_ = bf16[4,128,128]{2,1,0:T(8,128)(2,1)S(1)} collective-permute-done((bf16[4,128,128]{2,1,0:T(8,128)(2,1)}, bf16[4,128,128]{2,1,0:T(8,128)(2,1)S(1)}, u32[]{:S(2)}, u32[]{:S(2)}) %collective-permute-start) | collective-permute-done | bytes 131104 | tf_op jit(solution)/shard_map/ppermute | solution.py:585
  15.0 4.2 %collective-permute-start.5 = (bf16[4,128,128]{2,1,0:T(8,128)(2,1)}, bf16[4,128,128]{2,1,0:T(8,128)(2,1)S(1)}, u32[]{:S(2)}, u32[]{:S(2)}) collective-permute-start(bf16[4,128,128]{2,1,0:T(8,128)(2,1)} %get-tuple-element.38), channel_id=1, source_target_pairs={{0,28},{4,24},{8,20},{12,16},{16,12},{20,8},{24,4},{28,0},{1,29},{... | collective-permute-start | bytes 393224 | tf_op jit(solution)/shard_map/ppermute | solution.py:585
  20.7 1.0 %copy-done.1 = bf16[4,64,1024]{2,1,0:T(8,128)(2,1)S(1)} copy-done((bf16[4,64,1024]{2,1,0:T(8,128)(2,1)S(1)}, bf16[4,64,1024]{2,1,0:T(8,128)(2,1)}, u32[]{:S(2)}) %copy-start.1) | copy-done | bytes 524312
  21.8 1.0 %copy-done.2 = bf16[4,64,1024]{2,1,0:T(8,128)(2,1)S(1)} copy-done((bf16[4,64,1024]{2,1,0:T(8,128)(2,1)S(1)}, bf16[4,64,1024]{2,1,0:T(8,128)(2,1)}, u32[]{:S(2)}) %copy-start.2) | copy-done | bytes 524312
  22.8 0.9 %copy-done.3 = bf16[4,128,128]{2,1,0:T(8,128)(2,1)S(1)} copy-done((bf16[4,128,128]{2,1,0:T(8,128)(2,1)S(1)}, bf16[4,128,128]{2,1,0:T(8,128)(2,1)}, u32[]{:S(2)}) %copy-start.3) | copy-done | bytes 131096
  24.5 2.5 %collective-permute-done.5.refs_6_ = bf16[4,128,128]{2,1,0:T(8,128)(2,1)S(1)} collective-permute-done((bf16[4,128,128]{2,1,0:T(8,128)(2,1)}, bf16[4,128,128]{2,1,0:T(8,128)(2,1)S(1)}, u32[]{:S(2)}, u32[]{:S(2)}) %collective-permute-start.5) | collective-permute-done | bytes 131104 | tf_op jit(solution)/shard_map/ppermute | solution.py:585
  27.4 4.0 %scores.1 = (bf16[1024,128]{1,0:T(8,128)(2,1)S(1)}, bf16[1152,128]{1,0:T(8,128)(2,1)S(1)}, bf16[1024,128]{1,0:T(8,128)(2,1)S(1)}, bf16[8,512,128]{2,1,0:T(8,128)...) custom-call(s32[4]{0:T(128)S(1)} %pad_add_fusion.place_ref, ...), custom_call_target="tpu_custom_call" | custom-call | flops 268435456 | bytes 1048576 | tf_op jit(solution)/shard_map/scores/pallas_call | solution.py:454
  31.6 1.6 %collective-permute-start.8 = (bf16[2,64,128]{2,1,0:T(8,128)(2,1)S(1)}, bf16[2,64,128]{2,1,0:T(8,128)(2,1)S(1)}, u32[]{:S(2)}, u32[]{:S(2)}) collective-permute-start(bf16[2,64,128]{2,1,0:T(8,128)(2,1)S(1)} %get-tuple-element.43), channel_id=1, source_target_pairs={{0,2},{1,3},{2,0},{3,1},{4,6},{5,7},{6,4},{7,5},{8,10},{9,11},{10,... | collective-permute-start | bytes 98312 | tf_op jit(solution)/shard_map/ppermute | solution.py:585
  33.4 2.7 %grads.1 = bf16[8,3,128,128]{3,2,1,0:T(8,128)(2,1)} custom-call(s32[48]{0:T(128)S(1)} %min.12.rand_ref, bf16[4,64,128]{2,1,0:T(8,128)(2,1)S(1)} %get-tuple-element.40.refs_8_.g_ref, bf16[1024,128]{1,0:T(8,128)(2,1)S(1)} %get-tuple-element.45.q_all, bf16[1152,128]{1,0:T(8,128)(2,1)S(1)} %get-tuple-element.46.k_all, ...), custom_call_target="tpu_custom_call" | custom-call | flops 402653184 | bytes 1048576 | tf_op jit(solution)/shard_map/grads/pallas_call | solution.py:513
  36.5 2.0 %collective-permute-start.12 = (bf16[2,64,128]{2,1,0:T(8,128)(2,1)S(1)}, bf16[2,64,128]{2,1,0:T(8,128)(2,1)S(1)}, u32[]{:S(2)}, u32[]{:S(2)}) collective-permute-start(bf16[2,64,128]{2,1,0:T(8,128)(2,1)S(1)} %get-tuple-element.59), channel_id=1, source_target_pairs={{0,24},{4,28},{8,16},{12,20},{16,8},{20,12},{24,0},{28,4},{1,25},{... | collective-permute-start | bytes 98312 | tf_op jit(solution)/shard_map/ppermute | solution.py:585
  38.5 4.7 %collective-permute-start.11 = (bf16[2,64,128]{2,1,0:T(8,128)(2,1)S(1)}, bf16[2,64,128]{2,1,0:T(8,128)(2,1)S(1)}, u32[]{:S(2)}, u32[]{:S(2)}) collective-permute-start(bf16[2,64,128]{2,1,0:T(8,128)(2,1)S(1)} %get-tuple-element.59), channel_id=1, source_target_pairs={{0,16},{4,20},{8,24},{12,28},{16,0},{20,4},{24,8},{28,12},{1,17},{... | collective-permute-start | bytes 98312 | tf_op jit(solution)/shard_map/ppermute | solution.py:585
  43.7 4.2 %all-to-all-start = ((bf16[8,3,128,128]{3,2,1,0:T(8,128)(2,1)}), bf16[8,3,128,128]{3,2,1,0:T(8,128)(2,1)S(1)}, u32[]{:S(2)}, u32[]{:S(2)}) async-start(bf16[8,3,128,128]{3,2,1,0:T(8,128)(2,1)} %grads.1), calls=%async_computation | async-start | bytes 1572864 | tf_op jit(solution)/shard_map/all_to_all | solution.py:605
  48.0 2.1 %collective-permute-start.13 = (bf16[4,2,64,128]{3,2,1,0:T(8,128)(2,1)S(1)}, bf16[4,2,64,128]{3,2,1,0:T(8,128)(2,1)S(1)}, u32[]{:S(2)}, u32[]{:S(2)}) collective-permute-start(bf16[4,2,64,128]{3,2,1,0:T(8,128)(2,1)S(1)} %pad_maximum_fusion), channel_id=1, source_target_pairs={{0,4},{4,0},{8,12},{12,8},{16,20},{20,16},{24,28},{28,24},{1,5},{5... | collective-permute-start | bytes 393224 | tf_op jit(solution)/shard_map/ppermute | solution.py:585
  50.1 8.8 %collective-permute-done.13 = bf16[4,2,64,128]{3,2,1,0:T(8,128)(2,1)S(1)} collective-permute-done((bf16[4,2,64,128]{3,2,1,0:T(8,128)(2,1)S(1)}, bf16[4,2,64,128]{3,2,1,0:T(8,128)(2,1)S(1)}, u32[]{:S(2)}, u32[]{:S(2)}) %collective-permute-start.13) | collective-permute-done | bytes 131104 | tf_op jit(solution)/shard_map/ppermute | solution.py:585
  58.9 1.4 %collective-permute-start.15 = (bf16[8,2,64,128]{3,2,1,0:T(8,128)(2,1)S(1)}, bf16[8,2,64,128]{3,2,1,0:T(8,128)(2,1)S(1)}, u32[]{:S(2)}, u32[]{:S(2)}) collective-permute-start(bf16[8,2,64,128]{3,2,1,0:T(8,128)(2,1)S(1)} %constant_dynamic-update-slice_fusion.refs_0_), channel_id=1, source_target_pairs={{0,2},{1,3},{2,0},{3,1},{4,6},{5,7},{6,4},{7,5},{8,10},{9,11},{10,... | collective-permute-start | bytes 786440 | tf_op jit(solution)/shard_map/ppermute | solution.py:585
  60.3 5.0 %collective-permute-done.15.refs_2_ = bf16[8,2,64,128]{3,2,1,0:T(8,128)(2,1)S(1)} collective-permute-done((bf16[8,2,64,128]{3,2,1,0:T(8,128)(2,1)S(1)}, bf16[8,2,64,128]{3,2,1,0:T(8,128)(2,1)S(1)}, u32[]{:S(2)}, u32[]{:S(2)}) %collective-permute-start.15) | collective-permute-done | bytes 262176 | tf_op jit(solution)/shard_map/ppermute | solution.py:585
  65.3 1.5 %collective-permute-done.16.refs_3_ = bf16[8,2,64,128]{3,2,1,0:T(8,128)(2,1)S(1)} collective-permute-done((bf16[8,2,64,128]{3,2,1,0:T(8,128)(2,1)S(1)}, bf16[8,2,64,128]{3,2,1,0:T(8,128)(2,1)S(1)}, u32[]{:S(2)}, u32[]{:S(2)}) %collective-permute-start.16) | collective-permute-done | bytes 262176 | tf_op jit(solution)/shard_map/ppermute | solution.py:585
  66.9 1.6 %whole_table.1 = f32[8,64,1024]{2,1,0:T(8,128)} custom-call(bf16[8,2,64,128]{3,2,1,0:T(8,128)(2,1)S(1)} %constant_dynamic-update-slice_fusion.refs_0_, bf16[8,2,64,128]{3,2,1,0:T(8,128)(2,1)S(1)} %collective-permute-done.14.refs_1_, bf16[8,2,64,128]{3,2,1,0:T(8,128)(2,1)S(1)} %collective-permute-done.15.refs_2_, ...), custom_call_target="tpu_custom_call" | custom-call | tf_op jit(solution)/shard_map/whole_table/pallas_call | solution.py:571
  68.4 1.1 %unpack_heads.1 = (bf16[1,128,1024]{2,1,0:T(8,128)(2,1)}, bf16[1,128,1024]{2,1,0:T(8,128)(2,1)}, bf16[1,128,1024]{2,1,0:T(8,128)(2,1)}) custom-call(bf16[8,3,128,128]{3,2,1,0:T(8,128)(2,1)S(1)} %all-to-all-done.x_ref), custom_call_target="tpu_custom_call" | custom-call | bytes 1572864 | tf_op jit(solution)/shard_map/unpack_heads/pallas_call | solution.py:540
  (37 shorter events, 4.2 us)
Async XLA Ops:
  0.6 13.3 %copy-start = (s32[8,16,3]{1,0,2:T(8,128)S(1)}, s32[8,16,3]{1,0,2:T(8,128)}, u32[]{:S(2)}) copy-start(s32[8,16,3]{1,0,2:T(8,128)} %param.15) | copy-start | bytes 4612
  2.9 12.1 %collective-permute-start = (bf16[4,128,128]{2,1,0:T(8,128)(2,1)}, bf16[4,128,128]{2,1,0:T(8,128)(2,1)S(1)}, u32[]{:S(2)}, u32[]{:S(2)}) collective-permute-start(bf16[4,128,128]{2,1,0:T(8,128)(2,1)} %get-tuple-element.33), channel_id=1, source_target_pairs={{0,16},{4,20},{8,24},{12,28},{16,0},{20,4},{24,8},{28,12},{1,17},{... | collective-permute-start | bytes 393224 | tf_op jit(solution)/shard_map/ppermute | solution.py:585
  7.0 12.2 %collective-permute-start.1 = (bf16[4,128,128]{2,1,0:T(8,128)(2,1)}, bf16[4,128,128]{2,1,0:T(8,128)(2,1)S(1)}, u32[]{:S(2)}, u32[]{:S(2)}) collective-permute-start(bf16[4,128,128]{2,1,0:T(8,128)(2,1)} %get-tuple-element.34), channel_id=1, source_target_pairs={{0,8},{4,12},{8,0},{12,4},{16,24},{20,28},{24,16},{28,20},{1,9},{5... | collective-permute-start | bytes 393224 | tf_op jit(solution)/shard_map/ppermute | solution.py:585
  8.6 15.9 %collective-permute-start.2 = (bf16[4,128,128]{2,1,0:T(8,128)(2,1)}, bf16[4,128,128]{2,1,0:T(8,128)(2,1)S(1)}, u32[]{:S(2)}, u32[]{:S(2)}) collective-permute-start(bf16[4,128,128]{2,1,0:T(8,128)(2,1)} %get-tuple-element.35), channel_id=1, source_target_pairs={{0,20},{4,16},{8,28},{12,24},{16,4},{20,0},{24,12},{28,8},{1,21},{... | collective-permute-start | bytes 393224 | tf_op jit(solution)/shard_map/ppermute | solution.py:585
  9.9 14.6 %collective-permute-start.3 = (bf16[4,128,128]{2,1,0:T(8,128)(2,1)}, bf16[4,128,128]{2,1,0:T(8,128)(2,1)S(1)}, u32[]{:S(2)}, u32[]{:S(2)}) collective-permute-start(bf16[4,128,128]{2,1,0:T(8,128)(2,1)} %get-tuple-element.36), channel_id=1, source_target_pairs={{0,12},{4,8},{8,4},{12,0},{16,28},{20,24},{24,20},{28,16},{1,13},{... | collective-permute-start | bytes 393224 | tf_op jit(solution)/shard_map/ppermute | solution.py:585
  10.0 14.5 %collective-permute-start.4 = (bf16[4,128,128]{2,1,0:T(8,128)(2,1)}, bf16[4,128,128]{2,1,0:T(8,128)(2,1)S(1)}, u32[]{:S(2)}, u32[]{:S(2)}) collective-permute-start(bf16[4,128,128]{2,1,0:T(8,128)(2,1)} %get-tuple-element.37), channel_id=1, source_target_pairs={{0,24},{4,28},{8,16},{12,20},{16,8},{20,12},{24,0},{28,4},{1,25},{... | collective-permute-start | bytes 393224 | tf_op jit(solution)/shard_map/ppermute | solution.py:585
  15.0 12.0 %collective-permute-start.5 = (bf16[4,128,128]{2,1,0:T(8,128)(2,1)}, bf16[4,128,128]{2,1,0:T(8,128)(2,1)S(1)}, u32[]{:S(2)}, u32[]{:S(2)}) collective-permute-start(bf16[4,128,128]{2,1,0:T(8,128)(2,1)} %get-tuple-element.38), channel_id=1, source_target_pairs={{0,28},{4,24},{8,20},{12,16},{16,12},{20,8},{24,4},{28,0},{1,29},{... | collective-permute-start | bytes 393224 | tf_op jit(solution)/shard_map/ppermute | solution.py:585
  19.3 8.2 %collective-permute-start.6 = (bf16[4,128,128]{2,1,0:T(8,128)(2,1)}, bf16[4,128,128]{2,1,0:T(8,128)(2,1)S(1)}, u32[]{:S(2)}, u32[]{:S(2)}) collective-permute-start(bf16[4,128,128]{2,1,0:T(8,128)(2,1)} %get-tuple-element.39), channel_id=1, source_target_pairs={{0,4},{4,0},{8,12},{12,8},{16,20},{20,16},{24,28},{28,24},{1,5},{5... | collective-permute-start | bytes 393224 | tf_op jit(solution)/shard_map/ppermute | solution.py:585
  20.7 1.0 %copy-start.1 = (bf16[4,64,1024]{2,1,0:T(8,128)(2,1)S(1)}, bf16[4,64,1024]{2,1,0:T(8,128)(2,1)}, u32[]{:S(2)}) copy-start(bf16[4,64,1024]{2,1,0:T(8,128)(2,1)} %gk_ref.1) | copy-start | bytes 1572868
  21.8 1.0 %copy-start.2 = (bf16[4,64,1024]{2,1,0:T(8,128)(2,1)S(1)}, bf16[4,64,1024]{2,1,0:T(8,128)(2,1)}, u32[]{:S(2)}) copy-start(bf16[4,64,1024]{2,1,0:T(8,128)(2,1)} %gv_ref.1) | copy-start | bytes 1572868
  22.8 0.9 %copy-start.3 = (bf16[4,128,128]{2,1,0:T(8,128)(2,1)S(1)}, bf16[4,128,128]{2,1,0:T(8,128)(2,1)}, u32[]{:S(2)}) copy-start(bf16[4,128,128]{2,1,0:T(8,128)(2,1)} %get-tuple-element.31.own_ref) | copy-start | bytes 393220
  31.5 4.6 %collective-permute-start.7 = (bf16[2,64,128]{2,1,0:T(8,128)(2,1)S(1)}, bf16[2,64,128]{2,1,0:T(8,128)(2,1)S(1)}, u32[]{:S(2)}, u32[]{:S(2)}) collective-permute-start(bf16[2,64,128]{2,1,0:T(8,128)(2,1)S(1)} %get-tuple-element.42), channel_id=1, source_target_pairs={{0,1},{1,0},{2,3},{3,2},{4,5},{5,4},{6,7},{7,6},{8,9},{9,8},{10,11... | collective-permute-start | bytes 98312 | tf_op jit(solution)/shard_map/ppermute | solution.py:585
  31.6 4.6 %collective-permute-start.8 = (bf16[2,64,128]{2,1,0:T(8,128)(2,1)S(1)}, bf16[2,64,128]{2,1,0:T(8,128)(2,1)S(1)}, u32[]{:S(2)}, u32[]{:S(2)}) collective-permute-start(bf16[2,64,128]{2,1,0:T(8,128)(2,1)S(1)} %get-tuple-element.43), channel_id=1, source_target_pairs={{0,2},{1,3},{2,0},{3,1},{4,6},{5,7},{6,4},{7,5},{8,10},{9,11},{10,... | collective-permute-start | bytes 98312 | tf_op jit(solution)/shard_map/ppermute | solution.py:585
  33.2 3.3 %collective-permute-start.9 = (bf16[2,64,128]{2,1,0:T(8,128)(2,1)S(1)}, bf16[2,64,128]{2,1,0:T(8,128)(2,1)S(1)}, u32[]{:S(2)}, u32[]{:S(2)}) collective-permute-start(bf16[2,64,128]{2,1,0:T(8,128)(2,1)S(1)} %get-tuple-element.44), channel_id=1, source_target_pairs={{0,3},{1,2},{2,1},{3,0},{4,7},{5,6},{6,5},{7,4},{8,11},{9,10},{10,... | collective-permute-start | bytes 98312 | tf_op jit(solution)/shard_map/ppermute | solution.py:585
  36.5 11.4 %collective-permute-start.12 = (bf16[2,64,128]{2,1,0:T(8,128)(2,1)S(1)}, bf16[2,64,128]{2,1,0:T(8,128)(2,1)S(1)}, u32[]{:S(2)}, u32[]{:S(2)}) collective-permute-start(bf16[2,64,128]{2,1,0:T(8,128)(2,1)S(1)} %get-tuple-element.59), channel_id=1, source_target_pairs={{0,24},{4,28},{8,16},{12,20},{16,8},{20,12},{24,0},{28,4},{1,25},{... | collective-permute-start | bytes 98312 | tf_op jit(solution)/shard_map/ppermute | solution.py:585
  38.5 9.4 %collective-permute-start.11 = (bf16[2,64,128]{2,1,0:T(8,128)(2,1)S(1)}, bf16[2,64,128]{2,1,0:T(8,128)(2,1)S(1)}, u32[]{:S(2)}, u32[]{:S(2)}) collective-permute-start(bf16[2,64,128]{2,1,0:T(8,128)(2,1)S(1)} %get-tuple-element.59), channel_id=1, source_target_pairs={{0,16},{4,20},{8,24},{12,28},{16,0},{20,4},{24,8},{28,12},{1,17},{... | collective-permute-start | bytes 98312 | tf_op jit(solution)/shard_map/ppermute | solution.py:585
  43.2 4.7 %collective-permute-start.10 = (bf16[2,64,128]{2,1,0:T(8,128)(2,1)S(1)}, bf16[2,64,128]{2,1,0:T(8,128)(2,1)S(1)}, u32[]{:S(2)}, u32[]{:S(2)}) collective-permute-start(bf16[2,64,128]{2,1,0:T(8,128)(2,1)S(1)} %get-tuple-element.59), channel_id=1, source_target_pairs={{0,8},{4,12},{8,0},{12,4},{16,24},{20,28},{24,16},{28,20},{1,9},{5... | collective-permute-start | bytes 98312 | tf_op jit(solution)/shard_map/ppermute | solution.py:585
  43.7 24.7 %all-to-all-start = ((bf16[8,3,128,128]{3,2,1,0:T(8,128)(2,1)}), bf16[8,3,128,128]{3,2,1,0:T(8,128)(2,1)S(1)}, u32[]{:S(2)}, u32[]{:S(2)}) async-start(bf16[8,3,128,128]{3,2,1,0:T(8,128)(2,1)} %grads.1), calls=%async_computation | async-start | bytes 1572864 | tf_op jit(solution)/shard_map/all_to_all | solution.py:605
  48.0 10.9 %collective-permute-start.13 = (bf16[4,2,64,128]{3,2,1,0:T(8,128)(2,1)S(1)}, bf16[4,2,64,128]{3,2,1,0:T(8,128)(2,1)S(1)}, u32[]{:S(2)}, u32[]{:S(2)}) collective-permute-start(bf16[4,2,64,128]{3,2,1,0:T(8,128)(2,1)S(1)} %pad_maximum_fusion), channel_id=1, source_target_pairs={{0,4},{4,0},{8,12},{12,8},{16,20},{20,16},{24,28},{28,24},{1,5},{5... | collective-permute-start | bytes 393224 | tf_op jit(solution)/shard_map/ppermute | solution.py:585
  58.9 6.4 %collective-permute-start.15 = (bf16[8,2,64,128]{3,2,1,0:T(8,128)(2,1)S(1)}, bf16[8,2,64,128]{3,2,1,0:T(8,128)(2,1)S(1)}, u32[]{:S(2)}, u32[]{:S(2)}) collective-permute-start(bf16[8,2,64,128]{3,2,1,0:T(8,128)(2,1)S(1)} %constant_dynamic-update-slice_fusion.refs_0_), channel_id=1, source_target_pairs={{0,2},{1,3},{2,0},{3,1},{4,6},{5,7},{6,4},{7,5},{8,10},{9,11},{10,... | collective-permute-start | bytes 786440 | tf_op jit(solution)/shard_map/ppermute | solution.py:585
  60.3 5.0 %collective-permute-start.14 = (bf16[8,2,64,128]{3,2,1,0:T(8,128)(2,1)S(1)}, bf16[8,2,64,128]{3,2,1,0:T(8,128)(2,1)S(1)}, u32[]{:S(2)}, u32[]{:S(2)}) collective-permute-start(bf16[8,2,64,128]{3,2,1,0:T(8,128)(2,1)S(1)} %constant_dynamic-update-slice_fusion.refs_0_), channel_id=1, source_target_pairs={{0,1},{1,0},{2,3},{3,2},{4,5},{5,4},{6,7},{7,6},{8,9},{9,8},{10,11... | collective-permute-start | bytes 786440 | tf_op jit(solution)/shard_map/ppermute | solution.py:585
  65.3 1.5 %collective-permute-start.16 = (bf16[8,2,64,128]{3,2,1,0:T(8,128)(2,1)S(1)}, bf16[8,2,64,128]{3,2,1,0:T(8,128)(2,1)S(1)}, u32[]{:S(2)}, u32[]{:S(2)}) collective-permute-start(bf16[8,2,64,128]{3,2,1,0:T(8,128)(2,1)S(1)} %collective-permute-done.15.refs_2_), channel_id=1, source_target_pairs={{0,1},{1,0},{2,3},{3,2},{4,5},{5,4},{6,7},{7,6},{8,9},{9,8},{10,11... | collective-permute-start | bytes 786440 | tf_op jit(solution)/shard_map/ppermute | solution.py:585

commit v4 on v3

--- a/solution.py
+++ b/solution.py
@@ -232,9 +232,12 @@
 VMEM_BYTES = 24 * 1024 * 1024
 SMALL_VMEM_BYTES = 4 * 1024 * 1024
 LARGE_VMEM_BYTES = 60 * 1024 * 1024
+FINISH_VMEM_BYTES = 24 * 1024 * 1024
 MASKED = -1e30
+EARLY_FLOPS = 5 * 10**9
+GROUP = 8
 ORDER = (0, 4, 2, 5, 3, 6, 7, 1)
-HEADS_ORDER = (0, 2, 4, 6, 1, 3, 5, 7)
+COLUMN = (0, 2, 4, 6)
 
 
 def dot(left, right, left_dim, right_dim):
@@ -365,7 +368,7 @@
     x_refs, g_ref = refs[:spans], refs[spans]
     q_all, k_all, o_all, p_all, ds_all = refs[spans + 1 : spans + 6]
     share_refs = refs[spans + 6 : spans + 6 + shares]
-    v_all, dgk, dgv, table = refs[spans + 6 + shares :]
+    v_all, table = refs[spans + 6 + shares :]
     _, rows, head_size = x_refs[0].shape
     rand_count = rand_ref.shape[0] // (2 * spans)
     scaling = 1.0 / math.sqrt(head_size)
@@ -384,51 +387,67 @@
     gv = [g_ref[2], g_ref[3]]
     own = (1 + rand_count) * BLK
     first = lax.broadcasted_iota(jnp.int32, (1, rows), 1) < BLK
-    for span in range(spans):
-        at = span * rows
-        q = q_all[at : at + rows]
-        o = o_all[at : at + rows]
-        places = list_places(rand_ref, span, rand_count)
-        k_own, k_both = gathered(k_all, at, places, gk)
-        v_own, v_both = gathered(v_all, at, places, gv)
-        s_own = dot(k_own, split_rows(q), 1, 1) * scaling
-        s_both = dot(k_both, q, 1, 1) * scaling
-        if span == 0 or span == spans - 1:
-            row = lax.broadcasted_iota(jnp.int32, (own, 1), 0) < BLK
-            outside = row & (first if span == 0 else jnp.logical_not(first))
-            s_own = jnp.where(outside, MASKED, s_own)
-        top_score = jnp.maximum(
-            jnp.max(s_own, axis=0, keepdims=True), jnp.max(s_both, axis=0, keepdims=True)
-        )
-        e_own = jnp.exp(s_own - top_score)
-        e_both = jnp.exp(s_both - top_score)
-        total = jnp.sum(e_own, axis=0, keepdims=True) + jnp.sum(e_both, axis=0, keepdims=True)
-        inverse = 1.0 / total
-        p_own = e_own * inverse
-        p_both = e_both * inverse
-        pb_own = p_own.astype(jnp.bfloat16)
-        pb_both = p_both.astype(jnp.bfloat16)
-        g_own = dot(v_own, split_rows(o), 1, 1)
-        g_both = dot(v_both, o, 1, 1)
-        row_dot = jnp.sum(pb_own.astype(jnp.float32) * g_own, axis=0, keepdims=True) + jnp.sum(
-            pb_both.astype(jnp.float32) * g_both, axis=0, keepdims=True
-        )
-        ds_own = (p_own * (g_own - row_dot) * scaling).astype(jnp.bfloat16)
-        ds_both = (p_both * (g_both - row_dot) * scaling).astype(jnp.bfloat16)
-        p_all[span, :own] = pb_own
-        p_all[span, own:] = pb_both
-        ds_all[span, :own] = ds_own
-        ds_all[span, own:] = ds_both
-        for weights, x, shared in ((ds_both, q, dgk), (pb_both, o, dgv)):
-            term = dot(weights[2 * BLK :], x, 1, 0)
-            if span == 0:
-                shared[...] = term
-            else:
-                shared[...] += term
+    table_terms = [None, None]
+    for group in range(0, spans, GROUP):
+        members = range(group, min(group + GROUP, spans))
+        made = []
+        for span in members:
+            at = span * rows
+            q = q_all[at : at + rows]
+            o = o_all[at : at + rows]
+            places = list_places(rand_ref, span, rand_count)
+            k_own, k_both = gathered(k_all, at, places, gk)
+            v_own, v_both = gathered(v_all, at, places, gv)
+            s_own = dot(k_own, split_rows(q), 1, 1) * scaling
+            s_both = dot(k_both, q, 1, 1) * scaling
+            g_own = dot(v_own, split_rows(o), 1, 1)
+            g_both = dot(v_both, o, 1, 1)
+            if span == 0 or span == spans - 1:
+                row = lax.broadcasted_iota(jnp.int32, (own, 1), 0) < BLK
+                outside = row & (first if span == 0 else jnp.logical_not(first))
+                s_own = jnp.where(outside, MASKED, s_own)
+            made.append((q, o, s_own, s_both, g_own, g_both))
+        tops = [
+            jnp.maximum(
+                jnp.max(s_own, axis=0, keepdims=True), jnp.max(s_both, axis=0, keepdims=True)
+            )
+            for _, _, s_own, s_both, _, _ in made
+        ]
+        powers = [
+            (jnp.exp(s_own - top_score), jnp.exp(s_both - top_score))
+            for top_score, (_, _, s_own, s_both, _, _) in zip(tops, made)
+        ]
+        inverses = [
+            1.0 / (jnp.sum(e_own, axis=0, keepdims=True) + jnp.sum(e_both, axis=0, keepdims=True))
+            for e_own, e_both in powers
+        ]
+        weights = []
+        for (e_own, e_both), inverse, (_, _, _, _, g_own, g_both) in zip(powers, inverses, made):
+            p_own = e_own * inverse
+            p_both = e_both * inverse
+            pb_own = p_own.astype(jnp.bfloat16)
+            pb_both = p_both.astype(jnp.bfloat16)
+            row_dot = jnp.sum(
+                pb_own.astype(jnp.float32) * g_own, axis=0, keepdims=True
+            ) + jnp.sum(pb_both.astype(jnp.float32) * g_both, axis=0, keepdims=True)
+            weights.append((p_own, p_both, pb_own, pb_both, row_dot))
+        for span, (q, o, _, _, g_own, g_both), (p_own, p_both, pb_own, pb_both, row_dot) in zip(
+            members, made, weights
+        ):
+            ds_own = (p_own * (g_own - row_dot) * scaling).astype(jnp.bfloat16)
+            ds_both = (p_both * (g_both - row_dot) * scaling).astype(jnp.bfloat16)
+            p_all[span, :own] = pb_own
+            p_all[span, own:] = pb_both
+            ds_all[span, :own] = ds_own
+            ds_all[span, own:] = ds_both
+            for kind, (weight, x) in enumerate(((ds_both, q), (pb_both, o))):
+                term = dot(weight[2 * BLK :], x, 1, 0)
+                so_far = table_terms[kind]
+                table_terms[kind] = term if so_far is None else so_far + term
     table[...] = jnp.zeros(table.shape, table.dtype)
     kinds = table.shape[0] // 2
     for slot in range(2):
-        for kind, shared in enumerate((dgk, dgv)):
+        for kind, shared in enumerate(table_terms):
             block = shared[slot * BLK : (slot + 1) * BLK]
             table[kind * kinds + place_ref[2 + slot]] = block
     for flip, ref in enumerate(share_refs):
@@ -458,8 +477,6 @@
         out_shape=outs,
         scratch_shapes=[
             pltpu.VMEM((padded_rows, head_size), jnp.bfloat16),
-            pltpu.VMEM((2 * BLK, head_size), jnp.float32),
-            pltpu.VMEM((2 * BLK, head_size), jnp.float32),
             pltpu.VMEM((2 * table_size, BLK, head_size), jnp.float32),
         ],
         compiler_params=pltpu.CompilerParams(vmem_limit_bytes=VMEM_BYTES),
@@ -473,49 +490,80 @@
     return results[:5], results[5:]
 
 
-def grad_kernel(rand_ref, g_ref, q_all, k_all, o_all, p_all, ds_all, send_ref, dk_all, dv_all):
-    spans, _, rows, head_size = send_ref.shape
+def far_spans(spans, rand_count):
+    return [(slot + 1) * spans // (rand_count + 1) for slot in range(rand_count)]
+
+
+def grad_kernel(
+    rand_ref, g_ref, q_all, k_all, o_all, p_all, ds_all, out_ref, made, sems
+):
+    spans, _, rows, head_size = made.shape
     rand_count = rand_ref.shape[0] // (2 * spans)
     own = (1 + rand_count) * BLK
-    for pool in (dk_all, dv_all):
-        pool[...] = jnp.zeros(pool.shape, pool.dtype)
     gk = [g_ref[0], g_ref[1]]
+    offsets = far_spans(spans, rand_count)
+    first = lax.broadcasted_iota(jnp.int32, (1, rows), 1) < BLK
+    terms = []
     for span in range(spans):
         at = span * rows
         q = q_all[at : at + rows]
         o = o_all[at : at + rows]
-        places = list_places(rand_ref, span, rand_count)
-        k_own, k_both = gathered(k_all, at, places, gk)
+        k_own, k_both = gathered(k_all, at, list_places(rand_ref, span, rand_count), gk)
         wide = dot(ds_all[span, :own], k_own, 0, 0)
         dq = jnp.concatenate([wide[:BLK, :head_size], wide[BLK:, head_size:]], axis=0)
         dq = dq + dot(ds_all[span, own:], k_both, 0, 0)
-        send_ref[span, 0] = dq.astype(send_ref.dtype)
-        for weights, x, pool in ((ds_all, q, dk_all), (p_all, o, dv_all)):
-            d_own = dot(weights[span, :own], split_rows(x), 1, 0)
-            d_both = dot(weights[span, own : own + 2 * BLK], x, 1, 0)
-            pool[at + BLK : at + 3 * BLK] += d_both
-            pool[at : at + BLK] += d_own[:BLK, :head_size]
-            pool[at + 3 * BLK : at + 4 * BLK] += d_own[:BLK, head_size:]
-            for half in range(2):
-                columns = slice(half * head_size, (half + 1) * head_size)
-                for slot, p in enumerate(places[half]):
-                    pool[pl.ds(p, BLK)] += d_own[(1 + slot) * BLK : (2 + slot) * BLK, columns]
+        made[span, 0] = dq.astype(made.dtype)
+        keeps = [first]
+        for slot, offset in enumerate(offsets):
+            lower = [
+                rand_ref[(2 * span + half) * rand_count + slot] == 2 * ((span + offset) % spans)
+                for half in range(2)
+            ]
+            keeps.append((first & lower[0]) | (jnp.logical_not(first) & lower[1]))
+        keeps = [jnp.where(keep, 1.0, 0.0).astype(made.dtype) for keep in keeps]
+        pair = []
+        for weights, x in ((ds_all, q), (p_all, o)):
+            parts = [weights[span, own : own + 2 * BLK]]
+            for place, keep in enumerate(keeps):
+                block = weights[span, place * BLK : (place + 1) * BLK]
+                lower = block * keep
+                parts += [lower, block - lower]
+            pair.append(dot(jnp.concatenate(parts, axis=0), x, 1, 0))
+        terms.append(pair)
+    copies = []
     for span in range(spans):
-        at = BLK + span * rows
-        send_ref[span, 1] = dk_all[at : at + rows].astype(send_ref.dtype)
-        send_ref[span, 2] = dv_all[at : at + rows].astype(send_ref.dtype)
+        for kind in range(2):
+            part = lambda source, start, count: terms[source][kind][start : start + count]
+            edges = [
+                part(span - 1, 3 * BLK, BLK) if span > 0 else None,
+                part(span + 1, 2 * BLK, BLK) if span < spans - 1 else None,
+            ]
+            edges = [jnp.zeros((BLK, head_size), jnp.float32) if e is None else e for e in edges]
+            total = part(span, 0, 2 * BLK) + jnp.concatenate(edges, axis=0)
+            for slot, offset in enumerate(offsets):
+                total = total + part((span - offset) % spans, (4 + 2 * slot) * BLK, 2 * BLK)
+            made[span, 1 + kind] = total.astype(made.dtype)
+        copy = pltpu.make_async_copy(made.at[span], out_ref.at[span], sems.at[span])
+        copy.start()
+        copies.append(copy)
+    for copy in copies:
+        copy.wait()
 
 
 def grads(rand_head, chosen, held):
     spans, keys, rows = held[3].shape
-    padded_rows, head_size = held[1].shape
+    head_size = held[1].shape[1]
     keys_each = spans * keys * rows
+    shape = (spans, 3, rows, head_size)
     return pl.pallas_call(
         grad_kernel,
         in_specs=[pl.BlockSpec(memory_space=pltpu.SMEM)] + in_vmem(1 + len(held)),
-        out_specs=pl.BlockSpec(memory_space=pltpu.VMEM),
-        out_shape=jax.ShapeDtypeStruct((spans, 3, rows, head_size), jnp.bfloat16),
-        scratch_shapes=[pltpu.VMEM((padded_rows, head_size), jnp.float32)] * 2,
+        out_specs=pl.BlockSpec(memory_space=pltpu.HBM),
+        out_shape=jax.ShapeDtypeStruct(shape, jnp.bfloat16),
+        scratch_shapes=[
+            pltpu.VMEM(shape, jnp.bfloat16),
+            pltpu.SemaphoreType.DMA((spans,)),
+        ],
         compiler_params=pltpu.CompilerParams(vmem_limit_bytes=VMEM_BYTES),
         cost_estimate=pl.CostEstimate(
             flops=6 * keys_each * head_size,
@@ -526,57 +574,93 @@
     )(rand_head, chosen, *held)
 
 
-def unpack_kernel(x_ref, *out_refs):
-    heads, _, _, head_size = x_ref.shape
-    for head in range(heads):
-        columns = slice(head * head_size, (head + 1) * head_size)
-        for place, ref in enumerate(out_refs):
-            ref[0, :, columns] = x_ref[head, place]
-
-
-def unpack(x):
-    heads, count, rows, head_size = x.shape
-    shape = jax.ShapeDtypeStruct((1, rows, heads * head_size), x.dtype)
+def early_kernel(sides, *refs):
+    parts, out_ref = refs[:-1], refs[-1]
+    head_size = parts[0].shape[2]
+    head = lax.axis_index("ctx")
+    share = lax.axis_index("dp")
+    for side, ref in zip(sides, parts):
+        for place in range(ref.shape[0]):
+            bits = side[place // len(COLUMN)]
+            flip = COLUMN[place % len(COLUMN)]
+            columns = pl.ds(pl.multiple_of((head ^ flip) * head_size, head_size), head_size)
+            out_ref[share ^ bits, :, columns] = ref[place].astype(out_ref.dtype)
+
+
+def early_table(shares, head_count, sides, parts):
+    _, rows, head_size = parts[0].shape
+    shape = (shares, rows, head_count * head_size)
     return pl.pallas_call(
-        unpack_kernel,
-        grid=(1,),
-        in_specs=[pl.BlockSpec(x.shape, lambda i: (0, 0, 0, 0))],
-        out_specs=[pl.BlockSpec(shape.shape, lambda i: (0, 0, 0))] * count,
-        out_shape=[shape] * count,
+        functools.partial(early_kernel, sides),
+        in_specs=in_vmem(len(parts)),
+        out_specs=pl.BlockSpec(memory_space=pltpu.VMEM),
+        out_shape=jax.ShapeDtypeStruct(shape, jnp.float32),
         compiler_params=pltpu.CompilerParams(vmem_limit_bytes=VMEM_BYTES),
         cost_estimate=pl.CostEstimate(
-            flops=0, bytes_accessed=4 * count * rows * heads * head_size, transcendentals=0
+            flops=EARLY_FLOPS, bytes_accessed=2**21, transcendentals=0
         ),
-        name="unpack_heads",
-    )(x)
-
-
-def table_kernel(*refs):
-    parts, out_ref = refs[:-1], refs[-1]
-    _, count, _, head_size = parts[0].shape
-    head = lax.axis_index("ctx")
+        name="early_table",
+    )(*parts)
+
+
+def finish_kernel(sides, *refs):
+    count = len(sides)
+    parts, x_ref = refs[:count], refs[count]
+    grad_refs, table_ref = refs[count + 2 : count + 5], refs[count + 5]
+    x_held, grad_made, table_made, x_sem, grad_sems, table_sems = refs[count + 6 :]
+    heads, _, _, head_size = x_held.shape
+    load = pltpu.make_async_copy(x_ref, x_held, x_sem)
+    load.start()
+    me = lax.axis_index("ctx")
     share = lax.axis_index("dp")
-    for bits, ref in enumerate(parts):
-        for place, flip in enumerate(HEADS_ORDER):
-            columns = pl.ds(pl.multiple_of((head ^ flip) * head_size, head_size), head_size)
-            for block in range(count):
-                out_ref[(share ^ bits) * count + block, :, columns] = ref[place, block].astype(
-                    out_ref.dtype
-                )
-
-
-def whole_table(parts):
-    heads, blocks, rows, head_size = parts[0].shape
-    shape = (len(parts) * blocks, rows, heads * head_size)
+    stores = []
+    for side, ref in zip(sides, parts):
+        for place in range(ref.shape[0]):
+            at = len(stores)
+            bits = side[place // len(COLUMN)]
+            flip = COLUMN[place % len(COLUMN)] ^ 1
+            columns = pl.ds(pl.multiple_of((me ^ flip) * head_size, head_size), head_size)
+            table_made[at] = ref[place].astype(table_made.dtype)
+            store = pltpu.make_async_copy(
+                table_made.at[at], table_ref.at[share ^ bits, :, columns], table_sems.at[at]
+            )
+            store.start()
+            stores.append(store)
+    load.wait()
+    for place, ref in enumerate(grad_refs):
+        for head in range(heads):
+            columns = slice(head * head_size, (head + 1) * head_size)
+            grad_made[place, :, columns] = x_held[head, place]
+        store = pltpu.make_async_copy(grad_made.at[place], ref.at[0], grad_sems.at[place])
+        store.start()
+        stores.append(store)
+    for store in stores:
+        store.wait()
+
+
+def finish(x, table, sides, parts):
+    heads, kinds, rows, head_size = x.shape
+    blocks = sum(part.shape[0] for part in parts)
+    in_hbm = pl.BlockSpec(memory_space=pltpu.HBM)
+    grad = jax.ShapeDtypeStruct((1, rows, heads * head_size), x.dtype)
     return pl.pallas_call(
-        table_kernel,
-        grid=(1,),
-        in_specs=[pl.BlockSpec(parts[0].shape, lambda i: (0, 0, 0, 0))] * len(parts),
-        out_specs=pl.BlockSpec(shape, lambda i: (0, 0, 0)),
-        out_shape=jax.ShapeDtypeStruct(shape, jnp.float32),
-        compiler_params=pltpu.CompilerParams(vmem_limit_bytes=VMEM_BYTES),
-        name="whole_table",
-    )(*parts)
+        functools.partial(finish_kernel, sides),
+        in_specs=in_vmem(len(parts)) + [in_hbm] * 2,
+        out_specs=[in_hbm] * (kinds + 1),
+        out_shape=[grad] * kinds + [jax.ShapeDtypeStruct(table.shape, table.dtype)],
+        scratch_shapes=[
+            pltpu.VMEM(x.shape, x.dtype),
+            pltpu.VMEM((kinds, rows, heads * head_size), x.dtype),
+            pltpu.VMEM((blocks, rows, head_size), table.dtype),
+            pltpu.SemaphoreType.DMA,
+            pltpu.SemaphoreType.DMA((kinds,)),
+            pltpu.SemaphoreType.DMA((blocks,)),
+        ],
+        input_output_aliases={len(parts) + 1: kinds},
+        compiler_params=pltpu.CompilerParams(vmem_limit_bytes=FINISH_VMEM_BYTES),
+        cost_estimate=pl.CostEstimate(flops=0, bytes_accessed=2**21, transcendentals=0),
+        name="finish",
+    )(*parts, x, table)
 
 
 def flipped(array, axis, bits):
@@ -604,13 +688,16 @@
     *terms, sent = lax.optimization_barrier((*terms, sent))
     back = lax.all_to_all(sent, "ctx", 0, 0)
     share = sum(term.astype(jnp.float32) for term in terms).astype(jnp.bfloat16)
-    column = jnp.stack([flipped(share, "ctx", flip) for flip in HEADS_ORDER[:4]])
-    quarter = jnp.concatenate([column, flipped(column, "ctx", 1)])
-    across = flipped(quarter, "dp", 2)
-    beside = flipped(quarter, "dp", 1)
-    corner = flipped(across, "dp", 1)
-    d_table = whole_table([quarter, beside, across, corner])
-    d_query, d_key, d_value = unpack(back)
+    share = share.reshape(1, -1, head_size)
+    column = jnp.concatenate([flipped(share, "ctx", flip) for flip in COLUMN])
+    even = jnp.concatenate([column, flipped(column, "dp", 2)])
+    odd = flipped(even, "ctx", 1)
+    beside_even = flipped(even, "dp", 1)
+    beside_odd = flipped(odd, "dp", 1)
+    d_table = early_table(shares, head_count, ((0, 2), (1, 3)), [even, beside_even])
+    d_query, d_key, d_value, d_table = finish(
+        back, d_table, ((0, 2), (1, 3)), [odd, beside_odd]
+    )
     return (d_query, d_key, d_value, d_table.reshape((2,) + glob_keys.shape))
 
 

time: 70.5 us -> 67.9 us (0.963)
  Pallas kernels: 12.5 us -> 11.1 us
    ppermute x17, waiting for transfers between devices: 19.8 us -> 18 us  [flipped(): lax.ppermute(array, axis, [(i, i ^ bits) for i in range(lax.axis_size(axi...]
    pallas_call x1, Pallas kernels: 4.04 us -> 2.49 us  [scores(): pl.pallas_call(functools.partial(score_kernel, spans, shares), in_specs=[...]
    all_to_all x1, waiting for transfers between devices: 0.01 us -> 1.47 us  [on_heads(): back = lax.all_to_all(sent, 'ctx', 0, 0)]
    unnamed x11 -> x12, local copies, waits for them, and re-layouts: 3.03 us -> 3.03 us
  transfers between devices with their start and end apart: 18 -> 18, of which waited for: 7 -> 8; matrix products, arithmetic and copies ran while one was open for 1% -> 1% of each run, Pallas kernels for 7% -> 7%
where the time goes in v4:
time: 67.9 us; the launch traced here: 67.5 us
  starting transfers between devices  32.3 us (48%)
  waiting for transfers between devices  19.4 us (29%)
  Pallas kernels  11.1 us (16%)
  local copies, waits for them, and re-layouts  3.22 us (5%)
  between operations  0.79 us (1%)
  other arithmetic  0.78 us (1%)
    ppermute x17, starting transfers between devices, flipped(): lax.ppermute(array, axis, [(i, i ^ bits) for i in range(lax.axis_size(axi...  28.1 us
    ppermute x17, waiting for transfers between devices, flipped(): lax.ppermute(array, axis, [(i, i ^ bits) for i in range(lax.axis_size(axi...  18 us
    all_to_all x1, starting transfers between devices, on_heads(): back = lax.all_to_all(sent, 'ctx', 0, 0)  4.2 us
    unnamed x12, local copies, waits for them, and re-layouts  3.03 us
    pallas_call x1, Pallas kernels, grads(): pl.pallas_call(grad_kernel, in_specs=[pl.BlockSpec(memory_space=pltpu.SME...  2.6 us
    pallas_call x1, Pallas kernels, scores(): pl.pallas_call(functools.partial(score_kernel, spans, shares), in_specs=[...  2.49 us
    pallas_call x1, Pallas kernels, pack(): pl.pallas_call(functools.partial(pack_kernel, head_count), in_specs=[in_h...  2.29 us
    all_to_all x1, waiting for transfers between devices, on_heads(): back = lax.all_to_all(sent, 'ctx', 0, 0)  1.47 us
  transfers between devices with their start and end apart: 18, of which 8 were waited for; matrix products, arithmetic and copies ran while one was open for 1% of the time, Pallas kernels for 7%

profile of v4, /device:TPU:0, one launch (start us, length us, event | category | flops | bytes accessed | tf_op | source)
XLA Modules:
  0.0 67.5 jit_solution(10439564233133477538)
XLA Ops:
  0.6 2.3 %pack_heads.1 = (bf16[4,128,128]{2,1,0:T(8,128)(2,1)}, bf16[4,128,128]{2,1,0:T(8,128)(2,1)}, bf16[4,128,128]{2,1,0:T(8,128)(2,1)}, bf16[4,128,128]{2,1,0:T(8,128...) custom-call(bf16[1,128,1024]{2,1,0:T(8,128)(2,1)} %refs_0_.1, ...), custom_call_target="tpu_custom_call" | custom-call | bytes 2097152 | tf_op jit(solution)/shard_map/pack_heads/pallas_call | solution.py:280
  2.9 4.1 %collective-permute-start = (bf16[4,128,128]{2,1,0:T(8,128)(2,1)}, bf16[4,128,128]{2,1,0:T(8,128)(2,1)S(1)}, u32[]{:S(2)}, u32[]{:S(2)}) collective-permute-start(bf16[4,128,128]{2,1,0:T(8,128)(2,1)} %get-tuple-element.34), channel_id=1, source_target_pairs={{0,16},{4,20},{8,24},{12,28},{16,0},{20,4},{24,8},{28,12},{1,17},{... | collective-permute-start | bytes 393224 | tf_op jit(solution)/shard_map/ppermute | solution.py:669
  7.0 1.6 %collective-permute-start.1 = (bf16[4,128,128]{2,1,0:T(8,128)(2,1)}, bf16[4,128,128]{2,1,0:T(8,128)(2,1)S(1)}, u32[]{:S(2)}, u32[]{:S(2)}) collective-permute-start(bf16[4,128,128]{2,1,0:T(8,128)(2,1)} %get-tuple-element.35), channel_id=1, source_target_pairs={{0,8},{4,12},{8,0},{12,4},{16,24},{20,28},{24,16},{28,20},{1,9},{5... | collective-permute-start | bytes 393224 | tf_op jit(solution)/shard_map/ppermute | solution.py:669
  8.6 1.3 %collective-permute-start.2 = (bf16[4,128,128]{2,1,0:T(8,128)(2,1)}, bf16[4,128,128]{2,1,0:T(8,128)(2,1)S(1)}, u32[]{:S(2)}, u32[]{:S(2)}) collective-permute-start(bf16[4,128,128]{2,1,0:T(8,128)(2,1)} %get-tuple-element.36), channel_id=1, source_target_pairs={{0,20},{4,16},{8,28},{12,24},{16,4},{20,0},{24,12},{28,8},{1,21},{... | collective-permute-start | bytes 393224 | tf_op jit(solution)/shard_map/ppermute | solution.py:669
  10.0 3.9 %collective-permute-start.4 = (bf16[4,128,128]{2,1,0:T(8,128)(2,1)}, bf16[4,128,128]{2,1,0:T(8,128)(2,1)S(1)}, u32[]{:S(2)}, u32[]{:S(2)}) collective-permute-start(bf16[4,128,128]{2,1,0:T(8,128)(2,1)} %get-tuple-element.38), channel_id=1, source_target_pairs={{0,24},{4,28},{8,16},{12,20},{16,8},{20,12},{24,0},{28,4},{1,25},{... | collective-permute-start | bytes 393224 | tf_op jit(solution)/shard_map/ppermute | solution.py:669
  13.9 1.1 %collective-permute-done.refs_1_ = bf16[4,128,128]{2,1,0:T(8,128)(2,1)S(1)} collective-permute-done((bf16[4,128,128]{2,1,0:T(8,128)(2,1)}, bf16[4,128,128]{2,1,0:T(8,128)(2,1)S(1)}, u32[]{:S(2)}, u32[]{:S(2)}) %collective-permute-start) | collective-permute-done | bytes 131104 | tf_op jit(solution)/shard_map/ppermute | solution.py:669
  15.0 4.2 %collective-permute-start.5 = (bf16[4,128,128]{2,1,0:T(8,128)(2,1)}, bf16[4,128,128]{2,1,0:T(8,128)(2,1)S(1)}, u32[]{:S(2)}, u32[]{:S(2)}) collective-permute-start(bf16[4,128,128]{2,1,0:T(8,128)(2,1)} %get-tuple-element.39), channel_id=1, source_target_pairs={{0,28},{4,24},{8,20},{12,16},{16,12},{20,8},{24,4},{28,0},{1,29},{... | collective-permute-start | bytes 393224 | tf_op jit(solution)/shard_map/ppermute | solution.py:669
  20.7 1.0 %copy-done.1 = bf16[4,64,1024]{2,1,0:T(8,128)(2,1)S(1)} copy-done((bf16[4,64,1024]{2,1,0:T(8,128)(2,1)S(1)}, bf16[4,64,1024]{2,1,0:T(8,128)(2,1)}, u32[]{:S(2)}) %copy-start.1) | copy-done | bytes 524312
  21.8 1.0 %copy-done.2 = bf16[4,64,1024]{2,1,0:T(8,128)(2,1)S(1)} copy-done((bf16[4,64,1024]{2,1,0:T(8,128)(2,1)S(1)}, bf16[4,64,1024]{2,1,0:T(8,128)(2,1)}, u32[]{:S(2)}) %copy-start.2) | copy-done | bytes 524312
  22.8 0.9 %copy-done.3 = bf16[4,128,128]{2,1,0:T(8,128)(2,1)S(1)} copy-done((bf16[4,128,128]{2,1,0:T(8,128)(2,1)S(1)}, bf16[4,128,128]{2,1,0:T(8,128)(2,1)}, u32[]{:S(2)}) %copy-start.3) | copy-done | bytes 131096
  24.5 2.5 %collective-permute-done.5.refs_6_ = bf16[4,128,128]{2,1,0:T(8,128)(2,1)S(1)} collective-permute-done((bf16[4,128,128]{2,1,0:T(8,128)(2,1)}, bf16[4,128,128]{2,1,0:T(8,128)(2,1)S(1)}, u32[]{:S(2)}, u32[]{:S(2)}) %collective-permute-start.5) | collective-permute-done | bytes 131104 | tf_op jit(solution)/shard_map/ppermute | solution.py:669
  27.4 2.5 %scores.1 = (bf16[1024,128]{1,0:T(8,128)(2,1)S(1)}, bf16[1152,128]{1,0:T(8,128)(2,1)S(1)}, bf16[1024,128]{1,0:T(8,128)(2,1)S(1)}, bf16[8,512,128]{2,1,0:T(8,128)...) custom-call(s32[4]{0:T(128)S(1)} %pad_add_fusion.place_ref, ...), custom_call_target="tpu_custom_call" | custom-call | flops 268435456 | bytes 1048576 | tf_op jit(solution)/shard_map/scores/pallas_call | solution.py:473
  30.0 1.6 %collective-permute-start.8 = (bf16[2,64,128]{2,1,0:T(8,128)(2,1)S(1)}, bf16[2,64,128]{2,1,0:T(8,128)(2,1)S(1)}, u32[]{:S(2)}, u32[]{:S(2)}) collective-permute-start(bf16[2,64,128]{2,1,0:T(8,128)(2,1)S(1)} %get-tuple-element.44), channel_id=1, source_target_pairs={{0,2},{1,3},{2,0},{3,1},{4,6},{5,7},{6,4},{7,5},{8,10},{9,11},{10,... | collective-permute-start | bytes 98312 | tf_op jit(solution)/shard_map/ppermute | solution.py:669
  31.9 2.6 %grads.1 = bf16[8,3,128,128]{3,2,1,0:T(8,128)(2,1)} custom-call(s32[48]{0:T(128)S(1)} %min.12.rand_ref, bf16[4,64,128]{2,1,0:T(8,128)(2,1)S(1)} %get-tuple-element.41.refs_8_.g_ref, bf16[1024,128]{1,0:T(8,128)(2,1)S(1)} %get-tuple-element.46.q_all, bf16[1152,128]{1,0:T(8,128)(2,1)S(1)} %get-tuple-element.47.k_all, ...), custom_call_target="tpu_custom_call" | custom-call | flops 402653184 | bytes 1048576 | tf_op jit(solution)/shard_map/grads/pallas_call | solution.py:558
  35.0 2.0 %collective-permute-start.12 = (bf16[1,128,128]{2,1,0:T(8,128)(2,1)S(1)}, bf16[1,128,128]{2,1,0:T(8,128)(2,1)S(1)}, u32[]{:S(2)}, u32[]{:S(2)}) collective-permute-start(bf16[1,128,128]{2,1,0:T(8,128)(2,1)S(1)} %bitcast.8), channel_id=1, source_target_pairs={{0,24},{4,28},{8,16},{12,20},{16,8},{20,12},{24,0},{28,4},{1,25},{... | collective-permute-start | bytes 98312 | tf_op jit(solution)/shard_map/ppermute | solution.py:669
  37.0 4.7 %collective-permute-start.11 = (bf16[1,128,128]{2,1,0:T(8,128)(2,1)S(1)}, bf16[1,128,128]{2,1,0:T(8,128)(2,1)S(1)}, u32[]{:S(2)}, u32[]{:S(2)}) collective-permute-start(bf16[1,128,128]{2,1,0:T(8,128)(2,1)S(1)} %bitcast.9), channel_id=1, source_target_pairs={{0,16},{4,20},{8,24},{12,28},{16,0},{20,4},{24,8},{28,12},{1,17},{... | collective-permute-start | bytes 98312 | tf_op jit(solution)/shard_map/ppermute | solution.py:669
  42.2 4.2 %all-to-all-start = ((bf16[8,3,128,128]{3,2,1,0:T(8,128)(2,1)}), bf16[8,3,128,128]{3,2,1,0:T(8,128)(2,1)S(1)}, u32[]{:S(2)}, u32[]{:S(2)}) async-start(bf16[8,3,128,128]{3,2,1,0:T(8,128)(2,1)} %grads.1), calls=%async_computation | async-start | bytes 1572864 | tf_op jit(solution)/shard_map/all_to_all | solution.py:689
  46.4 1.2 %collective-permute-start.13 = (bf16[4,128,128]{2,1,0:T(8,128)(2,1)S(1)}, bf16[4,128,128]{2,1,0:T(8,128)(2,1)S(1)}, u32[]{:S(2)}, u32[]{:S(2)}) collective-permute-start(bf16[4,128,128]{2,1,0:T(8,128)(2,1)S(1)} %pad_maximum_fusion), channel_id=1, source_target_pairs={{0,2},{1,3},{2,0},{3,1},{4,6},{5,7},{6,4},{7,5},{8,10},{9,11},{10,... | collective-permute-start | bytes 393224 | tf_op jit(solution)/shard_map/ppermute | solution.py:669
  47.6 3.9 %collective-permute-done.13 = bf16[4,128,128]{2,1,0:T(8,128)(2,1)S(1)} collective-permute-done((bf16[4,128,128]{2,1,0:T(8,128)(2,1)S(1)}, bf16[4,128,128]{2,1,0:T(8,128)(2,1)S(1)}, u32[]{:S(2)}, u32[]{:S(2)}) %collective-permute-start.13) | collective-permute-done | bytes 131104 | tf_op jit(solution)/shard_map/ppermute | solution.py:669
  51.5 2.1 %collective-permute-start.14 = (bf16[8,128,128]{2,1,0:T(8,128)(2,1)S(1)}, bf16[8,128,128]{2,1,0:T(8,128)(2,1)S(1)}, u32[]{:S(2)}, u32[]{:S(2)}) collective-permute-start(bf16[8,128,128]{2,1,0:T(8,128)(2,1)S(1)} %constant_dynamic-update-slice_fusion.refs_0_), channel_id=1, source_target_pairs={{0,4},{4,0},{8,12},{12,8},{16,20},{20,16},{24,28},{28,24},{1,5},{5... | collective-permute-start | bytes 786440 | tf_op jit(solution)/shard_map/ppermute | solution.py:669
  53.6 9.5 %collective-permute-done.14.refs_0_ = bf16[8,128,128]{2,1,0:T(8,128)(2,1)S(1)} collective-permute-done((bf16[8,128,128]{2,1,0:T(8,128)(2,1)S(1)}, bf16[8,128,128]{2,1,0:T(8,128)(2,1)S(1)}, u32[]{:S(2)}, u32[]{:S(2)}) %collective-permute-start.14) | collective-permute-done | bytes 262176 | tf_op jit(solution)/shard_map/ppermute | solution.py:669
  63.1 1.4 %early_table.1.refs_3_ = f32[4,128,1024]{2,1,0:T(8,128)} custom-call(bf16[8,128,128]{2,1,0:T(8,128)(2,1)S(1)} %constant_dynamic-update-slice_fusion.refs_0_, bf16[8,128,128]{2,1,0:T(8,128)(2,1)S(1)} %collective-permute-done.16.refs_1_), custom_call_target="tpu_custom_call" | custom-call | flops 5000000000 | bytes 2097152 | tf_op jit(solution)/shard_map/early_table/pallas_call | solution.py:593
  64.6 1.5 %all-to-all-done.refs_2_ = bf16[8,3,128,128]{3,2,1,0:T(8,128)(2,1)S(1)} async-done(((bf16[8,3,128,128]{3,2,1,0:T(8,128)(2,1)}), bf16[8,3,128,128]{3,2,1,0:T(8,128)(2,1)S(1)}, u32[]{:S(2)}, u32[]{:S(2)}) %all-to-all-start) | async-done | bytes 786464 | tf_op jit(solution)/shard_map/all_to_all | solution.py:689
  66.1 1.5 %finish.1 = (bf16[1,128,1024]{2,1,0:T(8,128)(2,1)}, bf16[1,128,1024]{2,1,0:T(8,128)(2,1)}, bf16[1,128,1024]{2,1,0:T(8,128)(2,1)}, f32[4,128,1024]{2,1,0:T(8,128)}) custom-call(bf16[8,128,128]{2,1,0:T(8,128)(2,1)S(1)} %collective-permute-done.14.refs_0_, bf16[8,128,128]{2,1,0:T(8,128)(2,1)S(1)} %collective-permute-done.15.refs_1_, ...), custom_call_target="tpu_custom_call", output_to_operand_aliasing={{3}: (3, {})} | custom-call | bytes 2097152 | tf_op jit(solution)/shard_map/finish/pallas_call | solution.py:646
  (38 shorter events, 4.3 us)
Async XLA Ops:
  0.6 13.3 %copy-start = (s32[8,16,3]{1,0,2:T(8,128)S(1)}, s32[8,16,3]{1,0,2:T(8,128)}, u32[]{:S(2)}) copy-start(s32[8,16,3]{1,0,2:T(8,128)} %param.15) | copy-start | bytes 4612
  2.9 12.1 %collective-permute-start = (bf16[4,128,128]{2,1,0:T(8,128)(2,1)}, bf16[4,128,128]{2,1,0:T(8,128)(2,1)S(1)}, u32[]{:S(2)}, u32[]{:S(2)}) collective-permute-start(bf16[4,128,128]{2,1,0:T(8,128)(2,1)} %get-tuple-element.34), channel_id=1, source_target_pairs={{0,16},{4,20},{8,24},{12,28},{16,0},{20,4},{24,8},{28,12},{1,17},{... | collective-permute-start | bytes 393224 | tf_op jit(solution)/shard_map/ppermute | solution.py:669
  7.0 12.2 %collective-permute-start.1 = (bf16[4,128,128]{2,1,0:T(8,128)(2,1)}, bf16[4,128,128]{2,1,0:T(8,128)(2,1)S(1)}, u32[]{:S(2)}, u32[]{:S(2)}) collective-permute-start(bf16[4,128,128]{2,1,0:T(8,128)(2,1)} %get-tuple-element.35), channel_id=1, source_target_pairs={{0,8},{4,12},{8,0},{12,4},{16,24},{20,28},{24,16},{28,20},{1,9},{5... | collective-permute-start | bytes 393224 | tf_op jit(solution)/shard_map/ppermute | solution.py:669
  8.6 15.9 %collective-permute-start.2 = (bf16[4,128,128]{2,1,0:T(8,128)(2,1)}, bf16[4,128,128]{2,1,0:T(8,128)(2,1)S(1)}, u32[]{:S(2)}, u32[]{:S(2)}) collective-permute-start(bf16[4,128,128]{2,1,0:T(8,128)(2,1)} %get-tuple-element.36), channel_id=1, source_target_pairs={{0,20},{4,16},{8,28},{12,24},{16,4},{20,0},{24,12},{28,8},{1,21},{... | collective-permute-start | bytes 393224 | tf_op jit(solution)/shard_map/ppermute | solution.py:669
  9.9 14.6 %collective-permute-start.3 = (bf16[4,128,128]{2,1,0:T(8,128)(2,1)}, bf16[4,128,128]{2,1,0:T(8,128)(2,1)S(1)}, u32[]{:S(2)}, u32[]{:S(2)}) collective-permute-start(bf16[4,128,128]{2,1,0:T(8,128)(2,1)} %get-tuple-element.37), channel_id=1, source_target_pairs={{0,12},{4,8},{8,4},{12,0},{16,28},{20,24},{24,20},{28,16},{1,13},{... | collective-permute-start | bytes 393224 | tf_op jit(solution)/shard_map/ppermute | solution.py:669
  10.0 14.5 %collective-permute-start.4 = (bf16[4,128,128]{2,1,0:T(8,128)(2,1)}, bf16[4,128,128]{2,1,0:T(8,128)(2,1)S(1)}, u32[]{:S(2)}, u32[]{:S(2)}) collective-permute-start(bf16[4,128,128]{2,1,0:T(8,128)(2,1)} %get-tuple-element.38), channel_id=1, source_target_pairs={{0,24},{4,28},{8,16},{12,20},{16,8},{20,12},{24,0},{28,4},{1,25},{... | collective-permute-start | bytes 393224 | tf_op jit(solution)/shard_map/ppermute | solution.py:669
  15.0 12.0 %collective-permute-start.5 = (bf16[4,128,128]{2,1,0:T(8,128)(2,1)}, bf16[4,128,128]{2,1,0:T(8,128)(2,1)S(1)}, u32[]{:S(2)}, u32[]{:S(2)}) collective-permute-start(bf16[4,128,128]{2,1,0:T(8,128)(2,1)} %get-tuple-element.39), channel_id=1, source_target_pairs={{0,28},{4,24},{8,20},{12,16},{16,12},{20,8},{24,4},{28,0},{1,29},{... | collective-permute-start | bytes 393224 | tf_op jit(solution)/shard_map/ppermute | solution.py:669
  19.3 8.2 %collective-permute-start.6 = (bf16[4,128,128]{2,1,0:T(8,128)(2,1)}, bf16[4,128,128]{2,1,0:T(8,128)(2,1)S(1)}, u32[]{:S(2)}, u32[]{:S(2)}) collective-permute-start(bf16[4,128,128]{2,1,0:T(8,128)(2,1)} %get-tuple-element.40), channel_id=1, source_target_pairs={{0,4},{4,0},{8,12},{12,8},{16,20},{20,16},{24,28},{28,24},{1,5},{5... | collective-permute-start | bytes 393224 | tf_op jit(solution)/shard_map/ppermute | solution.py:669
  20.7 1.0 %copy-start.1 = (bf16[4,64,1024]{2,1,0:T(8,128)(2,1)S(1)}, bf16[4,64,1024]{2,1,0:T(8,128)(2,1)}, u32[]{:S(2)}) copy-start(bf16[4,64,1024]{2,1,0:T(8,128)(2,1)} %gk_ref.1) | copy-start | bytes 1572868
  21.8 1.0 %copy-start.2 = (bf16[4,64,1024]{2,1,0:T(8,128)(2,1)S(1)}, bf16[4,64,1024]{2,1,0:T(8,128)(2,1)}, u32[]{:S(2)}) copy-start(bf16[4,64,1024]{2,1,0:T(8,128)(2,1)} %gv_ref.1) | copy-start | bytes 1572868
  22.8 0.9 %copy-start.3 = (bf16[4,128,128]{2,1,0:T(8,128)(2,1)S(1)}, bf16[4,128,128]{2,1,0:T(8,128)(2,1)}, u32[]{:S(2)}) copy-start(bf16[4,128,128]{2,1,0:T(8,128)(2,1)} %get-tuple-element.32.own_ref) | copy-start | bytes 393220
  29.9 4.5 %collective-permute-start.7 = (bf16[2,64,128]{2,1,0:T(8,128)(2,1)S(1)}, bf16[2,64,128]{2,1,0:T(8,128)(2,1)S(1)}, u32[]{:S(2)}, u32[]{:S(2)}) collective-permute-start(bf16[2,64,128]{2,1,0:T(8,128)(2,1)S(1)} %get-tuple-element.43), channel_id=1, source_target_pairs={{0,1},{1,0},{2,3},{3,2},{4,5},{5,4},{6,7},{7,6},{8,9},{9,8},{10,11... | collective-permute-start | bytes 98312 | tf_op jit(solution)/shard_map/ppermute | solution.py:669
  30.0 4.5 %collective-permute-start.8 = (bf16[2,64,128]{2,1,0:T(8,128)(2,1)S(1)}, bf16[2,64,128]{2,1,0:T(8,128)(2,1)S(1)}, u32[]{:S(2)}, u32[]{:S(2)}) collective-permute-start(bf16[2,64,128]{2,1,0:T(8,128)(2,1)S(1)} %get-tuple-element.44), channel_id=1, source_target_pairs={{0,2},{1,3},{2,0},{3,1},{4,6},{5,7},{6,4},{7,5},{8,10},{9,11},{10,... | collective-permute-start | bytes 98312 | tf_op jit(solution)/shard_map/ppermute | solution.py:669
  31.6 3.3 %collective-permute-start.9 = (bf16[2,64,128]{2,1,0:T(8,128)(2,1)S(1)}, bf16[2,64,128]{2,1,0:T(8,128)(2,1)S(1)}, u32[]{:S(2)}, u32[]{:S(2)}) collective-permute-start(bf16[2,64,128]{2,1,0:T(8,128)(2,1)S(1)} %get-tuple-element.45), channel_id=1, source_target_pairs={{0,3},{1,2},{2,1},{3,0},{4,7},{5,6},{6,5},{7,4},{8,11},{9,10},{10,... | collective-permute-start | bytes 98312 | tf_op jit(solution)/shard_map/ppermute | solution.py:669
  35.0 11.4 %collective-permute-start.12 = (bf16[1,128,128]{2,1,0:T(8,128)(2,1)S(1)}, bf16[1,128,128]{2,1,0:T(8,128)(2,1)S(1)}, u32[]{:S(2)}, u32[]{:S(2)}) collective-permute-start(bf16[1,128,128]{2,1,0:T(8,128)(2,1)S(1)} %bitcast.8), channel_id=1, source_target_pairs={{0,24},{4,28},{8,16},{12,20},{16,8},{20,12},{24,0},{28,4},{1,25},{... | collective-permute-start | bytes 98312 | tf_op jit(solution)/shard_map/ppermute | solution.py:669
  37.0 9.4 %collective-permute-start.11 = (bf16[1,128,128]{2,1,0:T(8,128)(2,1)S(1)}, bf16[1,128,128]{2,1,0:T(8,128)(2,1)S(1)}, u32[]{:S(2)}, u32[]{:S(2)}) collective-permute-start(bf16[1,128,128]{2,1,0:T(8,128)(2,1)S(1)} %bitcast.9), channel_id=1, source_target_pairs={{0,16},{4,20},{8,24},{12,28},{16,0},{20,4},{24,8},{28,12},{1,17},{... | collective-permute-start | bytes 98312 | tf_op jit(solution)/shard_map/ppermute | solution.py:669
  41.7 4.7 %collective-permute-start.10 = (bf16[1,128,128]{2,1,0:T(8,128)(2,1)S(1)}, bf16[1,128,128]{2,1,0:T(8,128)(2,1)S(1)}, u32[]{:S(2)}, u32[]{:S(2)}) collective-permute-start(bf16[1,128,128]{2,1,0:T(8,128)(2,1)S(1)} %bitcast.10), channel_id=1, source_target_pairs={{0,8},{4,12},{8,0},{12,4},{16,24},{20,28},{24,16},{28,20},{1,9},{5... | collective-permute-start | bytes 98312 | tf_op jit(solution)/shard_map/ppermute | solution.py:669
  42.2 23.9 %all-to-all-start = ((bf16[8,3,128,128]{3,2,1,0:T(8,128)(2,1)}), bf16[8,3,128,128]{3,2,1,0:T(8,128)(2,1)S(1)}, u32[]{:S(2)}, u32[]{:S(2)}) async-start(bf16[8,3,128,128]{3,2,1,0:T(8,128)(2,1)} %grads.1), calls=%async_computation | async-start | bytes 1572864 | tf_op jit(solution)/shard_map/all_to_all | solution.py:689
  46.4 5.0 %collective-permute-start.13 = (bf16[4,128,128]{2,1,0:T(8,128)(2,1)S(1)}, bf16[4,128,128]{2,1,0:T(8,128)(2,1)S(1)}, u32[]{:S(2)}, u32[]{:S(2)}) collective-permute-start(bf16[4,128,128]{2,1,0:T(8,128)(2,1)S(1)} %pad_maximum_fusion), channel_id=1, source_target_pairs={{0,2},{1,3},{2,0},{3,1},{4,6},{5,7},{6,4},{7,5},{8,10},{9,11},{10,... | collective-permute-start | bytes 393224 | tf_op jit(solution)/shard_map/ppermute | solution.py:669
  51.5 11.6 %collective-permute-start.14 = (bf16[8,128,128]{2,1,0:T(8,128)(2,1)S(1)}, bf16[8,128,128]{2,1,0:T(8,128)(2,1)S(1)}, u32[]{:S(2)}, u32[]{:S(2)}) collective-permute-start(bf16[8,128,128]{2,1,0:T(8,128)(2,1)S(1)} %constant_dynamic-update-slice_fusion.refs_0_), channel_id=1, source_target_pairs={{0,4},{4,0},{8,12},{12,8},{16,20},{20,16},{24,28},{28,24},{1,5},{5... | collective-permute-start | bytes 786440 | tf_op jit(solution)/shard_map/ppermute | solution.py:669
  53.6 9.5 %collective-permute-start.16 = (bf16[8,128,128]{2,1,0:T(8,128)(2,1)S(1)}, bf16[8,128,128]{2,1,0:T(8,128)(2,1)S(1)}, u32[]{:S(2)}, u32[]{:S(2)}) collective-permute-start(bf16[8,128,128]{2,1,0:T(8,128)(2,1)S(1)} %constant_dynamic-update-slice_fusion.refs_0_), channel_id=1, source_target_pairs={{0,1},{1,0},{2,3},{3,2},{4,5},{5,4},{6,7},{7,6},{8,9},{9,8},{10,11... | collective-permute-start | bytes 786440 | tf_op jit(solution)/shard_map/ppermute | solution.py:669
  63.1 1.5 %collective-permute-start.15 = (bf16[8,128,128]{2,1,0:T(8,128)(2,1)S(1)}, bf16[8,128,128]{2,1,0:T(8,128)(2,1)S(1)}, u32[]{:S(2)}, u32[]{:S(2)}) collective-permute-start(bf16[8,128,128]{2,1,0:T(8,128)(2,1)S(1)} %collective-permute-done.14.refs_0_), channel_id=1, source_target_pairs={{0,1},{1,0},{2,3},{3,2},{4,5},{5,4},{6,7},{7,6},{8,9},{9,8},{10,11... | collective-permute-start | bytes 786440 | tf_op jit(solution)/shard_map/ppermute | solution.py:669

commit v5 on v4

--- a/solution.py
+++ b/solution.py
@@ -234,6 +234,7 @@
 LARGE_VMEM_BYTES = 60 * 1024 * 1024
 FINISH_VMEM_BYTES = 24 * 1024 * 1024
 MASKED = -1e30
+PACK_FLOPS = 2 * 10**9
 EARLY_FLOPS = 5 * 10**9
 GROUP = 8
 ORDER = (0, 4, 2, 5, 3, 6, 7, 1)
@@ -249,9 +250,27 @@
     return [pl.BlockSpec(memory_space=pltpu.VMEM)] * count
 
 
+def first_kernel(q_ref, k_ref, v_ref, o_ref, out_ref, held, sems, out_sem):
+    head_size = out_ref.shape[2]
+    at = pl.multiple_of((lax.axis_index("ctx") ^ ORDER[1]) * head_size, head_size)
+    copies = [
+        pltpu.make_async_copy(
+            ref.at[0, :, pl.ds(at, head_size)], held.at[place], sems.at[place]
+        )
+        for place, ref in enumerate((q_ref, k_ref, v_ref, o_ref))
+    ]
+    for copy in copies:
+        copy.start()
+    for copy in copies:
+        copy.wait()
+    store = pltpu.make_async_copy(held, out_ref, out_sem)
+    store.start()
+    store.wait()
+
+
 def pack_kernel(count, *refs):
-    ins, outs = refs[:4], refs[4 : 4 + count]
-    held, made, in_sems, out_sems = refs[4 + count :]
+    ins, outs = refs[:4], refs[5 : 5 + count]
+    held, made, in_sems, out_sems = refs[5 + count :]
     head_size = made.shape[3]
     me = lax.axis_index("ctx")
     loads = [
@@ -263,10 +282,10 @@
     for load in loads:
         load.wait()
     stores = []
-    for flip in ORDER:
+    for place, flip in enumerate(ORDER[2:] + ORDER[:1]):
         at = pl.multiple_of((me ^ flip) * head_size, head_size)
-        made[flip] = held[:, :, pl.ds(at, head_size)]
-        store = pltpu.make_async_copy(made.at[flip], outs[flip], out_sems.at[flip])
+        made[place] = held[:, :, pl.ds(at, head_size)]
+        store = pltpu.make_async_copy(made.at[place], outs[place], out_sems.at[place])
         store.start()
         stores.append(store)
     for store in stores:
@@ -275,23 +294,42 @@
 
 def pack(query, key, value, dout, head_count):
     _, rows, width = query.shape
+    arrays = (query, key, value, dout)
     chunk = (4, rows, width // head_count)
+    shape = jax.ShapeDtypeStruct(chunk, query.dtype)
     in_hbm = pl.BlockSpec(memory_space=pltpu.HBM)
-    return pl.pallas_call(
-        functools.partial(pack_kernel, head_count),
+    first = pl.pallas_call(
+        first_kernel,
         in_specs=[in_hbm] * 4,
-        out_specs=[in_hbm] * head_count,
-        out_shape=[jax.ShapeDtypeStruct(chunk, query.dtype)] * head_count,
+        out_specs=in_hbm,
+        out_shape=shape,
+        scratch_shapes=[
+            pltpu.VMEM(chunk, query.dtype),
+            pltpu.SemaphoreType.DMA((4,)),
+            pltpu.SemaphoreType.DMA,
+        ],
+        compiler_params=pltpu.CompilerParams(vmem_limit_bytes=LARGE_VMEM_BYTES),
+        cost_estimate=pl.CostEstimate(flops=0, bytes_accessed=2 * rows * width, transcendentals=0),
+        name="pack_first",
+    )(*arrays)
+    others = pl.pallas_call(
+        functools.partial(pack_kernel, head_count - 1),
+        in_specs=[in_hbm] * 5,
+        out_specs=[in_hbm] * (head_count - 1),
+        out_shape=[shape] * (head_count - 1),
         scratch_shapes=[
             pltpu.VMEM((4, rows, width), query.dtype),
-            pltpu.VMEM((head_count,) + chunk, query.dtype),
+            pltpu.VMEM((head_count - 1,) + chunk, query.dtype),
             pltpu.SemaphoreType.DMA((4,)),
-            pltpu.SemaphoreType.DMA((head_count,)),
+            pltpu.SemaphoreType.DMA((head_count - 1,)),
         ],
         compiler_params=pltpu.CompilerParams(vmem_limit_bytes=LARGE_VMEM_BYTES),
-        cost_estimate=pl.CostEstimate(flops=0, bytes_accessed=16 * rows * width, transcendentals=0),
+        cost_estimate=pl.CostEstimate(
+            flops=PACK_FLOPS, bytes_accessed=16 * rows * width, transcendentals=0
+        ),
         name="pack_heads",
-    )(query, key, value, dout)
+    )(*arrays, first)
+    return dict(zip(ORDER[2:] + ORDER[:1], others)) | {ORDER[1]: first}
 
 
 def choose_kernel(place_ref, gk_ref, gv_ref, own_ref, out_ref, held_ref, sems):
@@ -299,7 +337,7 @@
     columns = pl.ds(pl.multiple_of(place_ref[0] * head_size, head_size), head_size)
     copies = [
         pltpu.make_async_copy(
-            ref.at[place_ref[2 + slot], :, columns],
+            ref.at[place_ref[1 + slot], :, columns],
             out_ref.at[2 * kind + slot],
             sems.at[2 * kind + slot],
         )
@@ -364,11 +402,10 @@
     return jnp.concatenate(lists, axis=1), both
 
 
-def score_kernel(spans, shares, place_ref, rand_ref, *refs):
+def score_kernel(spans, place_ref, rand_ref, *refs):
     x_refs, g_ref = refs[:spans], refs[spans]
     q_all, k_all, o_all, p_all, ds_all = refs[spans + 1 : spans + 6]
-    share_refs = refs[spans + 6 : spans + 6 + shares]
-    v_all, table = refs[spans + 6 + shares :]
+    term_refs, v_all = refs[spans + 6 : spans + 8], refs[spans + 8]
     _, rows, head_size = x_refs[0].shape
     rand_count = rand_ref.shape[0] // (2 * spans)
     scaling = 1.0 / math.sqrt(head_size)
@@ -444,19 +481,16 @@
                 term = dot(weight[2 * BLK :], x, 1, 0)
                 so_far = table_terms[kind]
                 table_terms[kind] = term if so_far is None else so_far + term
-    table[...] = jnp.zeros(table.shape, table.dtype)
-    kinds = table.shape[0] // 2
-    for slot in range(2):
-        for kind, shared in enumerate(table_terms):
-            block = shared[slot * BLK : (slot + 1) * BLK]
-            table[kind * kinds + place_ref[2 + slot]] = block
-    for flip, ref in enumerate(share_refs):
-        count = table.shape[0] // shares
-        start = (place_ref[1] ^ flip) * count
-        ref[...] = table[pl.ds(start, count)].astype(ref.dtype)
-
-
-def scores(chunks, chosen, place, rand_head, table_size, shares):
+    mine = lax.axis_index("dp") % 2
+    for flip, ref in enumerate(term_refs):
+        ref[...] = jnp.zeros(ref.shape, ref.dtype)
+        term = jnp.where(mine == flip, table_terms[0], table_terms[1]).astype(ref.dtype)
+        for slot in range(2):
+            at = pl.multiple_of(place_ref[1 + slot] * BLK, BLK)
+            ref[pl.ds(at, BLK)] = term[slot * BLK : (slot + 1) * BLK]
+
+
+def scores(chunks, chosen, place, rand_head, table_size):
     spans = len(chunks)
     _, rows, head_size = chunks[0].shape
     keys = 8 * BLK
@@ -469,15 +503,14 @@
         half(spans * rows, head_size),
         half(spans, keys, rows),
         half(spans, keys, rows),
-    ] + [half(2 * table_size // shares, BLK, head_size)] * shares
+    ] + [half(table_size * BLK, head_size)] * 2
     results = pl.pallas_call(
-        functools.partial(score_kernel, spans, shares),
+        functools.partial(score_kernel, spans),
         in_specs=[pl.BlockSpec(memory_space=pltpu.SMEM)] * 2 + in_vmem(spans + 1),
         out_specs=in_vmem(len(outs)),
         out_shape=outs,
         scratch_shapes=[
             pltpu.VMEM((padded_rows, head_size), jnp.bfloat16),
-            pltpu.VMEM((2 * table_size, BLK, head_size), jnp.float32),
         ],
         compiler_params=pltpu.CompilerParams(vmem_limit_bytes=VMEM_BYTES),
         cost_estimate=pl.CostEstimate(
@@ -488,6 +521,10 @@
         name="scores",
     )(place, rand_head, *chunks, chosen)
     return results[:5], results[5:]
+
+
+def added(left, right):
+    return (left.astype(jnp.float32) + right.astype(jnp.float32)).astype(left.dtype)
 
 
 def far_spans(spans, rand_count):
@@ -578,7 +615,7 @@
     parts, out_ref = refs[:-1], refs[-1]
     head_size = parts[0].shape[2]
     head = lax.axis_index("ctx")
-    share = lax.axis_index("dp")
+    share = lax.axis_index("dp") % 2
     for side, ref in zip(sides, parts):
         for place in range(ref.shape[0]):
             bits = side[place // len(COLUMN)]
@@ -587,9 +624,9 @@
             out_ref[share ^ bits, :, columns] = ref[place].astype(out_ref.dtype)
 
 
-def early_table(shares, head_count, sides, parts):
+def early_table(head_count, sides, parts):
     _, rows, head_size = parts[0].shape
-    shape = (shares, rows, head_count * head_size)
+    shape = (2, rows, head_count * head_size)
     return pl.pallas_call(
         functools.partial(early_kernel, sides),
         in_specs=in_vmem(len(parts)),
@@ -612,7 +649,7 @@
     load = pltpu.make_async_copy(x_ref, x_held, x_sem)
     load.start()
     me = lax.axis_index("ctx")
-    share = lax.axis_index("dp")
+    share = lax.axis_index("dp") % 2
     stores = []
     for side, ref in zip(sides, parts):
         for place in range(ref.shape[0]):
@@ -651,7 +688,7 @@
         scratch_shapes=[
             pltpu.VMEM(x.shape, x.dtype),
             pltpu.VMEM((kinds, rows, heads * head_size), x.dtype),
-            pltpu.VMEM((blocks, rows, head_size), table.dtype),
+            pltpu.VMEM((blocks,) + parts[0].shape[1:], table.dtype),
             pltpu.SemaphoreType.DMA,
             pltpu.SemaphoreType.DMA((kinds,)),
             pltpu.SemaphoreType.DMA((blocks,)),
@@ -673,30 +710,27 @@
     head_count, block_count, _ = rand_blocks.shape
     head_size = query.shape[2] // head_count
     table_size = glob_keys.shape[0]
-    shares = lax.axis_size("dp")
     head = lax.axis_index("ctx").astype(jnp.int32)
-    sequence = lax.axis_index("dp").astype(jnp.int32)
     packed = pack(query, key, value, dout, head_count)
     chunks = [flipped(packed[flip], "ctx", flip) for flip in ORDER]
-    place = jnp.concatenate([head[None], sequence[None], glob_ids[0]])
+    place = jnp.concatenate([head[None], glob_ids[0]])
     rand_head = lax.dynamic_index_in_dim(rand_blocks, head, 0, keepdims=False).reshape(-1)
     rand_head = jnp.clip(rand_head, 0, block_count - 1)
     chosen, chunks[0] = choose(place, glob_keys, glob_values, packed[0])
-    held, terms = scores(chunks, chosen, place, rand_head, table_size, shares)
+    held, (kept, given) = scores(chunks, chosen, place, rand_head, table_size)
+    given = flipped(given, "dp", 1)
     sent = grads(rand_head, chosen, held)
-    terms = [flipped(terms[bits], "dp", bits) for bits in range(shares)]
-    *terms, sent = lax.optimization_barrier((*terms, sent))
+    given, sent = lax.optimization_barrier((given, sent))
     back = lax.all_to_all(sent, "ctx", 0, 0)
-    share = sum(term.astype(jnp.float32) for term in terms).astype(jnp.bfloat16)
-    share = share.reshape(1, -1, head_size)
-    column = jnp.concatenate([flipped(share, "ctx", flip) for flip in COLUMN])
-    even = jnp.concatenate([column, flipped(column, "dp", 2)])
+    chip = added(kept, given)
+    column = jnp.stack([flipped(chip, "ctx", flip) for flip in COLUMN])
+    even = added(column, flipped(column, "dp", 2))
     odd = flipped(even, "ctx", 1)
     beside_even = flipped(even, "dp", 1)
     beside_odd = flipped(odd, "dp", 1)
-    d_table = early_table(shares, head_count, ((0, 2), (1, 3)), [even, beside_even])
+    d_table = early_table(head_count, ((0,), (1,)), [even, beside_even])
     d_query, d_key, d_value, d_table = finish(
-        back, d_table, ((0, 2), (1, 3)), [odd, beside_odd]
+        back, d_table, ((0,), (1,)), [odd, beside_odd]
     )
     return (d_query, d_key, d_value, d_table.reshape((2,) + glob_keys.shape))
 

time: 67.9 us -> 65.3 us (0.962)
  starting transfers between devices: 32.3 us -> 26.7 us
  waiting for transfers between devices: 19.4 us -> 23.7 us
  local copies, waits for them, and re-layouts: 3.22 us -> 1.11 us
  Pallas kernels: 11.1 us -> 12.5 us
    ppermute x17 -> x15, waiting for transfers between devices: 18 us -> 23.7 us  [flipped(): lax.ppermute(array, axis, [(i, i ^ bits) for i in range(lax.axis_size(axi...]
    ppermute x17 -> x15, starting transfers between devices: 28.1 us -> 22.5 us  [flipped(): lax.ppermute(array, axis, [(i, i ^ bits) for i in range(lax.axis_size(axi...]
    unnamed x12 -> x10, local copies, waits for them, and re-layouts: 3.03 us -> 0.93 us
    pallas_call x2 -> x3, Pallas kernels: 4.78 us -> 6.27 us  [the longest x1 2.5 us: scores(): pl.pallas_call(functools.partial(score_kernel, spans), in_specs=[pl.Block...]
    all_to_all x1, waiting for transfers between devices: 1.47 us -> 0.01 us  [on_heads(): back = lax.all_to_all(sent, 'ctx', 0, 0)]
  transfers between devices with their start and end apart: 18 -> 16, of which waited for: 8 -> 8; matrix products, arithmetic and copies ran while one was open for 1% -> 1% of each run, Pallas kernels for 7% -> 11%
where the time goes in v5:
time: 65.3 us; the launch traced here: 65 us
  starting transfers between devices  26.7 us (41%)
  waiting for transfers between devices  23.7 us (36%)
  Pallas kernels  12.5 us (19%)
  local copies, waits for them, and re-layouts  1.11 us (2%)
  between operations  0.78 us (1%)
    ppermute x15, waiting for transfers between devices, flipped(): lax.ppermute(array, axis, [(i, i ^ bits) for i in range(lax.axis_size(axi...  23.7 us
    ppermute x15, starting transfers between devices, flipped(): lax.ppermute(array, axis, [(i, i ^ bits) for i in range(lax.axis_size(axi...  22.5 us
    all_to_all x1, starting transfers between devices, on_heads(): back = lax.all_to_all(sent, 'ctx', 0, 0)  4.21 us
    pallas_call x1, Pallas kernels, grads(): pl.pallas_call(grad_kernel, in_specs=[pl.BlockSpec(memory_space=pltpu.SME...  2.6 us
    pallas_call x1, Pallas kernels, scores(): pl.pallas_call(functools.partial(score_kernel, spans), in_specs=[pl.Block...  2.5 us
    pallas_call x1, Pallas kernels, pack(): pl.pallas_call(functools.partial(pack_kernel, head_count - 1), in_specs=[...  2.22 us
    pallas_call x1, Pallas kernels, pack(): pl.pallas_call(first_kernel, in_specs=[in_hbm] * 4, out_specs=in_hbm, out...  1.56 us
    pallas_call x1, Pallas kernels, early_table(): pl.pallas_call(functools.partial(early_kernel, sides), in_specs=in_vmem(l...  1.45 us
  transfers between devices with their start and end apart: 16, of which 8 were waited for; matrix products, arithmetic and copies ran while one was open for 1% of the time, Pallas kernels for 11%

profile of v5, /device:TPU:0, one launch (start us, length us, event | category | flops | bytes accessed | tf_op | source)
XLA Modules:
  0.0 65.0 jit_solution(9187528605982331937)
XLA Ops:
  0.6 1.6 %pack_first.1.refs_4_ = bf16[4,128,128]{2,1,0:T(8,128)(2,1)} custom-call(bf16[1,128,1024]{2,1,0:T(8,128)(2,1)} %refs_0_.1, bf16[1,128,1024]{2,1,0:T(8,128)(2,1)} %refs_1_.1, bf16[1,128,1024]{2,1,0:T(8,128)(2,1)} %refs_2_.1, bf16[1,128,1024]{2,1,0:T(8,128)(2,1)} %refs_3_.1), custom_call_target="tpu_custom_call" | custom-call | bytes 262144 | tf_op jit(solution)/shard_map/pack_first/pallas_call | solution.py:301
  2.2 4.1 %collective-permute-start = (bf16[4,128,128]{2,1,0:T(8,128)(2,1)}, bf16[4,128,128]{2,1,0:T(8,128)(2,1)S(1)}, u32[]{:S(2)}, u32[]{:S(2)}) collective-permute-start(bf16[4,128,128]{2,1,0:T(8,128)(2,1)} %pack_first.1.refs_4_), channel_id=1, source_target_pairs={{0,16},{4,20},{8,24},{12,28},{16,0},{20,4},{24,8},{28,12},{1,17},{... | collective-permute-start | bytes 393224 | tf_op jit(solution)/shard_map/ppermute | solution.py:706
  6.3 2.2 %pack_heads.1 = (bf16[4,128,128]{2,1,0:T(8,128)(2,1)}, bf16[4,128,128]{2,1,0:T(8,128)(2,1)}, bf16[4,128,128]{2,1,0:T(8,128)(2,1)}, bf16[4,128,128]{2,1,0:T(8,128...) custom-call(bf16[1,128,1024]{2,1,0:T(8,128)(2,1)} %refs_0_.1, ...), custom_call_target="tpu_custom_call" | custom-call | flops 2000000000 | bytes 2097152 | tf_op jit(solution)/shard_map/pack_heads/pallas_call | solution.py:315
  8.6 1.6 %collective-permute-start.1 = (bf16[4,128,128]{2,1,0:T(8,128)(2,1)}, bf16[4,128,128]{2,1,0:T(8,128)(2,1)S(1)}, u32[]{:S(2)}, u32[]{:S(2)}) collective-permute-start(bf16[4,128,128]{2,1,0:T(8,128)(2,1)} %get-tuple-element.28), channel_id=1, source_target_pairs={{0,8},{4,12},{8,0},{12,4},{16,24},{20,28},{24,16},{28,20},{1,9},{5... | collective-permute-start | bytes 393224 | tf_op jit(solution)/shard_map/ppermute | solution.py:706
  10.2 1.3 %collective-permute-start.2 = (bf16[4,128,128]{2,1,0:T(8,128)(2,1)}, bf16[4,128,128]{2,1,0:T(8,128)(2,1)S(1)}, u32[]{:S(2)}, u32[]{:S(2)}) collective-permute-start(bf16[4,128,128]{2,1,0:T(8,128)(2,1)} %get-tuple-element.29), channel_id=1, source_target_pairs={{0,20},{4,16},{8,28},{12,24},{16,4},{20,0},{24,12},{28,8},{1,21},{... | collective-permute-start | bytes 393224 | tf_op jit(solution)/shard_map/ppermute | solution.py:706
  11.7 3.8 %collective-permute-start.4 = (bf16[4,128,128]{2,1,0:T(8,128)(2,1)}, bf16[4,128,128]{2,1,0:T(8,128)(2,1)S(1)}, u32[]{:S(2)}, u32[]{:S(2)}) collective-permute-start(bf16[4,128,128]{2,1,0:T(8,128)(2,1)} %get-tuple-element.31), channel_id=1, source_target_pairs={{0,24},{4,28},{8,16},{12,20},{16,8},{20,12},{24,0},{28,4},{1,25},{... | collective-permute-start | bytes 393224 | tf_op jit(solution)/shard_map/ppermute | solution.py:706
  15.5 2.8 %collective-permute-start.5 = (bf16[4,128,128]{2,1,0:T(8,128)(2,1)}, bf16[4,128,128]{2,1,0:T(8,128)(2,1)S(1)}, u32[]{:S(2)}, u32[]{:S(2)}) collective-permute-start(bf16[4,128,128]{2,1,0:T(8,128)(2,1)} %get-tuple-element.32), channel_id=1, source_target_pairs={{0,28},{4,24},{8,20},{12,16},{16,12},{20,8},{24,4},{28,0},{1,29},{... | collective-permute-start | bytes 393224 | tf_op jit(solution)/shard_map/ppermute | solution.py:706
  18.3 0.7 %collective-permute-start.6 = (bf16[4,128,128]{2,1,0:T(8,128)(2,1)}, bf16[4,128,128]{2,1,0:T(8,128)(2,1)S(1)}, u32[]{:S(2)}, u32[]{:S(2)}) collective-permute-start(bf16[4,128,128]{2,1,0:T(8,128)(2,1)} %get-tuple-element.33), channel_id=1, source_target_pairs={{0,4},{4,0},{8,12},{12,8},{16,20},{20,16},{24,28},{28,24},{1,5},{5... | collective-permute-start | bytes 393224 | tf_op jit(solution)/shard_map/ppermute | solution.py:706
  19.2 0.9 %copy-done.3 = bf16[4,128,128]{2,1,0:T(8,128)(2,1)S(1)} copy-done((bf16[4,128,128]{2,1,0:T(8,128)(2,1)S(1)}, bf16[4,128,128]{2,1,0:T(8,128)(2,1)}, u32[]{:S(2)}) %copy-start.3) | copy-done | bytes 131096
  20.1 0.8 %choose_blocks.1 = (bf16[4,64,128]{2,1,0:T(8,128)(2,1)S(1)}, bf16[4,128,128]{2,1,0:T(8,128)(2,1)S(1)}) custom-call(s32[3]{0:T(128)S(1)} %pad_add_fusion.place_ref, bf16[4,64,1024]{2,1,0:T(8,128)(2,1)S(1)} %copy-done.1, bf16[4,64,1024]{2,1,0:T(8,128)(2,1)S(1)} %copy-done.2, bf16[4,128,128]{2,1,0:T(8,128)(2,1)S(1)} %copy-done.3), custom_call_target="tpu_custom_call" | custom-call | bytes 131072 | tf_op jit(solution)/shard_map/choose_blocks/pallas_call | solution.py:356
  20.9 0.5 collective-permute-done.2.refs_3_
  21.4 6.3 %collective-permute-done.3.refs_4_ = bf16[4,128,128]{2,1,0:T(8,128)(2,1)S(1)} collective-permute-done((bf16[4,128,128]{2,1,0:T(8,128)(2,1)}, bf16[4,128,128]{2,1,0:T(8,128)(2,1)S(1)}, u32[]{:S(2)}, u32[]{:S(2)}) %collective-permute-start.3) | collective-permute-done | bytes 131104 | tf_op jit(solution)/shard_map/ppermute | solution.py:706
  28.1 2.5 %scores.1 = (bf16[1024,128]{1,0:T(8,128)(2,1)S(1)}, bf16[1152,128]{1,0:T(8,128)(2,1)S(1)}, bf16[1024,128]{1,0:T(8,128)(2,1)S(1)}, bf16[8,512,128]{2,1,0:T(8,128)...) custom-call(s32[3]{0:T(128)S(1)} %pad_add_fusion.place_ref, ...), custom_call_target="tpu_custom_call" | custom-call | flops 268435456 | bytes 1048576 | tf_op jit(solution)/shard_map/scores/pallas_call | solution.py:507
  30.6 2.6 %grads.1 = bf16[8,3,128,128]{3,2,1,0:T(8,128)(2,1)} custom-call(s32[48]{0:T(128)S(1)} %min.12.rand_ref, bf16[4,64,128]{2,1,0:T(8,128)(2,1)S(1)} %get-tuple-element.34.refs_8_.g_ref, bf16[1024,128]{1,0:T(8,128)(2,1)S(1)} %get-tuple-element.37.q_all, bf16[1152,128]{1,0:T(8,128)(2,1)S(1)} %get-tuple-element.38.k_all, ...), custom_call_target="tpu_custom_call" | custom-call | flops 402653184 | bytes 1048576 | tf_op jit(solution)/shard_map/grads/pallas_call | solution.py:595
  33.3 2.8 %collective-permute-start.10 = (bf16[256,128]{1,0:T(8,128)(2,1)S(1)}, bf16[256,128]{1,0:T(8,128)(2,1)S(1)}, u32[]{:S(2)}, u32[]{:S(2)}) collective-permute-start(bf16[256,128]{1,0:T(8,128)(2,1)S(1)} %add_convert_fusion.1), channel_id=1, source_target_pairs={{0,24},{4,28},{8,16},{12,20},{16,8},{20,12},{24,0},{28,4},{1,25},{... | collective-permute-start | bytes 196616 | tf_op jit(solution)/shard_map/ppermute | solution.py:706
  36.1 2.6 %collective-permute-start.9 = (bf16[256,128]{1,0:T(8,128)(2,1)S(1)}, bf16[256,128]{1,0:T(8,128)(2,1)S(1)}, u32[]{:S(2)}, u32[]{:S(2)}) collective-permute-start(bf16[256,128]{1,0:T(8,128)(2,1)S(1)} %add_convert_fusion.1), channel_id=1, source_target_pairs={{0,16},{4,20},{8,24},{12,28},{16,0},{20,4},{24,8},{28,12},{1,17},{... | collective-permute-start | bytes 196616 | tf_op jit(solution)/shard_map/ppermute | solution.py:706
  38.7 0.5 collective-permute-start.8
  39.2 4.2 %all-to-all-start = ((bf16[8,3,128,128]{3,2,1,0:T(8,128)(2,1)}), bf16[8,3,128,128]{3,2,1,0:T(8,128)(2,1)S(1)}, u32[]{:S(2)}, u32[]{:S(2)}) async-start(bf16[8,3,128,128]{3,2,1,0:T(8,128)(2,1)} %grads.1), calls=%async_computation | async-start | bytes 1572864 | tf_op jit(solution)/shard_map/all_to_all | solution.py:724
  43.4 0.5 collective-permute-done.9
  44.2 1.6 %collective-permute-start.11 = (bf16[4,256,128]{2,1,0:T(8,128)(2,1)S(1)}, bf16[4,256,128]{2,1,0:T(8,128)(2,1)S(1)}, u32[]{:S(2)}, u32[]{:S(2)}) collective-permute-start(bf16[4,256,128]{2,1,0:T(8,128)(2,1)S(1)} %pad_maximum_fusion), channel_id=1, source_target_pairs={{0,2},{1,3},{2,0},{3,1},{4,6},{5,7},{6,4},{7,5},{8,10},{9,11},{10,... | collective-permute-start | bytes 786440 | tf_op jit(solution)/shard_map/ppermute | solution.py:706
  45.8 6.7 %collective-permute-done.11 = bf16[4,256,128]{2,1,0:T(8,128)(2,1)S(1)} collective-permute-done((bf16[4,256,128]{2,1,0:T(8,128)(2,1)S(1)}, bf16[4,256,128]{2,1,0:T(8,128)(2,1)S(1)}, u32[]{:S(2)}, u32[]{:S(2)}) %collective-permute-start.11) | collective-permute-done | bytes 262176 | tf_op jit(solution)/shard_map/ppermute | solution.py:706
  53.0 9.0 %collective-permute-done.12.refs_0_ = bf16[4,256,128]{2,1,0:T(8,128)(2,1)S(1)} collective-permute-done((bf16[4,256,128]{2,1,0:T(8,128)(2,1)S(1)}, bf16[4,256,128]{2,1,0:T(8,128)(2,1)S(1)}, u32[]{:S(2)}, u32[]{:S(2)}) %collective-permute-start.12) | collective-permute-done | bytes 262176 | tf_op jit(solution)/shard_map/ppermute | solution.py:706
  62.0 1.5 %early_table.1.refs_3_ = f32[2,256,1024]{2,1,0:T(8,128)} custom-call(bf16[4,256,128]{2,1,0:T(8,128)(2,1)S(1)} %add_convert_fusion.refs_0_, bf16[4,256,128]{2,1,0:T(8,128)(2,1)S(1)} %collective-permute-done.14.refs_1_), custom_call_target="tpu_custom_call" | custom-call | flops 5000000000 | bytes 2097152 | tf_op jit(solution)/shard_map/early_table/pallas_call | solution.py:630
  63.6 1.4 %finish.1 = (bf16[1,128,1024]{2,1,0:T(8,128)(2,1)}, bf16[1,128,1024]{2,1,0:T(8,128)(2,1)}, bf16[1,128,1024]{2,1,0:T(8,128)(2,1)}, f32[2,256,1024]{2,1,0:T(8,128)}) custom-call(bf16[4,256,128]{2,1,0:T(8,128)(2,1)S(1)} %collective-permute-done.12.refs_0_, bf16[4,256,128]{2,1,0:T(8,128)(2,1)S(1)} %collective-permute-done.13.refs_1_, ...), custom_call_target="tpu_custom_call", output_to_operand_aliasing={{3}: (3, {})} | custom-call | bytes 2097152 | tf_op jit(solution)/shard_map/finish/pallas_call | solution.py:683
  (33 shorter events, 1.8 us)
Async XLA Ops:
  0.6 14.8 %copy-start = (s32[8,16,3]{1,0,2:T(8,128)S(1)}, s32[8,16,3]{1,0,2:T(8,128)}, u32[]{:S(2)}) copy-start(s32[8,16,3]{1,0,2:T(8,128)} %param.15) | copy-start | bytes 4612
  2.2 16.9 %copy-start.4 = (s32[1,2]{1,0:T(1,128)S(1)}, s32[1,2]{1,0:T(1,128)}, u32[]{:S(2)}) copy-start(s32[1,2]{1,0:T(1,128)} %param.14) | copy-start | bytes 28
  2.2 17.0 %copy-start.1 = (bf16[4,64,1024]{2,1,0:T(8,128)(2,1)S(1)}, bf16[4,64,1024]{2,1,0:T(8,128)(2,1)}, u32[]{:S(2)}) copy-start(bf16[4,64,1024]{2,1,0:T(8,128)(2,1)} %gk_ref.1) | copy-start | bytes 1572868
  2.2 17.0 %copy-start.2 = (bf16[4,64,1024]{2,1,0:T(8,128)(2,1)S(1)}, bf16[4,64,1024]{2,1,0:T(8,128)(2,1)}, u32[]{:S(2)}) copy-start(bf16[4,64,1024]{2,1,0:T(8,128)(2,1)} %gv_ref.1) | copy-start | bytes 1572868
  2.2 13.2 %collective-permute-start = (bf16[4,128,128]{2,1,0:T(8,128)(2,1)}, bf16[4,128,128]{2,1,0:T(8,128)(2,1)S(1)}, u32[]{:S(2)}, u32[]{:S(2)}) collective-permute-start(bf16[4,128,128]{2,1,0:T(8,128)(2,1)} %pack_first.1.refs_4_), channel_id=1, source_target_pairs={{0,16},{4,20},{8,24},{12,28},{16,0},{20,4},{24,8},{28,12},{1,17},{... | collective-permute-start | bytes 393224 | tf_op jit(solution)/shard_map/ppermute | solution.py:706
  8.6 9.7 %collective-permute-start.1 = (bf16[4,128,128]{2,1,0:T(8,128)(2,1)}, bf16[4,128,128]{2,1,0:T(8,128)(2,1)S(1)}, u32[]{:S(2)}, u32[]{:S(2)}) collective-permute-start(bf16[4,128,128]{2,1,0:T(8,128)(2,1)} %get-tuple-element.28), channel_id=1, source_target_pairs={{0,8},{4,12},{8,0},{12,4},{16,24},{20,28},{24,16},{28,20},{1,9},{5... | collective-permute-start | bytes 393224 | tf_op jit(solution)/shard_map/ppermute | solution.py:706
  10.2 11.3 %collective-permute-start.2 = (bf16[4,128,128]{2,1,0:T(8,128)(2,1)}, bf16[4,128,128]{2,1,0:T(8,128)(2,1)S(1)}, u32[]{:S(2)}, u32[]{:S(2)}) collective-permute-start(bf16[4,128,128]{2,1,0:T(8,128)(2,1)} %get-tuple-element.29), channel_id=1, source_target_pairs={{0,20},{4,16},{8,28},{12,24},{16,4},{20,0},{24,12},{28,8},{1,21},{... | collective-permute-start | bytes 393224 | tf_op jit(solution)/shard_map/ppermute | solution.py:706
  11.5 16.3 %collective-permute-start.3 = (bf16[4,128,128]{2,1,0:T(8,128)(2,1)}, bf16[4,128,128]{2,1,0:T(8,128)(2,1)S(1)}, u32[]{:S(2)}, u32[]{:S(2)}) collective-permute-start(bf16[4,128,128]{2,1,0:T(8,128)(2,1)} %get-tuple-element.30), channel_id=1, source_target_pairs={{0,12},{4,8},{8,4},{12,0},{16,28},{20,24},{24,20},{28,16},{1,13},{... | collective-permute-start | bytes 393224 | tf_op jit(solution)/shard_map/ppermute | solution.py:706
  11.7 16.1 %collective-permute-start.4 = (bf16[4,128,128]{2,1,0:T(8,128)(2,1)}, bf16[4,128,128]{2,1,0:T(8,128)(2,1)S(1)}, u32[]{:S(2)}, u32[]{:S(2)}) collective-permute-start(bf16[4,128,128]{2,1,0:T(8,128)(2,1)} %get-tuple-element.31), channel_id=1, source_target_pairs={{0,24},{4,28},{8,16},{12,20},{16,8},{20,12},{24,0},{28,4},{1,25},{... | collective-permute-start | bytes 393224 | tf_op jit(solution)/shard_map/ppermute | solution.py:706
  15.5 12.2 %collective-permute-start.5 = (bf16[4,128,128]{2,1,0:T(8,128)(2,1)}, bf16[4,128,128]{2,1,0:T(8,128)(2,1)S(1)}, u32[]{:S(2)}, u32[]{:S(2)}) collective-permute-start(bf16[4,128,128]{2,1,0:T(8,128)(2,1)} %get-tuple-element.32), channel_id=1, source_target_pairs={{0,28},{4,24},{8,20},{12,16},{16,12},{20,8},{24,4},{28,0},{1,29},{... | collective-permute-start | bytes 393224 | tf_op jit(solution)/shard_map/ppermute | solution.py:706
  18.3 9.8 %collective-permute-start.6 = (bf16[4,128,128]{2,1,0:T(8,128)(2,1)}, bf16[4,128,128]{2,1,0:T(8,128)(2,1)S(1)}, u32[]{:S(2)}, u32[]{:S(2)}) collective-permute-start(bf16[4,128,128]{2,1,0:T(8,128)(2,1)} %get-tuple-element.33), channel_id=1, source_target_pairs={{0,4},{4,0},{8,12},{12,8},{16,20},{20,16},{24,28},{28,24},{1,5},{5... | collective-permute-start | bytes 393224 | tf_op jit(solution)/shard_map/ppermute | solution.py:706
  19.2 0.9 %copy-start.3 = (bf16[4,128,128]{2,1,0:T(8,128)(2,1)S(1)}, bf16[4,128,128]{2,1,0:T(8,128)(2,1)}, u32[]{:S(2)}) copy-start(bf16[4,128,128]{2,1,0:T(8,128)(2,1)} %get-tuple-element.26.own_ref) | copy-start | bytes 393220
  30.6 2.7 %collective-permute-start.7 = (bf16[256,128]{1,0:T(8,128)(2,1)S(1)}, bf16[256,128]{1,0:T(8,128)(2,1)S(1)}, u32[]{:S(2)}, u32[]{:S(2)}) collective-permute-start(bf16[256,128]{1,0:T(8,128)(2,1)S(1)} %get-tuple-element.36), channel_id=1, source_target_pairs={{0,1},{1,0},{2,3},{3,2},{4,5},{5,4},{6,7},{7,6},{8,9},{9,8},{10,11... | collective-permute-start | bytes 196616 | tf_op jit(solution)/shard_map/ppermute | solution.py:706
  33.3 10.1 %collective-permute-start.10 = (bf16[256,128]{1,0:T(8,128)(2,1)S(1)}, bf16[256,128]{1,0:T(8,128)(2,1)S(1)}, u32[]{:S(2)}, u32[]{:S(2)}) collective-permute-start(bf16[256,128]{1,0:T(8,128)(2,1)S(1)} %add_convert_fusion.1), channel_id=1, source_target_pairs={{0,24},{4,28},{8,16},{12,20},{16,8},{20,12},{24,0},{28,4},{1,25},{... | collective-permute-start | bytes 196616 | tf_op jit(solution)/shard_map/ppermute | solution.py:706
  36.1 7.8 %collective-permute-start.9 = (bf16[256,128]{1,0:T(8,128)(2,1)S(1)}, bf16[256,128]{1,0:T(8,128)(2,1)S(1)}, u32[]{:S(2)}, u32[]{:S(2)}) collective-permute-start(bf16[256,128]{1,0:T(8,128)(2,1)S(1)} %add_convert_fusion.1), channel_id=1, source_target_pairs={{0,16},{4,20},{8,24},{12,28},{16,0},{20,4},{24,8},{28,12},{1,17},{... | collective-permute-start | bytes 196616 | tf_op jit(solution)/shard_map/ppermute | solution.py:706
  38.7 5.5 %collective-permute-start.8 = (bf16[256,128]{1,0:T(8,128)(2,1)S(1)}, bf16[256,128]{1,0:T(8,128)(2,1)S(1)}, u32[]{:S(2)}, u32[]{:S(2)}) collective-permute-start(bf16[256,128]{1,0:T(8,128)(2,1)S(1)} %add_convert_fusion.1), channel_id=1, source_target_pairs={{0,8},{4,12},{8,0},{12,4},{16,24},{20,28},{24,16},{28,20},{1,9},{5... | collective-permute-start | bytes 196616 | tf_op jit(solution)/shard_map/ppermute | solution.py:706
  39.2 24.4 %all-to-all-start = ((bf16[8,3,128,128]{3,2,1,0:T(8,128)(2,1)}), bf16[8,3,128,128]{3,2,1,0:T(8,128)(2,1)S(1)}, u32[]{:S(2)}, u32[]{:S(2)}) async-start(bf16[8,3,128,128]{3,2,1,0:T(8,128)(2,1)} %grads.1), calls=%async_computation | async-start | bytes 1572864 | tf_op jit(solution)/shard_map/all_to_all | solution.py:724
  44.2 8.3 %collective-permute-start.11 = (bf16[4,256,128]{2,1,0:T(8,128)(2,1)S(1)}, bf16[4,256,128]{2,1,0:T(8,128)(2,1)S(1)}, u32[]{:S(2)}, u32[]{:S(2)}) collective-permute-start(bf16[4,256,128]{2,1,0:T(8,128)(2,1)S(1)} %pad_maximum_fusion), channel_id=1, source_target_pairs={{0,2},{1,3},{2,0},{3,1},{4,6},{5,7},{6,4},{7,5},{8,10},{9,11},{10,... | collective-permute-start | bytes 786440 | tf_op jit(solution)/shard_map/ppermute | solution.py:706
  52.5 9.5 %collective-permute-start.12 = (bf16[4,256,128]{2,1,0:T(8,128)(2,1)S(1)}, bf16[4,256,128]{2,1,0:T(8,128)(2,1)S(1)}, u32[]{:S(2)}, u32[]{:S(2)}) collective-permute-start(bf16[4,256,128]{2,1,0:T(8,128)(2,1)S(1)} %add_convert_fusion.refs_0_), channel_id=1, source_target_pairs={{0,4},{4,0},{8,12},{12,8},{16,20},{20,16},{24,28},{28,24},{1,5},{5... | collective-permute-start | bytes 786440 | tf_op jit(solution)/shard_map/ppermute | solution.py:706
  53.0 9.1 %collective-permute-start.14 = (bf16[4,256,128]{2,1,0:T(8,128)(2,1)S(1)}, bf16[4,256,128]{2,1,0:T(8,128)(2,1)S(1)}, u32[]{:S(2)}, u32[]{:S(2)}) collective-permute-start(bf16[4,256,128]{2,1,0:T(8,128)(2,1)S(1)} %add_convert_fusion.refs_0_), channel_id=1, source_target_pairs={{0,1},{1,0},{2,3},{3,2},{4,5},{5,4},{6,7},{7,6},{8,9},{9,8},{10,11... | collective-permute-start | bytes 786440 | tf_op jit(solution)/shard_map/ppermute | solution.py:706
  62.0 1.5 %collective-permute-start.13 = (bf16[4,256,128]{2,1,0:T(8,128)(2,1)S(1)}, bf16[4,256,128]{2,1,0:T(8,128)(2,1)S(1)}, u32[]{:S(2)}, u32[]{:S(2)}) collective-permute-start(bf16[4,256,128]{2,1,0:T(8,128)(2,1)S(1)} %collective-permute-done.12.refs_0_), channel_id=1, source_target_pairs={{0,1},{1,0},{2,3},{3,2},{4,5},{5,4},{6,7},{7,6},{8,9},{9,8},{10,11... | collective-permute-start | bytes 786440 | tf_op jit(solution)/shard_map/ppermute | solution.py:706

commit v6 on v5

--- a/solution.py
+++ b/solution.py
@@ -234,6 +234,7 @@
 LARGE_VMEM_BYTES = 60 * 1024 * 1024
 FINISH_VMEM_BYTES = 24 * 1024 * 1024
 MASKED = -1e30
+FIRST_BYTES = 60 * 1024 * 1024
 PACK_FLOPS = 2 * 10**9
 EARLY_FLOPS = 5 * 10**9
 GROUP = 8
@@ -250,12 +251,12 @@
     return [pl.BlockSpec(memory_space=pltpu.VMEM)] * count
 
 
-def first_kernel(q_ref, k_ref, v_ref, o_ref, out_ref, held, sems, out_sem):
+def first_kernel(q_ref, k_ref, v_ref, o_ref, out_ref, sems):
     head_size = out_ref.shape[2]
     at = pl.multiple_of((lax.axis_index("ctx") ^ ORDER[1]) * head_size, head_size)
     copies = [
         pltpu.make_async_copy(
-            ref.at[0, :, pl.ds(at, head_size)], held.at[place], sems.at[place]
+            ref.at[0, :, pl.ds(at, head_size)], out_ref.at[place], sems.at[place]
         )
         for place, ref in enumerate((q_ref, k_ref, v_ref, o_ref))
     ]
@@ -263,9 +264,6 @@
         copy.start()
     for copy in copies:
         copy.wait()
-    store = pltpu.make_async_copy(held, out_ref, out_sem)
-    store.start()
-    store.wait()
 
 
 def pack_kernel(count, *refs):
@@ -301,14 +299,10 @@
     first = pl.pallas_call(
         first_kernel,
         in_specs=[in_hbm] * 4,
-        out_specs=in_hbm,
+        out_specs=pl.BlockSpec(memory_space=pltpu.VMEM),
         out_shape=shape,
-        scratch_shapes=[
-            pltpu.VMEM(chunk, query.dtype),
-            pltpu.SemaphoreType.DMA((4,)),
-            pltpu.SemaphoreType.DMA,
-        ],
-        compiler_params=pltpu.CompilerParams(vmem_limit_bytes=LARGE_VMEM_BYTES),
+        scratch_shapes=[pltpu.SemaphoreType.DMA((4,))],
+        compiler_params=pltpu.CompilerParams(vmem_limit_bytes=FIRST_BYTES),
         cost_estimate=pl.CostEstimate(flops=0, bytes_accessed=2 * rows * width, transcendentals=0),
         name="pack_first",
     )(*arrays)
@@ -409,6 +403,7 @@
     _, rows, head_size = x_refs[0].shape
     rand_count = rand_ref.shape[0] // (2 * spans)
     scaling = 1.0 / math.sqrt(head_size)
+    rate = scaling * math.log2(math.e)
     me = place_ref[0]
     top = BLK + spans * rows
     for pool in (k_all, v_all):
@@ -434,32 +429,35 @@
             o = o_all[at : at + rows]
             places = list_places(rand_ref, span, rand_count)
             k_own, k_both = gathered(k_all, at, places, gk)
-            v_own, v_both = gathered(v_all, at, places, gv)
-            s_own = dot(k_own, split_rows(q), 1, 1) * scaling
-            s_both = dot(k_both, q, 1, 1) * scaling
-            g_own = dot(v_own, split_rows(o), 1, 1)
-            g_both = dot(v_both, o, 1, 1)
+            s_own = dot(k_own, split_rows(q), 1, 1)
+            s_both = dot(k_both, q, 1, 1)
             if span == 0 or span == spans - 1:
                 row = lax.broadcasted_iota(jnp.int32, (own, 1), 0) < BLK
                 outside = row & (first if span == 0 else jnp.logical_not(first))
-                s_own = jnp.where(outside, MASKED, s_own)
-            made.append((q, o, s_own, s_both, g_own, g_both))
+                s_own = jnp.where(outside, MASKED / scaling, s_own)
+            made.append((q, o, s_own, s_both))
         tops = [
             jnp.maximum(
                 jnp.max(s_own, axis=0, keepdims=True), jnp.max(s_both, axis=0, keepdims=True)
             )
-            for _, _, s_own, s_both, _, _ in made
+            for _, _, s_own, s_both in made
         ]
-        powers = [
-            (jnp.exp(s_own - top_score), jnp.exp(s_both - top_score))
-            for top_score, (_, _, s_own, s_both, _, _) in zip(tops, made)
-        ]
+        powers = []
+        values = []
+        for span, top_score, (q, o, s_own, s_both) in zip(members, tops, made):
+            places = list_places(rand_ref, span, rand_count)
+            v_own, v_both = gathered(v_all, span * rows, places, gv)
+            values.append((dot(v_own, split_rows(o), 1, 1), dot(v_both, o, 1, 1)))
+            powers.append(
+                (jnp.exp2((s_own - top_score) * rate), jnp.exp2((s_both - top_score) * rate))
+            )
         inverses = [
             1.0 / (jnp.sum(e_own, axis=0, keepdims=True) + jnp.sum(e_both, axis=0, keepdims=True))
             for e_own, e_both in powers
         ]
-        weights = []
-        for (e_own, e_both), inverse, (_, _, _, _, g_own, g_both) in zip(powers, inverses, made):
+        for span, (e_own, e_both), inverse, (q, o, _, _), (g_own, g_both) in zip(
+            members, powers, inverses, made, values
+        ):
             p_own = e_own * inverse
             p_both = e_both * inverse
             pb_own = p_own.astype(jnp.bfloat16)
@@ -467,10 +465,6 @@
             row_dot = jnp.sum(
                 pb_own.astype(jnp.float32) * g_own, axis=0, keepdims=True
             ) + jnp.sum(pb_both.astype(jnp.float32) * g_both, axis=0, keepdims=True)
-            weights.append((p_own, p_both, pb_own, pb_both, row_dot))
-        for span, (q, o, _, _, g_own, g_both), (p_own, p_both, pb_own, pb_both, row_dot) in zip(
-            members, made, weights
-        ):
             ds_own = (p_own * (g_own - row_dot) * scaling).astype(jnp.bfloat16)
             ds_both = (p_both * (g_both - row_dot) * scaling).astype(jnp.bfloat16)
             p_all[span, :own] = pb_own
@@ -545,11 +539,6 @@
         at = span * rows
         q = q_all[at : at + rows]
         o = o_all[at : at + rows]
-        k_own, k_both = gathered(k_all, at, list_places(rand_ref, span, rand_count), gk)
-        wide = dot(ds_all[span, :own], k_own, 0, 0)
-        dq = jnp.concatenate([wide[:BLK, :head_size], wide[BLK:, head_size:]], axis=0)
-        dq = dq + dot(ds_all[span, own:], k_both, 0, 0)
-        made[span, 0] = dq.astype(made.dtype)
         keeps = [first]
         for slot, offset in enumerate(offsets):
             lower = [
@@ -569,6 +558,12 @@
         terms.append(pair)
     copies = []
     for span in range(spans):
+        at = span * rows
+        k_own, k_both = gathered(k_all, at, list_places(rand_ref, span, rand_count), gk)
+        wide = dot(ds_all[span, :own], k_own, 0, 0)
+        dq = jnp.concatenate([wide[:BLK, :head_size], wide[BLK:, head_size:]], axis=0)
+        dq = dq + dot(ds_all[span, own:], k_both, 0, 0)
+        made[span, 0] = dq.astype(made.dtype)
         for kind in range(2):
             part = lambda source, start, count: terms[source][kind][start : start + count]
             edges = [

time: 65.3 us -> 64.8 us (level)
  no operation moved by 1% of the time
where the time goes in v6:
time: 64.8 us; the launch traced here: 64.5 us
  starting transfers between devices  26.7 us (41%)
  waiting for transfers between devices  23.7 us (37%)
  Pallas kernels  12 us (19%)
  local copies, waits for them, and re-layouts  1.11 us (2%)
  between operations  0.78 us (1%)
    ppermute x15, waiting for transfers between devices, flipped(): lax.ppermute(array, axis, [(i, i ^ bits) for i in range(lax.axis_size(axi...  23.7 us
    ppermute x15, starting transfers between devices, flipped(): lax.ppermute(array, axis, [(i, i ^ bits) for i in range(lax.axis_size(axi...  22.5 us
    all_to_all x1, starting transfers between devices, on_heads(): back = lax.all_to_all(sent, 'ctx', 0, 0)  4.21 us
    pallas_call x1, Pallas kernels, grads(): pl.pallas_call(grad_kernel, in_specs=[pl.BlockSpec(memory_space=pltpu.SME...  2.38 us
    pallas_call x1, Pallas kernels, scores(): pl.pallas_call(functools.partial(score_kernel, spans), in_specs=[pl.Block...  2.23 us
    pallas_call x1, Pallas kernels, pack(): pl.pallas_call(functools.partial(pack_kernel, head_count - 1), in_specs=[...  2.22 us
    pallas_call x1, Pallas kernels, pack(): pl.pallas_call(first_kernel, in_specs=[in_hbm] * 4, out_specs=pl.BlockSpe...  1.55 us
    pallas_call x1, Pallas kernels, early_table(): pl.pallas_call(functools.partial(early_kernel, sides), in_specs=in_vmem(l...  1.45 us
  transfers between devices with their start and end apart: 16, of which 8 were waited for; matrix products, arithmetic and copies ran while one was open for 1% of the time, Pallas kernels for 11%

profile of v6, /device:TPU:0, one launch (start us, length us, event | category | flops | bytes accessed | tf_op | source)
XLA Modules:
  0.0 64.5 jit_solution(14451528487218277408)
XLA Ops:
  0.6 1.5 %pack_first.1.refs_4_ = bf16[4,128,128]{2,1,0:T(8,128)(2,1)} custom-call(bf16[1,128,1024]{2,1,0:T(8,128)(2,1)} %refs_0_.1, bf16[1,128,1024]{2,1,0:T(8,128)(2,1)} %refs_1_.1, bf16[1,128,1024]{2,1,0:T(8,128)(2,1)} %refs_2_.1, bf16[1,128,1024]{2,1,0:T(8,128)(2,1)} %refs_3_.1), custom_call_target="tpu_custom_call" | custom-call | bytes 262144 | tf_op jit(solution)/shard_map/pack_first/pallas_call | solution.py:299
  2.2 4.1 %collective-permute-start = (bf16[4,128,128]{2,1,0:T(8,128)(2,1)}, bf16[4,128,128]{2,1,0:T(8,128)(2,1)S(1)}, u32[]{:S(2)}, u32[]{:S(2)}) collective-permute-start(bf16[4,128,128]{2,1,0:T(8,128)(2,1)} %pack_first.1.refs_4_), channel_id=1, source_target_pairs={{0,16},{4,20},{8,24},{12,28},{16,0},{20,4},{24,8},{28,12},{1,17},{... | collective-permute-start | bytes 393224 | tf_op jit(solution)/shard_map/ppermute | solution.py:701
  6.3 2.2 %pack_heads.1 = (bf16[4,128,128]{2,1,0:T(8,128)(2,1)}, bf16[4,128,128]{2,1,0:T(8,128)(2,1)}, bf16[4,128,128]{2,1,0:T(8,128)(2,1)}, bf16[4,128,128]{2,1,0:T(8,128...) custom-call(bf16[1,128,1024]{2,1,0:T(8,128)(2,1)} %refs_0_.1, ...), custom_call_target="tpu_custom_call" | custom-call | flops 2000000000 | bytes 2097152 | tf_op jit(solution)/shard_map/pack_heads/pallas_call | solution.py:309
  8.6 1.6 %collective-permute-start.1 = (bf16[4,128,128]{2,1,0:T(8,128)(2,1)}, bf16[4,128,128]{2,1,0:T(8,128)(2,1)S(1)}, u32[]{:S(2)}, u32[]{:S(2)}) collective-permute-start(bf16[4,128,128]{2,1,0:T(8,128)(2,1)} %get-tuple-element.28), channel_id=1, source_target_pairs={{0,8},{4,12},{8,0},{12,4},{16,24},{20,28},{24,16},{28,20},{1,9},{5... | collective-permute-start | bytes 393224 | tf_op jit(solution)/shard_map/ppermute | solution.py:701
  10.2 1.3 %collective-permute-start.2 = (bf16[4,128,128]{2,1,0:T(8,128)(2,1)}, bf16[4,128,128]{2,1,0:T(8,128)(2,1)S(1)}, u32[]{:S(2)}, u32[]{:S(2)}) collective-permute-start(bf16[4,128,128]{2,1,0:T(8,128)(2,1)} %get-tuple-element.29), channel_id=1, source_target_pairs={{0,20},{4,16},{8,28},{12,24},{16,4},{20,0},{24,12},{28,8},{1,21},{... | collective-permute-start | bytes 393224 | tf_op jit(solution)/shard_map/ppermute | solution.py:701
  11.6 3.8 %collective-permute-start.4 = (bf16[4,128,128]{2,1,0:T(8,128)(2,1)}, bf16[4,128,128]{2,1,0:T(8,128)(2,1)S(1)}, u32[]{:S(2)}, u32[]{:S(2)}) collective-permute-start(bf16[4,128,128]{2,1,0:T(8,128)(2,1)} %get-tuple-element.31), channel_id=1, source_target_pairs={{0,24},{4,28},{8,16},{12,20},{16,8},{20,12},{24,0},{28,4},{1,25},{... | collective-permute-start | bytes 393224 | tf_op jit(solution)/shard_map/ppermute | solution.py:701
  15.5 2.8 %collective-permute-start.5 = (bf16[4,128,128]{2,1,0:T(8,128)(2,1)}, bf16[4,128,128]{2,1,0:T(8,128)(2,1)S(1)}, u32[]{:S(2)}, u32[]{:S(2)}) collective-permute-start(bf16[4,128,128]{2,1,0:T(8,128)(2,1)} %get-tuple-element.32), channel_id=1, source_target_pairs={{0,28},{4,24},{8,20},{12,16},{16,12},{20,8},{24,4},{28,0},{1,29},{... | collective-permute-start | bytes 393224 | tf_op jit(solution)/shard_map/ppermute | solution.py:701
  18.3 0.7 %collective-permute-start.6 = (bf16[4,128,128]{2,1,0:T(8,128)(2,1)}, bf16[4,128,128]{2,1,0:T(8,128)(2,1)S(1)}, u32[]{:S(2)}, u32[]{:S(2)}) collective-permute-start(bf16[4,128,128]{2,1,0:T(8,128)(2,1)} %get-tuple-element.33), channel_id=1, source_target_pairs={{0,4},{4,0},{8,12},{12,8},{16,20},{20,16},{24,28},{28,24},{1,5},{5... | collective-permute-start | bytes 393224 | tf_op jit(solution)/shard_map/ppermute | solution.py:701
  19.2 0.9 %copy-done.3 = bf16[4,128,128]{2,1,0:T(8,128)(2,1)S(1)} copy-done((bf16[4,128,128]{2,1,0:T(8,128)(2,1)S(1)}, bf16[4,128,128]{2,1,0:T(8,128)(2,1)}, u32[]{:S(2)}) %copy-start.3) | copy-done | bytes 131096
  20.1 0.8 %choose_blocks.1 = (bf16[4,64,128]{2,1,0:T(8,128)(2,1)S(1)}, bf16[4,128,128]{2,1,0:T(8,128)(2,1)S(1)}) custom-call(s32[3]{0:T(128)S(1)} %pad_add_fusion.place_ref, bf16[4,64,1024]{2,1,0:T(8,128)(2,1)S(1)} %copy-done.1, bf16[4,64,1024]{2,1,0:T(8,128)(2,1)S(1)} %copy-done.2, bf16[4,128,128]{2,1,0:T(8,128)(2,1)S(1)} %copy-done.3), custom_call_target="tpu_custom_call" | custom-call | bytes 131072 | tf_op jit(solution)/shard_map/choose_blocks/pallas_call | solution.py:350
  20.9 0.5 collective-permute-done.2.refs_3_
  21.4 6.3 %collective-permute-done.3.refs_4_ = bf16[4,128,128]{2,1,0:T(8,128)(2,1)S(1)} collective-permute-done((bf16[4,128,128]{2,1,0:T(8,128)(2,1)}, bf16[4,128,128]{2,1,0:T(8,128)(2,1)S(1)}, u32[]{:S(2)}, u32[]{:S(2)}) %collective-permute-start.3) | collective-permute-done | bytes 131104 | tf_op jit(solution)/shard_map/ppermute | solution.py:701
  28.1 2.2 %scores.1 = (bf16[1024,128]{1,0:T(8,128)(2,1)S(1)}, bf16[1152,128]{1,0:T(8,128)(2,1)S(1)}, bf16[1024,128]{1,0:T(8,128)(2,1)S(1)}, bf16[8,512,128]{2,1,0:T(8,128)...) custom-call(s32[3]{0:T(128)S(1)} %pad_add_fusion.place_ref, ...), custom_call_target="tpu_custom_call" | custom-call | flops 268435456 | bytes 1048576 | tf_op jit(solution)/shard_map/scores/pallas_call | solution.py:501
  30.4 2.4 %grads.1 = bf16[8,3,128,128]{3,2,1,0:T(8,128)(2,1)} custom-call(s32[48]{0:T(128)S(1)} %min.12.rand_ref, bf16[4,64,128]{2,1,0:T(8,128)(2,1)S(1)} %get-tuple-element.34.refs_8_.g_ref, bf16[1024,128]{1,0:T(8,128)(2,1)S(1)} %get-tuple-element.37.q_all, bf16[1152,128]{1,0:T(8,128)(2,1)S(1)} %get-tuple-element.38.k_all, ...), custom_call_target="tpu_custom_call" | custom-call | flops 402653184 | bytes 1048576 | tf_op jit(solution)/shard_map/grads/pallas_call | solution.py:590
  32.8 2.8 %collective-permute-start.10 = (bf16[256,128]{1,0:T(8,128)(2,1)S(1)}, bf16[256,128]{1,0:T(8,128)(2,1)S(1)}, u32[]{:S(2)}, u32[]{:S(2)}) collective-permute-start(bf16[256,128]{1,0:T(8,128)(2,1)S(1)} %add_convert_fusion.1), channel_id=1, source_target_pairs={{0,24},{4,28},{8,16},{12,20},{16,8},{20,12},{24,0},{28,4},{1,25},{... | collective-permute-start | bytes 196616 | tf_op jit(solution)/shard_map/ppermute | solution.py:701
  35.6 2.6 %collective-permute-start.9 = (bf16[256,128]{1,0:T(8,128)(2,1)S(1)}, bf16[256,128]{1,0:T(8,128)(2,1)S(1)}, u32[]{:S(2)}, u32[]{:S(2)}) collective-permute-start(bf16[256,128]{1,0:T(8,128)(2,1)S(1)} %add_convert_fusion.1), channel_id=1, source_target_pairs={{0,16},{4,20},{8,24},{12,28},{16,0},{20,4},{24,8},{28,12},{1,17},{... | collective-permute-start | bytes 196616 | tf_op jit(solution)/shard_map/ppermute | solution.py:701
  38.2 0.5 collective-permute-start.8
  38.7 4.2 %all-to-all-start = ((bf16[8,3,128,128]{3,2,1,0:T(8,128)(2,1)}), bf16[8,3,128,128]{3,2,1,0:T(8,128)(2,1)S(1)}, u32[]{:S(2)}, u32[]{:S(2)}) async-start(bf16[8,3,128,128]{3,2,1,0:T(8,128)(2,1)} %grads.1), calls=%async_computation | async-start | bytes 1572864 | tf_op jit(solution)/shard_map/all_to_all | solution.py:719
  42.9 0.5 collective-permute-done.9
  43.7 1.6 %collective-permute-start.11 = (bf16[4,256,128]{2,1,0:T(8,128)(2,1)S(1)}, bf16[4,256,128]{2,1,0:T(8,128)(2,1)S(1)}, u32[]{:S(2)}, u32[]{:S(2)}) collective-permute-start(bf16[4,256,128]{2,1,0:T(8,128)(2,1)S(1)} %pad_maximum_fusion), channel_id=1, source_target_pairs={{0,2},{1,3},{2,0},{3,1},{4,6},{5,7},{6,4},{7,5},{8,10},{9,11},{10,... | collective-permute-start | bytes 786440 | tf_op jit(solution)/shard_map/ppermute | solution.py:701
  45.3 6.7 %collective-permute-done.11 = bf16[4,256,128]{2,1,0:T(8,128)(2,1)S(1)} collective-permute-done((bf16[4,256,128]{2,1,0:T(8,128)(2,1)S(1)}, bf16[4,256,128]{2,1,0:T(8,128)(2,1)S(1)}, u32[]{:S(2)}, u32[]{:S(2)}) %collective-permute-start.11) | collective-permute-done | bytes 262176 | tf_op jit(solution)/shard_map/ppermute | solution.py:701
  52.5 9.0 %collective-permute-done.12.refs_0_ = bf16[4,256,128]{2,1,0:T(8,128)(2,1)S(1)} collective-permute-done((bf16[4,256,128]{2,1,0:T(8,128)(2,1)S(1)}, bf16[4,256,128]{2,1,0:T(8,128)(2,1)S(1)}, u32[]{:S(2)}, u32[]{:S(2)}) %collective-permute-start.12) | collective-permute-done | bytes 262176 | tf_op jit(solution)/shard_map/ppermute | solution.py:701
  61.5 1.5 %early_table.1.refs_3_ = f32[2,256,1024]{2,1,0:T(8,128)} custom-call(bf16[4,256,128]{2,1,0:T(8,128)(2,1)S(1)} %add_convert_fusion.refs_0_, bf16[4,256,128]{2,1,0:T(8,128)(2,1)S(1)} %collective-permute-done.14.refs_1_), custom_call_target="tpu_custom_call" | custom-call | flops 5000000000 | bytes 2097152 | tf_op jit(solution)/shard_map/early_table/pallas_call | solution.py:625
  63.1 1.4 %finish.1 = (bf16[1,128,1024]{2,1,0:T(8,128)(2,1)}, bf16[1,128,1024]{2,1,0:T(8,128)(2,1)}, bf16[1,128,1024]{2,1,0:T(8,128)(2,1)}, f32[2,256,1024]{2,1,0:T(8,128)}) custom-call(bf16[4,256,128]{2,1,0:T(8,128)(2,1)S(1)} %collective-permute-done.12.refs_0_, bf16[4,256,128]{2,1,0:T(8,128)(2,1)S(1)} %collective-permute-done.13.refs_1_, ...), custom_call_target="tpu_custom_call", output_to_operand_aliasing={{3}: (3, {})} | custom-call | bytes 2097152 | tf_op jit(solution)/shard_map/finish/pallas_call | solution.py:678
  (33 shorter events, 1.8 us)
Async XLA Ops:
  0.6 14.8 %copy-start = (s32[8,16,3]{1,0,2:T(8,128)S(1)}, s32[8,16,3]{1,0,2:T(8,128)}, u32[]{:S(2)}) copy-start(s32[8,16,3]{1,0,2:T(8,128)} %param.15) | copy-start | bytes 4612
  2.2 16.9 %copy-start.4 = (s32[1,2]{1,0:T(1,128)S(1)}, s32[1,2]{1,0:T(1,128)}, u32[]{:S(2)}) copy-start(s32[1,2]{1,0:T(1,128)} %param.14) | copy-start | bytes 28
  2.2 17.0 %copy-start.1 = (bf16[4,64,1024]{2,1,0:T(8,128)(2,1)S(1)}, bf16[4,64,1024]{2,1,0:T(8,128)(2,1)}, u32[]{:S(2)}) copy-start(bf16[4,64,1024]{2,1,0:T(8,128)(2,1)} %gk_ref.1) | copy-start | bytes 1572868
  2.2 17.0 %copy-start.2 = (bf16[4,64,1024]{2,1,0:T(8,128)(2,1)S(1)}, bf16[4,64,1024]{2,1,0:T(8,128)(2,1)}, u32[]{:S(2)}) copy-start(bf16[4,64,1024]{2,1,0:T(8,128)(2,1)} %gv_ref.1) | copy-start | bytes 1572868
  2.2 13.2 %collective-permute-start = (bf16[4,128,128]{2,1,0:T(8,128)(2,1)}, bf16[4,128,128]{2,1,0:T(8,128)(2,1)S(1)}, u32[]{:S(2)}, u32[]{:S(2)}) collective-permute-start(bf16[4,128,128]{2,1,0:T(8,128)(2,1)} %pack_first.1.refs_4_), channel_id=1, source_target_pairs={{0,16},{4,20},{8,24},{12,28},{16,0},{20,4},{24,8},{28,12},{1,17},{... | collective-permute-start | bytes 393224 | tf_op jit(solution)/shard_map/ppermute | solution.py:701
  8.6 9.7 %collective-permute-start.1 = (bf16[4,128,128]{2,1,0:T(8,128)(2,1)}, bf16[4,128,128]{2,1,0:T(8,128)(2,1)S(1)}, u32[]{:S(2)}, u32[]{:S(2)}) collective-permute-start(bf16[4,128,128]{2,1,0:T(8,128)(2,1)} %get-tuple-element.28), channel_id=1, source_target_pairs={{0,8},{4,12},{8,0},{12,4},{16,24},{20,28},{24,16},{28,20},{1,9},{5... | collective-permute-start | bytes 393224 | tf_op jit(solution)/shard_map/ppermute | solution.py:701
  10.2 11.3 %collective-permute-start.2 = (bf16[4,128,128]{2,1,0:T(8,128)(2,1)}, bf16[4,128,128]{2,1,0:T(8,128)(2,1)S(1)}, u32[]{:S(2)}, u32[]{:S(2)}) collective-permute-start(bf16[4,128,128]{2,1,0:T(8,128)(2,1)} %get-tuple-element.29), channel_id=1, source_target_pairs={{0,20},{4,16},{8,28},{12,24},{16,4},{20,0},{24,12},{28,8},{1,21},{... | collective-permute-start | bytes 393224 | tf_op jit(solution)/shard_map/ppermute | solution.py:701
  11.4 16.3 %collective-permute-start.3 = (bf16[4,128,128]{2,1,0:T(8,128)(2,1)}, bf16[4,128,128]{2,1,0:T(8,128)(2,1)S(1)}, u32[]{:S(2)}, u32[]{:S(2)}) collective-permute-start(bf16[4,128,128]{2,1,0:T(8,128)(2,1)} %get-tuple-element.30), channel_id=1, source_target_pairs={{0,12},{4,8},{8,4},{12,0},{16,28},{20,24},{24,20},{28,16},{1,13},{... | collective-permute-start | bytes 393224 | tf_op jit(solution)/shard_map/ppermute | solution.py:701
  11.6 16.1 %collective-permute-start.4 = (bf16[4,128,128]{2,1,0:T(8,128)(2,1)}, bf16[4,128,128]{2,1,0:T(8,128)(2,1)S(1)}, u32[]{:S(2)}, u32[]{:S(2)}) collective-permute-start(bf16[4,128,128]{2,1,0:T(8,128)(2,1)} %get-tuple-element.31), channel_id=1, source_target_pairs={{0,24},{4,28},{8,16},{12,20},{16,8},{20,12},{24,0},{28,4},{1,25},{... | collective-permute-start | bytes 393224 | tf_op jit(solution)/shard_map/ppermute | solution.py:701
  15.5 12.2 %collective-permute-start.5 = (bf16[4,128,128]{2,1,0:T(8,128)(2,1)}, bf16[4,128,128]{2,1,0:T(8,128)(2,1)S(1)}, u32[]{:S(2)}, u32[]{:S(2)}) collective-permute-start(bf16[4,128,128]{2,1,0:T(8,128)(2,1)} %get-tuple-element.32), channel_id=1, source_target_pairs={{0,28},{4,24},{8,20},{12,16},{16,12},{20,8},{24,4},{28,0},{1,29},{... | collective-permute-start | bytes 393224 | tf_op jit(solution)/shard_map/ppermute | solution.py:701
  18.3 9.8 %collective-permute-start.6 = (bf16[4,128,128]{2,1,0:T(8,128)(2,1)}, bf16[4,128,128]{2,1,0:T(8,128)(2,1)S(1)}, u32[]{:S(2)}, u32[]{:S(2)}) collective-permute-start(bf16[4,128,128]{2,1,0:T(8,128)(2,1)} %get-tuple-element.33), channel_id=1, source_target_pairs={{0,4},{4,0},{8,12},{12,8},{16,20},{20,16},{24,28},{28,24},{1,5},{5... | collective-permute-start | bytes 393224 | tf_op jit(solution)/shard_map/ppermute | solution.py:701
  19.2 0.9 %copy-start.3 = (bf16[4,128,128]{2,1,0:T(8,128)(2,1)S(1)}, bf16[4,128,128]{2,1,0:T(8,128)(2,1)}, u32[]{:S(2)}) copy-start(bf16[4,128,128]{2,1,0:T(8,128)(2,1)} %get-tuple-element.26.own_ref) | copy-start | bytes 393220
  30.3 2.5 %collective-permute-start.7 = (bf16[256,128]{1,0:T(8,128)(2,1)S(1)}, bf16[256,128]{1,0:T(8,128)(2,1)S(1)}, u32[]{:S(2)}, u32[]{:S(2)}) collective-permute-start(bf16[256,128]{1,0:T(8,128)(2,1)S(1)} %get-tuple-element.36), channel_id=1, source_target_pairs={{0,1},{1,0},{2,3},{3,2},{4,5},{5,4},{6,7},{7,6},{8,9},{9,8},{10,11... | collective-permute-start | bytes 196616 | tf_op jit(solution)/shard_map/ppermute | solution.py:701
  32.8 10.1 %collective-permute-start.10 = (bf16[256,128]{1,0:T(8,128)(2,1)S(1)}, bf16[256,128]{1,0:T(8,128)(2,1)S(1)}, u32[]{:S(2)}, u32[]{:S(2)}) collective-permute-start(bf16[256,128]{1,0:T(8,128)(2,1)S(1)} %add_convert_fusion.1), channel_id=1, source_target_pairs={{0,24},{4,28},{8,16},{12,20},{16,8},{20,12},{24,0},{28,4},{1,25},{... | collective-permute-start | bytes 196616 | tf_op jit(solution)/shard_map/ppermute | solution.py:701
  35.6 7.8 %collective-permute-start.9 = (bf16[256,128]{1,0:T(8,128)(2,1)S(1)}, bf16[256,128]{1,0:T(8,128)(2,1)S(1)}, u32[]{:S(2)}, u32[]{:S(2)}) collective-permute-start(bf16[256,128]{1,0:T(8,128)(2,1)S(1)} %add_convert_fusion.1), channel_id=1, source_target_pairs={{0,16},{4,20},{8,24},{12,28},{16,0},{20,4},{24,8},{28,12},{1,17},{... | collective-permute-start | bytes 196616 | tf_op jit(solution)/shard_map/ppermute | solution.py:701
  38.2 5.4 %collective-permute-start.8 = (bf16[256,128]{1,0:T(8,128)(2,1)S(1)}, bf16[256,128]{1,0:T(8,128)(2,1)S(1)}, u32[]{:S(2)}, u32[]{:S(2)}) collective-permute-start(bf16[256,128]{1,0:T(8,128)(2,1)S(1)} %add_convert_fusion.1), channel_id=1, source_target_pairs={{0,8},{4,12},{8,0},{12,4},{16,24},{20,28},{24,16},{28,20},{1,9},{5... | collective-permute-start | bytes 196616 | tf_op jit(solution)/shard_map/ppermute | solution.py:701
  38.7 24.4 %all-to-all-start = ((bf16[8,3,128,128]{3,2,1,0:T(8,128)(2,1)}), bf16[8,3,128,128]{3,2,1,0:T(8,128)(2,1)S(1)}, u32[]{:S(2)}, u32[]{:S(2)}) async-start(bf16[8,3,128,128]{3,2,1,0:T(8,128)(2,1)} %grads.1), calls=%async_computation | async-start | bytes 1572864 | tf_op jit(solution)/shard_map/all_to_all | solution.py:719
  43.7 8.3 %collective-permute-start.11 = (bf16[4,256,128]{2,1,0:T(8,128)(2,1)S(1)}, bf16[4,256,128]{2,1,0:T(8,128)(2,1)S(1)}, u32[]{:S(2)}, u32[]{:S(2)}) collective-permute-start(bf16[4,256,128]{2,1,0:T(8,128)(2,1)S(1)} %pad_maximum_fusion), channel_id=1, source_target_pairs={{0,2},{1,3},{2,0},{3,1},{4,6},{5,7},{6,4},{7,5},{8,10},{9,11},{10,... | collective-permute-start | bytes 786440 | tf_op jit(solution)/shard_map/ppermute | solution.py:701
  52.0 9.5 %collective-permute-start.12 = (bf16[4,256,128]{2,1,0:T(8,128)(2,1)S(1)}, bf16[4,256,128]{2,1,0:T(8,128)(2,1)S(1)}, u32[]{:S(2)}, u32[]{:S(2)}) collective-permute-start(bf16[4,256,128]{2,1,0:T(8,128)(2,1)S(1)} %add_convert_fusion.refs_0_), channel_id=1, source_target_pairs={{0,4},{4,0},{8,12},{12,8},{16,20},{20,16},{24,28},{28,24},{1,5},{5... | collective-permute-start | bytes 786440 | tf_op jit(solution)/shard_map/ppermute | solution.py:701
  52.5 9.1 %collective-permute-start.14 = (bf16[4,256,128]{2,1,0:T(8,128)(2,1)S(1)}, bf16[4,256,128]{2,1,0:T(8,128)(2,1)S(1)}, u32[]{:S(2)}, u32[]{:S(2)}) collective-permute-start(bf16[4,256,128]{2,1,0:T(8,128)(2,1)S(1)} %add_convert_fusion.refs_0_), channel_id=1, source_target_pairs={{0,1},{1,0},{2,3},{3,2},{4,5},{5,4},{6,7},{7,6},{8,9},{9,8},{10,11... | collective-permute-start | bytes 786440 | tf_op jit(solution)/shard_map/ppermute | solution.py:701
  61.5 1.5 %collective-permute-start.13 = (bf16[4,256,128]{2,1,0:T(8,128)(2,1)S(1)}, bf16[4,256,128]{2,1,0:T(8,128)(2,1)S(1)}, u32[]{:S(2)}, u32[]{:S(2)}) collective-permute-start(bf16[4,256,128]{2,1,0:T(8,128)(2,1)S(1)} %collective-permute-done.12.refs_0_), channel_id=1, source_target_pairs={{0,1},{1,0},{2,3},{3,2},{4,5},{5,4},{6,7},{7,6},{8,9},{9,8},{10,11... | collective-permute-start | bytes 786440 | tf_op jit(solution)/shard_map/ppermute | solution.py:701

commit v7 on v6

--- a/solution.py
+++ b/solution.py
@@ -639,10 +639,8 @@
     count = len(sides)
     parts, x_ref = refs[:count], refs[count]
     grad_refs, table_ref = refs[count + 2 : count + 5], refs[count + 5]
-    x_held, grad_made, table_made, x_sem, grad_sems, table_sems = refs[count + 6 :]
-    heads, _, _, head_size = x_held.shape
-    load = pltpu.make_async_copy(x_ref, x_held, x_sem)
-    load.start()
+    grad_made, table_made, grad_sems, table_sems = refs[count + 6 :]
+    heads, _, _, head_size = x_ref.shape
     me = lax.axis_index("ctx")
     share = lax.axis_index("dp") % 2
     stores = []
@@ -658,11 +656,10 @@
             )
             store.start()
             stores.append(store)
-    load.wait()
     for place, ref in enumerate(grad_refs):
         for head in range(heads):
             columns = slice(head * head_size, (head + 1) * head_size)
-            grad_made[place, :, columns] = x_held[head, place]
+            grad_made[place, :, columns] = x_ref[head, place]
         store = pltpu.make_async_copy(grad_made.at[place], ref.at[0], grad_sems.at[place])
         store.start()
         stores.append(store)
@@ -677,14 +674,12 @@
     grad = jax.ShapeDtypeStruct((1, rows, heads * head_size), x.dtype)
     return pl.pallas_call(
         functools.partial(finish_kernel, sides),
-        in_specs=in_vmem(len(parts)) + [in_hbm] * 2,
+        in_specs=in_vmem(len(parts) + 1) + [in_hbm],
         out_specs=[in_hbm] * (kinds + 1),
         out_shape=[grad] * kinds + [jax.ShapeDtypeStruct(table.shape, table.dtype)],
         scratch_shapes=[
-            pltpu.VMEM(x.shape, x.dtype),
             pltpu.VMEM((kinds, rows, heads * head_size), x.dtype),
             pltpu.VMEM((blocks,) + parts[0].shape[1:], table.dtype),
-            pltpu.SemaphoreType.DMA,
             pltpu.SemaphoreType.DMA((kinds,)),
             pltpu.SemaphoreType.DMA((blocks,)),
         ],

time: 64.8 us -> 64.7 us (level)
  no operation moved by 1% of the time
where the time goes in v7:
time: 64.7 us; the launch traced here: 64.4 us
  starting transfers between devices  26.7 us (41%)
  waiting for transfers between devices  23.7 us (37%)
  Pallas kernels  12 us (19%)
  local copies, waits for them, and re-layouts  1.11 us (2%)
  between operations  0.78 us (1%)
    ppermute x15, waiting for transfers between devices, flipped(): lax.ppermute(array, axis, [(i, i ^ bits) for i in range(lax.axis_size(axi...  23.7 us
    ppermute x15, starting transfers between devices, flipped(): lax.ppermute(array, axis, [(i, i ^ bits) for i in range(lax.axis_size(axi...  22.5 us
    all_to_all x1, starting transfers between devices, on_heads(): back = lax.all_to_all(sent, 'ctx', 0, 0)  4.21 us
    pallas_call x1, Pallas kernels, grads(): pl.pallas_call(grad_kernel, in_specs=[pl.BlockSpec(memory_space=pltpu.SME...  2.38 us
    pallas_call x1, Pallas kernels, scores(): pl.pallas_call(functools.partial(score_kernel, spans), in_specs=[pl.Block...  2.23 us
    pallas_call x1, Pallas kernels, pack(): pl.pallas_call(functools.partial(pack_kernel, head_count - 1), in_specs=[...  2.22 us
    pallas_call x1, Pallas kernels, pack(): pl.pallas_call(first_kernel, in_specs=[in_hbm] * 4, out_specs=pl.BlockSpe...  1.55 us
    pallas_call x1, Pallas kernels, early_table(): pl.pallas_call(functools.partial(early_kernel, sides), in_specs=in_vmem(l...  1.45 us
  transfers between devices with their start and end apart: 16, of which 8 were waited for; matrix products, arithmetic and copies ran while one was open for 1% of the time, Pallas kernels for 11%

profile of v7, /device:TPU:0, one launch (start us, length us, event | category | flops | bytes accessed | tf_op | source)
XLA Modules:
  0.0 64.4 jit_solution(8311311368219405581)
XLA Ops:
  0.6 1.5 %pack_first.1.refs_4_ = bf16[4,128,128]{2,1,0:T(8,128)(2,1)} custom-call(bf16[1,128,1024]{2,1,0:T(8,128)(2,1)} %refs_0_.1, bf16[1,128,1024]{2,1,0:T(8,128)(2,1)} %refs_1_.1, bf16[1,128,1024]{2,1,0:T(8,128)(2,1)} %refs_2_.1, bf16[1,128,1024]{2,1,0:T(8,128)(2,1)} %refs_3_.1), custom_call_target="tpu_custom_call" | custom-call | bytes 262144 | tf_op jit(solution)/shard_map/pack_first/pallas_call | solution.py:299
  2.2 4.1 %collective-permute-start = (bf16[4,128,128]{2,1,0:T(8,128)(2,1)}, bf16[4,128,128]{2,1,0:T(8,128)(2,1)S(1)}, u32[]{:S(2)}, u32[]{:S(2)}) collective-permute-start(bf16[4,128,128]{2,1,0:T(8,128)(2,1)} %pack_first.1.refs_4_), channel_id=1, source_target_pairs={{0,16},{4,20},{8,24},{12,28},{16,0},{20,4},{24,8},{28,12},{1,17},{... | collective-permute-start | bytes 393224 | tf_op jit(solution)/shard_map/ppermute | solution.py:696
  6.3 2.2 %pack_heads.1 = (bf16[4,128,128]{2,1,0:T(8,128)(2,1)}, bf16[4,128,128]{2,1,0:T(8,128)(2,1)}, bf16[4,128,128]{2,1,0:T(8,128)(2,1)}, bf16[4,128,128]{2,1,0:T(8,128...) custom-call(bf16[1,128,1024]{2,1,0:T(8,128)(2,1)} %refs_0_.1, ...), custom_call_target="tpu_custom_call" | custom-call | flops 2000000000 | bytes 2097152 | tf_op jit(solution)/shard_map/pack_heads/pallas_call | solution.py:309
  8.6 1.6 %collective-permute-start.1 = (bf16[4,128,128]{2,1,0:T(8,128)(2,1)}, bf16[4,128,128]{2,1,0:T(8,128)(2,1)S(1)}, u32[]{:S(2)}, u32[]{:S(2)}) collective-permute-start(bf16[4,128,128]{2,1,0:T(8,128)(2,1)} %get-tuple-element.28), channel_id=1, source_target_pairs={{0,8},{4,12},{8,0},{12,4},{16,24},{20,28},{24,16},{28,20},{1,9},{5... | collective-permute-start | bytes 393224 | tf_op jit(solution)/shard_map/ppermute | solution.py:696
  10.2 1.3 %collective-permute-start.2 = (bf16[4,128,128]{2,1,0:T(8,128)(2,1)}, bf16[4,128,128]{2,1,0:T(8,128)(2,1)S(1)}, u32[]{:S(2)}, u32[]{:S(2)}) collective-permute-start(bf16[4,128,128]{2,1,0:T(8,128)(2,1)} %get-tuple-element.29), channel_id=1, source_target_pairs={{0,20},{4,16},{8,28},{12,24},{16,4},{20,0},{24,12},{28,8},{1,21},{... | collective-permute-start | bytes 393224 | tf_op jit(solution)/shard_map/ppermute | solution.py:696
  11.6 3.8 %collective-permute-start.4 = (bf16[4,128,128]{2,1,0:T(8,128)(2,1)}, bf16[4,128,128]{2,1,0:T(8,128)(2,1)S(1)}, u32[]{:S(2)}, u32[]{:S(2)}) collective-permute-start(bf16[4,128,128]{2,1,0:T(8,128)(2,1)} %get-tuple-element.31), channel_id=1, source_target_pairs={{0,24},{4,28},{8,16},{12,20},{16,8},{20,12},{24,0},{28,4},{1,25},{... | collective-permute-start | bytes 393224 | tf_op jit(solution)/shard_map/ppermute | solution.py:696
  15.5 2.8 %collective-permute-start.5 = (bf16[4,128,128]{2,1,0:T(8,128)(2,1)}, bf16[4,128,128]{2,1,0:T(8,128)(2,1)S(1)}, u32[]{:S(2)}, u32[]{:S(2)}) collective-permute-start(bf16[4,128,128]{2,1,0:T(8,128)(2,1)} %get-tuple-element.32), channel_id=1, source_target_pairs={{0,28},{4,24},{8,20},{12,16},{16,12},{20,8},{24,4},{28,0},{1,29},{... | collective-permute-start | bytes 393224 | tf_op jit(solution)/shard_map/ppermute | solution.py:696
  18.3 0.7 %collective-permute-start.6 = (bf16[4,128,128]{2,1,0:T(8,128)(2,1)}, bf16[4,128,128]{2,1,0:T(8,128)(2,1)S(1)}, u32[]{:S(2)}, u32[]{:S(2)}) collective-permute-start(bf16[4,128,128]{2,1,0:T(8,128)(2,1)} %get-tuple-element.33), channel_id=1, source_target_pairs={{0,4},{4,0},{8,12},{12,8},{16,20},{20,16},{24,28},{28,24},{1,5},{5... | collective-permute-start | bytes 393224 | tf_op jit(solution)/shard_map/ppermute | solution.py:696
  19.2 0.9 %copy-done.3 = bf16[4,128,128]{2,1,0:T(8,128)(2,1)S(1)} copy-done((bf16[4,128,128]{2,1,0:T(8,128)(2,1)S(1)}, bf16[4,128,128]{2,1,0:T(8,128)(2,1)}, u32[]{:S(2)}) %copy-start.3) | copy-done | bytes 131096
  20.1 0.8 %choose_blocks.1 = (bf16[4,64,128]{2,1,0:T(8,128)(2,1)S(1)}, bf16[4,128,128]{2,1,0:T(8,128)(2,1)S(1)}) custom-call(s32[3]{0:T(128)S(1)} %pad_add_fusion.place_ref, bf16[4,64,1024]{2,1,0:T(8,128)(2,1)S(1)} %copy-done.1, bf16[4,64,1024]{2,1,0:T(8,128)(2,1)S(1)} %copy-done.2, bf16[4,128,128]{2,1,0:T(8,128)(2,1)S(1)} %copy-done.3), custom_call_target="tpu_custom_call" | custom-call | bytes 131072 | tf_op jit(solution)/shard_map/choose_blocks/pallas_call | solution.py:350
  20.9 0.5 collective-permute-done.2.refs_3_
  21.4 6.3 %collective-permute-done.3.refs_4_ = bf16[4,128,128]{2,1,0:T(8,128)(2,1)S(1)} collective-permute-done((bf16[4,128,128]{2,1,0:T(8,128)(2,1)}, bf16[4,128,128]{2,1,0:T(8,128)(2,1)S(1)}, u32[]{:S(2)}, u32[]{:S(2)}) %collective-permute-start.3) | collective-permute-done | bytes 131104 | tf_op jit(solution)/shard_map/ppermute | solution.py:696
  28.1 2.2 %scores.1 = (bf16[1024,128]{1,0:T(8,128)(2,1)S(1)}, bf16[1152,128]{1,0:T(8,128)(2,1)S(1)}, bf16[1024,128]{1,0:T(8,128)(2,1)S(1)}, bf16[8,512,128]{2,1,0:T(8,128)...) custom-call(s32[3]{0:T(128)S(1)} %pad_add_fusion.place_ref, ...), custom_call_target="tpu_custom_call" | custom-call | flops 268435456 | bytes 1048576 | tf_op jit(solution)/shard_map/scores/pallas_call | solution.py:501
  30.4 2.4 %grads.1 = bf16[8,3,128,128]{3,2,1,0:T(8,128)(2,1)} custom-call(s32[48]{0:T(128)S(1)} %min.12.rand_ref, bf16[4,64,128]{2,1,0:T(8,128)(2,1)S(1)} %get-tuple-element.34.refs_8_.g_ref, bf16[1024,128]{1,0:T(8,128)(2,1)S(1)} %get-tuple-element.37.q_all, bf16[1152,128]{1,0:T(8,128)(2,1)S(1)} %get-tuple-element.38.k_all, ...), custom_call_target="tpu_custom_call" | custom-call | flops 402653184 | bytes 1048576 | tf_op jit(solution)/shard_map/grads/pallas_call | solution.py:590
  32.8 2.8 %collective-permute-start.10 = (bf16[256,128]{1,0:T(8,128)(2,1)S(1)}, bf16[256,128]{1,0:T(8,128)(2,1)S(1)}, u32[]{:S(2)}, u32[]{:S(2)}) collective-permute-start(bf16[256,128]{1,0:T(8,128)(2,1)S(1)} %add_convert_fusion.1), channel_id=1, source_target_pairs={{0,24},{4,28},{8,16},{12,20},{16,8},{20,12},{24,0},{28,4},{1,25},{... | collective-permute-start | bytes 196616 | tf_op jit(solution)/shard_map/ppermute | solution.py:696
  35.6 2.6 %collective-permute-start.9 = (bf16[256,128]{1,0:T(8,128)(2,1)S(1)}, bf16[256,128]{1,0:T(8,128)(2,1)S(1)}, u32[]{:S(2)}, u32[]{:S(2)}) collective-permute-start(bf16[256,128]{1,0:T(8,128)(2,1)S(1)} %add_convert_fusion.1), channel_id=1, source_target_pairs={{0,16},{4,20},{8,24},{12,28},{16,0},{20,4},{24,8},{28,12},{1,17},{... | collective-permute-start | bytes 196616 | tf_op jit(solution)/shard_map/ppermute | solution.py:696
  38.2 0.5 collective-permute-start.8
  38.7 4.2 %all-to-all-start = ((bf16[8,3,128,128]{3,2,1,0:T(8,128)(2,1)}), bf16[8,3,128,128]{3,2,1,0:T(8,128)(2,1)S(1)}, u32[]{:S(2)}, u32[]{:S(2)}) async-start(bf16[8,3,128,128]{3,2,1,0:T(8,128)(2,1)} %grads.1), calls=%async_computation | async-start | bytes 1572864 | tf_op jit(solution)/shard_map/all_to_all | solution.py:714
  42.9 0.5 collective-permute-done.9
  43.7 1.6 %collective-permute-start.11 = (bf16[4,256,128]{2,1,0:T(8,128)(2,1)S(1)}, bf16[4,256,128]{2,1,0:T(8,128)(2,1)S(1)}, u32[]{:S(2)}, u32[]{:S(2)}) collective-permute-start(bf16[4,256,128]{2,1,0:T(8,128)(2,1)S(1)} %pad_maximum_fusion), channel_id=1, source_target_pairs={{0,2},{1,3},{2,0},{3,1},{4,6},{5,7},{6,4},{7,5},{8,10},{9,11},{10,... | collective-permute-start | bytes 786440 | tf_op jit(solution)/shard_map/ppermute | solution.py:696
  45.3 6.7 %collective-permute-done.11 = bf16[4,256,128]{2,1,0:T(8,128)(2,1)S(1)} collective-permute-done((bf16[4,256,128]{2,1,0:T(8,128)(2,1)S(1)}, bf16[4,256,128]{2,1,0:T(8,128)(2,1)S(1)}, u32[]{:S(2)}, u32[]{:S(2)}) %collective-permute-start.11) | collective-permute-done | bytes 262176 | tf_op jit(solution)/shard_map/ppermute | solution.py:696
  52.5 9.0 %collective-permute-done.12.refs_0_ = bf16[4,256,128]{2,1,0:T(8,128)(2,1)S(1)} collective-permute-done((bf16[4,256,128]{2,1,0:T(8,128)(2,1)S(1)}, bf16[4,256,128]{2,1,0:T(8,128)(2,1)S(1)}, u32[]{:S(2)}, u32[]{:S(2)}) %collective-permute-start.12) | collective-permute-done | bytes 262176 | tf_op jit(solution)/shard_map/ppermute | solution.py:696
  61.5 1.5 %early_table.1.refs_3_ = f32[2,256,1024]{2,1,0:T(8,128)} custom-call(bf16[4,256,128]{2,1,0:T(8,128)(2,1)S(1)} %add_convert_fusion.refs_0_, bf16[4,256,128]{2,1,0:T(8,128)(2,1)S(1)} %collective-permute-done.14.refs_1_), custom_call_target="tpu_custom_call" | custom-call | flops 5000000000 | bytes 2097152 | tf_op jit(solution)/shard_map/early_table/pallas_call | solution.py:625
  63.1 1.3 %finish.1 = (bf16[1,128,1024]{2,1,0:T(8,128)(2,1)}, bf16[1,128,1024]{2,1,0:T(8,128)(2,1)}, bf16[1,128,1024]{2,1,0:T(8,128)(2,1)}, f32[2,256,1024]{2,1,0:T(8,128)}) custom-call(bf16[4,256,128]{2,1,0:T(8,128)(2,1)S(1)} %collective-permute-done.12.refs_0_, bf16[4,256,128]{2,1,0:T(8,128)(2,1)S(1)} %collective-permute-done.13.refs_1_, ...), custom_call_target="tpu_custom_call", output_to_operand_aliasing={{3}: (3, {})} | custom-call | bytes 2097152 | tf_op jit(solution)/shard_map/finish/pallas_call | solution.py:675
  (33 shorter events, 1.8 us)
Async XLA Ops:
  0.6 14.8 %copy-start = (s32[8,16,3]{1,0,2:T(8,128)S(1)}, s32[8,16,3]{1,0,2:T(8,128)}, u32[]{:S(2)}) copy-start(s32[8,16,3]{1,0,2:T(8,128)} %param.15) | copy-start | bytes 4612
  2.2 16.9 %copy-start.4 = (s32[1,2]{1,0:T(1,128)S(1)}, s32[1,2]{1,0:T(1,128)}, u32[]{:S(2)}) copy-start(s32[1,2]{1,0:T(1,128)} %param.14) | copy-start | bytes 28
  2.2 17.0 %copy-start.1 = (bf16[4,64,1024]{2,1,0:T(8,128)(2,1)S(1)}, bf16[4,64,1024]{2,1,0:T(8,128)(2,1)}, u32[]{:S(2)}) copy-start(bf16[4,64,1024]{2,1,0:T(8,128)(2,1)} %gk_ref.1) | copy-start | bytes 1572868
  2.2 17.0 %copy-start.2 = (bf16[4,64,1024]{2,1,0:T(8,128)(2,1)S(1)}, bf16[4,64,1024]{2,1,0:T(8,128)(2,1)}, u32[]{:S(2)}) copy-start(bf16[4,64,1024]{2,1,0:T(8,128)(2,1)} %gv_ref.1) | copy-start | bytes 1572868
  2.2 13.2 %collective-permute-start = (bf16[4,128,128]{2,1,0:T(8,128)(2,1)}, bf16[4,128,128]{2,1,0:T(8,128)(2,1)S(1)}, u32[]{:S(2)}, u32[]{:S(2)}) collective-permute-start(bf16[4,128,128]{2,1,0:T(8,128)(2,1)} %pack_first.1.refs_4_), channel_id=1, source_target_pairs={{0,16},{4,20},{8,24},{12,28},{16,0},{20,4},{24,8},{28,12},{1,17},{... | collective-permute-start | bytes 393224 | tf_op jit(solution)/shard_map/ppermute | solution.py:696
  8.6 9.7 %collective-permute-start.1 = (bf16[4,128,128]{2,1,0:T(8,128)(2,1)}, bf16[4,128,128]{2,1,0:T(8,128)(2,1)S(1)}, u32[]{:S(2)}, u32[]{:S(2)}) collective-permute-start(bf16[4,128,128]{2,1,0:T(8,128)(2,1)} %get-tuple-element.28), channel_id=1, source_target_pairs={{0,8},{4,12},{8,0},{12,4},{16,24},{20,28},{24,16},{28,20},{1,9},{5... | collective-permute-start | bytes 393224 | tf_op jit(solution)/shard_map/ppermute | solution.py:696
  10.2 11.3 %collective-permute-start.2 = (bf16[4,128,128]{2,1,0:T(8,128)(2,1)}, bf16[4,128,128]{2,1,0:T(8,128)(2,1)S(1)}, u32[]{:S(2)}, u32[]{:S(2)}) collective-permute-start(bf16[4,128,128]{2,1,0:T(8,128)(2,1)} %get-tuple-element.29), channel_id=1, source_target_pairs={{0,20},{4,16},{8,28},{12,24},{16,4},{20,0},{24,12},{28,8},{1,21},{... | collective-permute-start | bytes 393224 | tf_op jit(solution)/shard_map/ppermute | solution.py:696
  11.4 16.3 %collective-permute-start.3 = (bf16[4,128,128]{2,1,0:T(8,128)(2,1)}, bf16[4,128,128]{2,1,0:T(8,128)(2,1)S(1)}, u32[]{:S(2)}, u32[]{:S(2)}) collective-permute-start(bf16[4,128,128]{2,1,0:T(8,128)(2,1)} %get-tuple-element.30), channel_id=1, source_target_pairs={{0,12},{4,8},{8,4},{12,0},{16,28},{20,24},{24,20},{28,16},{1,13},{... | collective-permute-start | bytes 393224 | tf_op jit(solution)/shard_map/ppermute | solution.py:696
  11.6 16.1 %collective-permute-start.4 = (bf16[4,128,128]{2,1,0:T(8,128)(2,1)}, bf16[4,128,128]{2,1,0:T(8,128)(2,1)S(1)}, u32[]{:S(2)}, u32[]{:S(2)}) collective-permute-start(bf16[4,128,128]{2,1,0:T(8,128)(2,1)} %get-tuple-element.31), channel_id=1, source_target_pairs={{0,24},{4,28},{8,16},{12,20},{16,8},{20,12},{24,0},{28,4},{1,25},{... | collective-permute-start | bytes 393224 | tf_op jit(solution)/shard_map/ppermute | solution.py:696
  15.5 12.2 %collective-permute-start.5 = (bf16[4,128,128]{2,1,0:T(8,128)(2,1)}, bf16[4,128,128]{2,1,0:T(8,128)(2,1)S(1)}, u32[]{:S(2)}, u32[]{:S(2)}) collective-permute-start(bf16[4,128,128]{2,1,0:T(8,128)(2,1)} %get-tuple-element.32), channel_id=1, source_target_pairs={{0,28},{4,24},{8,20},{12,16},{16,12},{20,8},{24,4},{28,0},{1,29},{... | collective-permute-start | bytes 393224 | tf_op jit(solution)/shard_map/ppermute | solution.py:696
  18.3 9.8 %collective-permute-start.6 = (bf16[4,128,128]{2,1,0:T(8,128)(2,1)}, bf16[4,128,128]{2,1,0:T(8,128)(2,1)S(1)}, u32[]{:S(2)}, u32[]{:S(2)}) collective-permute-start(bf16[4,128,128]{2,1,0:T(8,128)(2,1)} %get-tuple-element.33), channel_id=1, source_target_pairs={{0,4},{4,0},{8,12},{12,8},{16,20},{20,16},{24,28},{28,24},{1,5},{5... | collective-permute-start | bytes 393224 | tf_op jit(solution)/shard_map/ppermute | solution.py:696
  19.2 0.9 %copy-start.3 = (bf16[4,128,128]{2,1,0:T(8,128)(2,1)S(1)}, bf16[4,128,128]{2,1,0:T(8,128)(2,1)}, u32[]{:S(2)}) copy-start(bf16[4,128,128]{2,1,0:T(8,128)(2,1)} %get-tuple-element.26.own_ref) | copy-start | bytes 393220
  30.3 2.5 %collective-permute-start.7 = (bf16[256,128]{1,0:T(8,128)(2,1)S(1)}, bf16[256,128]{1,0:T(8,128)(2,1)S(1)}, u32[]{:S(2)}, u32[]{:S(2)}) collective-permute-start(bf16[256,128]{1,0:T(8,128)(2,1)S(1)} %get-tuple-element.36), channel_id=1, source_target_pairs={{0,1},{1,0},{2,3},{3,2},{4,5},{5,4},{6,7},{7,6},{8,9},{9,8},{10,11... | collective-permute-start | bytes 196616 | tf_op jit(solution)/shard_map/ppermute | solution.py:696
  32.8 10.1 %collective-permute-start.10 = (bf16[256,128]{1,0:T(8,128)(2,1)S(1)}, bf16[256,128]{1,0:T(8,128)(2,1)S(1)}, u32[]{:S(2)}, u32[]{:S(2)}) collective-permute-start(bf16[256,128]{1,0:T(8,128)(2,1)S(1)} %add_convert_fusion.1), channel_id=1, source_target_pairs={{0,24},{4,28},{8,16},{12,20},{16,8},{20,12},{24,0},{28,4},{1,25},{... | collective-permute-start | bytes 196616 | tf_op jit(solution)/shard_map/ppermute | solution.py:696
  35.6 7.8 %collective-permute-start.9 = (bf16[256,128]{1,0:T(8,128)(2,1)S(1)}, bf16[256,128]{1,0:T(8,128)(2,1)S(1)}, u32[]{:S(2)}, u32[]{:S(2)}) collective-permute-start(bf16[256,128]{1,0:T(8,128)(2,1)S(1)} %add_convert_fusion.1), channel_id=1, source_target_pairs={{0,16},{4,20},{8,24},{12,28},{16,0},{20,4},{24,8},{28,12},{1,17},{... | collective-permute-start | bytes 196616 | tf_op jit(solution)/shard_map/ppermute | solution.py:696
  38.2 5.5 %collective-permute-start.8 = (bf16[256,128]{1,0:T(8,128)(2,1)S(1)}, bf16[256,128]{1,0:T(8,128)(2,1)S(1)}, u32[]{:S(2)}, u32[]{:S(2)}) collective-permute-start(bf16[256,128]{1,0:T(8,128)(2,1)S(1)} %add_convert_fusion.1), channel_id=1, source_target_pairs={{0,8},{4,12},{8,0},{12,4},{16,24},{20,28},{24,16},{28,20},{1,9},{5... | collective-permute-start | bytes 196616 | tf_op jit(solution)/shard_map/ppermute | solution.py:696
  38.7 24.4 %all-to-all-start = ((bf16[8,3,128,128]{3,2,1,0:T(8,128)(2,1)}), bf16[8,3,128,128]{3,2,1,0:T(8,128)(2,1)S(1)}, u32[]{:S(2)}, u32[]{:S(2)}) async-start(bf16[8,3,128,128]{3,2,1,0:T(8,128)(2,1)} %grads.1), calls=%async_computation | async-start | bytes 1572864 | tf_op jit(solution)/shard_map/all_to_all | solution.py:714
  43.7 8.3 %collective-permute-start.11 = (bf16[4,256,128]{2,1,0:T(8,128)(2,1)S(1)}, bf16[4,256,128]{2,1,0:T(8,128)(2,1)S(1)}, u32[]{:S(2)}, u32[]{:S(2)}) collective-permute-start(bf16[4,256,128]{2,1,0:T(8,128)(2,1)S(1)} %pad_maximum_fusion), channel_id=1, source_target_pairs={{0,2},{1,3},{2,0},{3,1},{4,6},{5,7},{6,4},{7,5},{8,10},{9,11},{10,... | collective-permute-start | bytes 786440 | tf_op jit(solution)/shard_map/ppermute | solution.py:696
  52.0 9.5 %collective-permute-start.12 = (bf16[4,256,128]{2,1,0:T(8,128)(2,1)S(1)}, bf16[4,256,128]{2,1,0:T(8,128)(2,1)S(1)}, u32[]{:S(2)}, u32[]{:S(2)}) collective-permute-start(bf16[4,256,128]{2,1,0:T(8,128)(2,1)S(1)} %add_convert_fusion.refs_0_), channel_id=1, source_target_pairs={{0,4},{4,0},{8,12},{12,8},{16,20},{20,16},{24,28},{28,24},{1,5},{5... | collective-permute-start | bytes 786440 | tf_op jit(solution)/shard_map/ppermute | solution.py:696
  52.5 9.1 %collective-permute-start.14 = (bf16[4,256,128]{2,1,0:T(8,128)(2,1)S(1)}, bf16[4,256,128]{2,1,0:T(8,128)(2,1)S(1)}, u32[]{:S(2)}, u32[]{:S(2)}) collective-permute-start(bf16[4,256,128]{2,1,0:T(8,128)(2,1)S(1)} %add_convert_fusion.refs_0_), channel_id=1, source_target_pairs={{0,1},{1,0},{2,3},{3,2},{4,5},{5,4},{6,7},{7,6},{8,9},{9,8},{10,11... | collective-permute-start | bytes 786440 | tf_op jit(solution)/shard_map/ppermute | solution.py:696
  61.5 1.5 %collective-permute-start.13 = (bf16[4,256,128]{2,1,0:T(8,128)(2,1)S(1)}, bf16[4,256,128]{2,1,0:T(8,128)(2,1)S(1)}, u32[]{:S(2)}, u32[]{:S(2)}) collective-permute-start(bf16[4,256,128]{2,1,0:T(8,128)(2,1)S(1)} %collective-permute-done.12.refs_0_), channel_id=1, source_target_pairs={{0,1},{1,0},{2,3},{3,2},{4,5},{5,4},{6,7},{7,6},{8,9},{9,8},{10,11... | collective-permute-start | bytes 786440 | tf_op jit(solution)/shard_map/ppermute | solution.py:696

commit v8 on v7

--- a/solution.py
+++ b/solution.py
@@ -238,7 +238,7 @@
 PACK_FLOPS = 2 * 10**9
 EARLY_FLOPS = 5 * 10**9
 GROUP = 8
-ORDER = (0, 4, 2, 5, 3, 6, 7, 1)
+ORDER = (0, 4, 3, 5, 2, 6, 7, 1)
 COLUMN = (0, 2, 4, 6)
 
 
@@ -251,19 +251,26 @@
     return [pl.BlockSpec(memory_space=pltpu.VMEM)] * count
 
 
-def first_kernel(q_ref, k_ref, v_ref, o_ref, out_ref, sems):
+def first_kernel(q_ref, k_ref, v_ref, o_ref, out_ref, held, in_sems, out_sems):
     head_size = out_ref.shape[2]
     at = pl.multiple_of((lax.axis_index("ctx") ^ ORDER[1]) * head_size, head_size)
-    copies = [
+    loads = [
         pltpu.make_async_copy(
-            ref.at[0, :, pl.ds(at, head_size)], out_ref.at[place], sems.at[place]
+            ref.at[0, :, pl.ds(at, head_size)], held.at[place], in_sems.at[place]
         )
         for place, ref in enumerate((q_ref, k_ref, v_ref, o_ref))
     ]
-    for copy in copies:
-        copy.start()
-    for copy in copies:
-        copy.wait()
+    stores = [
+        pltpu.make_async_copy(held.at[place], out_ref.at[place], out_sems.at[place])
+        for place in range(len(loads))
+    ]
+    for load in loads:
+        load.start()
+    for load, store in zip(loads, stores):
+        load.wait()
+        store.start()
+    for store in stores:
+        store.wait()
 
 
 def pack_kernel(count, *refs):
@@ -299,9 +306,13 @@
     first = pl.pallas_call(
         first_kernel,
         in_specs=[in_hbm] * 4,
-        out_specs=pl.BlockSpec(memory_space=pltpu.VMEM),
+        out_specs=in_hbm,
         out_shape=shape,
-        scratch_shapes=[pltpu.SemaphoreType.DMA((4,))],
+        scratch_shapes=[
+            pltpu.VMEM(chunk, query.dtype),
+            pltpu.SemaphoreType.DMA((4,)),
+            pltpu.SemaphoreType.DMA((4,)),
+        ],
         compiler_params=pltpu.CompilerParams(vmem_limit_bytes=FIRST_BYTES),
         cost_estimate=pl.CostEstimate(flops=0, bytes_accessed=2 * rows * width, transcendentals=0),
         name="pack_first",

time: 64.7 us -> 64.6 us (level)
  waiting for transfers between devices: 23.7 us -> 22.2 us
  starting transfers between devices: 26.7 us -> 28 us
    ppermute x15, waiting for transfers between devices: 23.7 us -> 21.8 us  [flipped(): lax.ppermute(array, axis, [(i, i ^ bits) for i in range(lax.axis_size(axi...]
    ppermute x15, starting transfers between devices: 22.5 us -> 23.8 us  [flipped(): lax.ppermute(array, axis, [(i, i ^ bits) for i in range(lax.axis_size(axi...]
where the time goes in v8:
time: 64.6 us; the launch traced here: 64.3 us
  starting transfers between devices  28 us (43%)
  waiting for transfers between devices  22.2 us (34%)
  Pallas kernels  11.9 us (18%)
  local copies, waits for them, and re-layouts  1.11 us (2%)
  between operations  0.78 us (1%)
    ppermute x15, starting transfers between devices, flipped(): lax.ppermute(array, axis, [(i, i ^ bits) for i in range(lax.axis_size(axi...  23.8 us
    ppermute x15, waiting for transfers between devices, flipped(): lax.ppermute(array, axis, [(i, i ^ bits) for i in range(lax.axis_size(axi...  21.8 us
    all_to_all x1, starting transfers between devices, on_heads(): back = lax.all_to_all(sent, 'ctx', 0, 0)  4.2 us
    pallas_call x1, Pallas kernels, grads(): pl.pallas_call(grad_kernel, in_specs=[pl.BlockSpec(memory_space=pltpu.SME...  2.38 us
    pallas_call x1, Pallas kernels, scores(): pl.pallas_call(functools.partial(score_kernel, spans), in_specs=[pl.Block...  2.24 us
    pallas_call x1, Pallas kernels, pack(): pl.pallas_call(functools.partial(pack_kernel, head_count - 1), in_specs=[...  2.22 us
    pallas_call x1, Pallas kernels, pack(): pl.pallas_call(first_kernel, in_specs=[in_hbm] * 4, out_specs=in_hbm, out...  1.54 us
    pallas_call x1, Pallas kernels, early_table(): pl.pallas_call(functools.partial(early_kernel, sides), in_specs=in_vmem(l...  1.45 us
  transfers between devices with their start and end apart: 16, of which 8 were waited for; matrix products, arithmetic and copies ran while one was open for 1% of the time, Pallas kernels for 11%

profile of v8, /device:TPU:0, one launch (start us, length us, event | category | flops | bytes accessed | tf_op | source)
XLA Modules:
  0.0 64.3 jit_solution(12480178234033909099)
XLA Ops:
  0.6 1.5 %pack_first.1.refs_4_ = bf16[4,128,128]{2,1,0:T(8,128)(2,1)} custom-call(bf16[1,128,1024]{2,1,0:T(8,128)(2,1)} %refs_0_.1, bf16[1,128,1024]{2,1,0:T(8,128)(2,1)} %refs_1_.1, bf16[1,128,1024]{2,1,0:T(8,128)(2,1)} %refs_2_.1, bf16[1,128,1024]{2,1,0:T(8,128)(2,1)} %refs_3_.1), custom_call_target="tpu_custom_call" | custom-call | bytes 262144 | tf_op jit(solution)/shard_map/pack_first/pallas_call | solution.py:306
  2.2 4.1 %collective-permute-start = (bf16[4,128,128]{2,1,0:T(8,128)(2,1)}, bf16[4,128,128]{2,1,0:T(8,128)(2,1)S(1)}, u32[]{:S(2)}, u32[]{:S(2)}) collective-permute-start(bf16[4,128,128]{2,1,0:T(8,128)(2,1)} %pack_first.1.refs_4_), channel_id=1, source_target_pairs={{0,16},{4,20},{8,24},{12,28},{16,0},{20,4},{24,8},{28,12},{1,17},{... | collective-permute-start | bytes 393224 | tf_op jit(solution)/shard_map/ppermute | solution.py:707
  6.3 2.2 %pack_heads.1 = (bf16[4,128,128]{2,1,0:T(8,128)(2,1)}, bf16[4,128,128]{2,1,0:T(8,128)(2,1)}, bf16[4,128,128]{2,1,0:T(8,128)(2,1)}, bf16[4,128,128]{2,1,0:T(8,128...) custom-call(bf16[1,128,1024]{2,1,0:T(8,128)(2,1)} %refs_0_.1, ...), custom_call_target="tpu_custom_call" | custom-call | flops 2000000000 | bytes 2097152 | tf_op jit(solution)/shard_map/pack_heads/pallas_call | solution.py:320
  8.6 2.5 %collective-permute-start.1 = (bf16[4,128,128]{2,1,0:T(8,128)(2,1)}, bf16[4,128,128]{2,1,0:T(8,128)(2,1)S(1)}, u32[]{:S(2)}, u32[]{:S(2)}) collective-permute-start(bf16[4,128,128]{2,1,0:T(8,128)(2,1)} %get-tuple-element.28), channel_id=1, source_target_pairs={{0,12},{4,8},{8,4},{12,0},{16,28},{20,24},{24,20},{28,16},{1,13},{... | collective-permute-start | bytes 393224 | tf_op jit(solution)/shard_map/ppermute | solution.py:707
  11.6 3.8 %collective-permute-start.4 = (bf16[4,128,128]{2,1,0:T(8,128)(2,1)}, bf16[4,128,128]{2,1,0:T(8,128)(2,1)S(1)}, u32[]{:S(2)}, u32[]{:S(2)}) collective-permute-start(bf16[4,128,128]{2,1,0:T(8,128)(2,1)} %get-tuple-element.31), channel_id=1, source_target_pairs={{0,24},{4,28},{8,16},{12,20},{16,8},{20,12},{24,0},{28,4},{1,25},{... | collective-permute-start | bytes 393224 | tf_op jit(solution)/shard_map/ppermute | solution.py:707
  15.5 2.8 %collective-permute-start.5 = (bf16[4,128,128]{2,1,0:T(8,128)(2,1)}, bf16[4,128,128]{2,1,0:T(8,128)(2,1)S(1)}, u32[]{:S(2)}, u32[]{:S(2)}) collective-permute-start(bf16[4,128,128]{2,1,0:T(8,128)(2,1)} %get-tuple-element.32), channel_id=1, source_target_pairs={{0,28},{4,24},{8,20},{12,16},{16,12},{20,8},{24,4},{28,0},{1,29},{... | collective-permute-start | bytes 393224 | tf_op jit(solution)/shard_map/ppermute | solution.py:707
  18.3 0.5 collective-permute-start.6
  19.0 0.9 %copy-done.3 = bf16[4,128,128]{2,1,0:T(8,128)(2,1)S(1)} copy-done((bf16[4,128,128]{2,1,0:T(8,128)(2,1)S(1)}, bf16[4,128,128]{2,1,0:T(8,128)(2,1)}, u32[]{:S(2)}) %copy-start.3) | copy-done | bytes 131096
  19.9 0.8 %choose_blocks.1 = (bf16[4,64,128]{2,1,0:T(8,128)(2,1)S(1)}, bf16[4,128,128]{2,1,0:T(8,128)(2,1)S(1)}) custom-call(s32[3]{0:T(128)S(1)} %pad_add_fusion.place_ref, bf16[4,64,1024]{2,1,0:T(8,128)(2,1)S(1)} %copy-done.1, bf16[4,64,1024]{2,1,0:T(8,128)(2,1)S(1)} %copy-done.2, bf16[4,128,128]{2,1,0:T(8,128)(2,1)S(1)} %copy-done.3), custom_call_target="tpu_custom_call" | custom-call | bytes 131072 | tf_op jit(solution)/shard_map/choose_blocks/pallas_call | solution.py:361
  20.7 5.8 %collective-permute-done.2.refs_3_ = bf16[4,128,128]{2,1,0:T(8,128)(2,1)S(1)} collective-permute-done((bf16[4,128,128]{2,1,0:T(8,128)(2,1)}, bf16[4,128,128]{2,1,0:T(8,128)(2,1)S(1)}, u32[]{:S(2)}, u32[]{:S(2)}) %collective-permute-start.2) | collective-permute-done | bytes 131104 | tf_op jit(solution)/shard_map/ppermute | solution.py:707
  26.5 0.3 collective-permute-done.3.refs_4_
  27.0 2.2 %scores.1 = (bf16[1024,128]{1,0:T(8,128)(2,1)S(1)}, bf16[1152,128]{1,0:T(8,128)(2,1)S(1)}, bf16[1024,128]{1,0:T(8,128)(2,1)S(1)}, bf16[8,512,128]{2,1,0:T(8,128)...) custom-call(s32[3]{0:T(128)S(1)} %pad_add_fusion.place_ref, ...), custom_call_target="tpu_custom_call" | custom-call | flops 268435456 | bytes 1048576 | tf_op jit(solution)/shard_map/scores/pallas_call | solution.py:512
  29.4 2.4 %grads.1 = bf16[8,3,128,128]{3,2,1,0:T(8,128)(2,1)} custom-call(s32[48]{0:T(128)S(1)} %min.12.rand_ref, bf16[4,64,128]{2,1,0:T(8,128)(2,1)S(1)} %get-tuple-element.34.refs_8_.g_ref, bf16[1024,128]{1,0:T(8,128)(2,1)S(1)} %get-tuple-element.37.q_all, bf16[1152,128]{1,0:T(8,128)(2,1)S(1)} %get-tuple-element.38.k_all, ...), custom_call_target="tpu_custom_call" | custom-call | flops 402653184 | bytes 1048576 | tf_op jit(solution)/shard_map/grads/pallas_call | solution.py:601
  31.8 3.5 %collective-permute-start.10 = (bf16[256,128]{1,0:T(8,128)(2,1)S(1)}, bf16[256,128]{1,0:T(8,128)(2,1)S(1)}, u32[]{:S(2)}, u32[]{:S(2)}) collective-permute-start(bf16[256,128]{1,0:T(8,128)(2,1)S(1)} %add_convert_fusion.1), channel_id=1, source_target_pairs={{0,24},{4,28},{8,16},{12,20},{16,8},{20,12},{24,0},{28,4},{1,25},{... | collective-permute-start | bytes 196616 | tf_op jit(solution)/shard_map/ppermute | solution.py:707
  35.3 3.2 %collective-permute-start.9 = (bf16[256,128]{1,0:T(8,128)(2,1)S(1)}, bf16[256,128]{1,0:T(8,128)(2,1)S(1)}, u32[]{:S(2)}, u32[]{:S(2)}) collective-permute-start(bf16[256,128]{1,0:T(8,128)(2,1)S(1)} %add_convert_fusion.1), channel_id=1, source_target_pairs={{0,16},{4,20},{8,24},{12,28},{16,0},{20,4},{24,8},{28,12},{1,17},{... | collective-permute-start | bytes 196616 | tf_op jit(solution)/shard_map/ppermute | solution.py:707
  38.7 4.2 %all-to-all-start = ((bf16[8,3,128,128]{3,2,1,0:T(8,128)(2,1)}), bf16[8,3,128,128]{3,2,1,0:T(8,128)(2,1)S(1)}, u32[]{:S(2)}, u32[]{:S(2)}) async-start(bf16[8,3,128,128]{3,2,1,0:T(8,128)(2,1)} %grads.1), calls=%async_computation | async-start | bytes 1572864 | tf_op jit(solution)/shard_map/all_to_all | solution.py:725
  42.9 0.8 %collective-permute-done.9 = bf16[256,128]{1,0:T(8,128)(2,1)S(1)} collective-permute-done((bf16[256,128]{1,0:T(8,128)(2,1)S(1)}, bf16[256,128]{1,0:T(8,128)(2,1)S(1)}, u32[]{:S(2)}, u32[]{:S(2)}) %collective-permute-start.9) | collective-permute-done | bytes 65568 | tf_op jit(solution)/shard_map/ppermute | solution.py:707
  43.8 1.6 %collective-permute-start.11 = (bf16[4,256,128]{2,1,0:T(8,128)(2,1)S(1)}, bf16[4,256,128]{2,1,0:T(8,128)(2,1)S(1)}, u32[]{:S(2)}, u32[]{:S(2)}) collective-permute-start(bf16[4,256,128]{2,1,0:T(8,128)(2,1)S(1)} %pad_maximum_fusion), channel_id=1, source_target_pairs={{0,2},{1,3},{2,0},{3,1},{4,6},{5,7},{6,4},{7,5},{8,10},{9,11},{10,... | collective-permute-start | bytes 786440 | tf_op jit(solution)/shard_map/ppermute | solution.py:707
  45.3 6.0 %collective-permute-done.11 = bf16[4,256,128]{2,1,0:T(8,128)(2,1)S(1)} collective-permute-done((bf16[4,256,128]{2,1,0:T(8,128)(2,1)S(1)}, bf16[4,256,128]{2,1,0:T(8,128)(2,1)S(1)}, u32[]{:S(2)}, u32[]{:S(2)}) %collective-permute-start.11) | collective-permute-done | bytes 262176 | tf_op jit(solution)/shard_map/ppermute | solution.py:707
  51.4 1.0 %collective-permute-start.12 = (bf16[4,256,128]{2,1,0:T(8,128)(2,1)S(1)}, bf16[4,256,128]{2,1,0:T(8,128)(2,1)S(1)}, u32[]{:S(2)}, u32[]{:S(2)}) collective-permute-start(bf16[4,256,128]{2,1,0:T(8,128)(2,1)S(1)} %add_convert_fusion.refs_0_), channel_id=1, source_target_pairs={{0,4},{4,0},{8,12},{12,8},{16,20},{20,16},{24,28},{28,24},{1,5},{5... | collective-permute-start | bytes 786440 | tf_op jit(solution)/shard_map/ppermute | solution.py:707
  52.5 8.5 %collective-permute-done.12.refs_0_ = bf16[4,256,128]{2,1,0:T(8,128)(2,1)S(1)} collective-permute-done((bf16[4,256,128]{2,1,0:T(8,128)(2,1)S(1)}, bf16[4,256,128]{2,1,0:T(8,128)(2,1)S(1)}, u32[]{:S(2)}, u32[]{:S(2)}) %collective-permute-start.12) | collective-permute-done | bytes 262176 | tf_op jit(solution)/shard_map/ppermute | solution.py:707
  61.0 1.5 %early_table.1.refs_3_ = f32[2,256,1024]{2,1,0:T(8,128)} custom-call(bf16[4,256,128]{2,1,0:T(8,128)(2,1)S(1)} %add_convert_fusion.refs_0_, bf16[4,256,128]{2,1,0:T(8,128)(2,1)S(1)} %collective-permute-done.14.refs_1_), custom_call_target="tpu_custom_call" | custom-call | flops 5000000000 | bytes 2097152 | tf_op jit(solution)/shard_map/early_table/pallas_call | solution.py:636
  62.5 0.4 all-to-all-done.refs_2_
  62.9 1.3 %finish.1 = (bf16[1,128,1024]{2,1,0:T(8,128)(2,1)}, bf16[1,128,1024]{2,1,0:T(8,128)(2,1)}, bf16[1,128,1024]{2,1,0:T(8,128)(2,1)}, f32[2,256,1024]{2,1,0:T(8,128)}) custom-call(bf16[4,256,128]{2,1,0:T(8,128)(2,1)S(1)} %collective-permute-done.12.refs_0_, bf16[4,256,128]{2,1,0:T(8,128)(2,1)S(1)} %collective-permute-done.13.refs_1_, ...), custom_call_target="tpu_custom_call", output_to_operand_aliasing={{3}: (3, {})} | custom-call | bytes 2097152 | tf_op jit(solution)/shard_map/finish/pallas_call | solution.py:686
  (33 shorter events, 1.4 us)
Async XLA Ops:
  0.6 14.8 %copy-start = (s32[8,16,3]{1,0,2:T(8,128)S(1)}, s32[8,16,3]{1,0,2:T(8,128)}, u32[]{:S(2)}) copy-start(s32[8,16,3]{1,0,2:T(8,128)} %param.15) | copy-start | bytes 4612
  2.2 16.7 %copy-start.4 = (s32[1,2]{1,0:T(1,128)S(1)}, s32[1,2]{1,0:T(1,128)}, u32[]{:S(2)}) copy-start(s32[1,2]{1,0:T(1,128)} %param.14) | copy-start | bytes 28
  2.2 16.8 %copy-start.1 = (bf16[4,64,1024]{2,1,0:T(8,128)(2,1)S(1)}, bf16[4,64,1024]{2,1,0:T(8,128)(2,1)}, u32[]{:S(2)}) copy-start(bf16[4,64,1024]{2,1,0:T(8,128)(2,1)} %gk_ref.1) | copy-start | bytes 1572868
  2.2 16.8 %copy-start.2 = (bf16[4,64,1024]{2,1,0:T(8,128)(2,1)S(1)}, bf16[4,64,1024]{2,1,0:T(8,128)(2,1)}, u32[]{:S(2)}) copy-start(bf16[4,64,1024]{2,1,0:T(8,128)(2,1)} %gv_ref.1) | copy-start | bytes 1572868
  2.2 13.2 %collective-permute-start = (bf16[4,128,128]{2,1,0:T(8,128)(2,1)}, bf16[4,128,128]{2,1,0:T(8,128)(2,1)S(1)}, u32[]{:S(2)}, u32[]{:S(2)}) collective-permute-start(bf16[4,128,128]{2,1,0:T(8,128)(2,1)} %pack_first.1.refs_4_), channel_id=1, source_target_pairs={{0,16},{4,20},{8,24},{12,28},{16,0},{20,4},{24,8},{28,12},{1,17},{... | collective-permute-start | bytes 393224 | tf_op jit(solution)/shard_map/ppermute | solution.py:707
  8.6 9.7 %collective-permute-start.1 = (bf16[4,128,128]{2,1,0:T(8,128)(2,1)}, bf16[4,128,128]{2,1,0:T(8,128)(2,1)S(1)}, u32[]{:S(2)}, u32[]{:S(2)}) collective-permute-start(bf16[4,128,128]{2,1,0:T(8,128)(2,1)} %get-tuple-element.28), channel_id=1, source_target_pairs={{0,12},{4,8},{8,4},{12,0},{16,28},{20,24},{24,20},{28,16},{1,13},{... | collective-permute-start | bytes 393224 | tf_op jit(solution)/shard_map/ppermute | solution.py:707
  11.1 15.4 %collective-permute-start.2 = (bf16[4,128,128]{2,1,0:T(8,128)(2,1)}, bf16[4,128,128]{2,1,0:T(8,128)(2,1)S(1)}, u32[]{:S(2)}, u32[]{:S(2)}) collective-permute-start(bf16[4,128,128]{2,1,0:T(8,128)(2,1)} %get-tuple-element.29), channel_id=1, source_target_pairs={{0,20},{4,16},{8,28},{12,24},{16,4},{20,0},{24,12},{28,8},{1,21},{... | collective-permute-start | bytes 393224 | tf_op jit(solution)/shard_map/ppermute | solution.py:707
  11.4 15.5 %collective-permute-start.3 = (bf16[4,128,128]{2,1,0:T(8,128)(2,1)}, bf16[4,128,128]{2,1,0:T(8,128)(2,1)S(1)}, u32[]{:S(2)}, u32[]{:S(2)}) collective-permute-start(bf16[4,128,128]{2,1,0:T(8,128)(2,1)} %get-tuple-element.30), channel_id=1, source_target_pairs={{0,8},{4,12},{8,0},{12,4},{16,24},{20,28},{24,16},{28,20},{1,9},{5... | collective-permute-start | bytes 393224 | tf_op jit(solution)/shard_map/ppermute | solution.py:707
  11.6 15.3 %collective-permute-start.4 = (bf16[4,128,128]{2,1,0:T(8,128)(2,1)}, bf16[4,128,128]{2,1,0:T(8,128)(2,1)S(1)}, u32[]{:S(2)}, u32[]{:S(2)}) collective-permute-start(bf16[4,128,128]{2,1,0:T(8,128)(2,1)} %get-tuple-element.31), channel_id=1, source_target_pairs={{0,24},{4,28},{8,16},{12,20},{16,8},{20,12},{24,0},{28,4},{1,25},{... | collective-permute-start | bytes 393224 | tf_op jit(solution)/shard_map/ppermute | solution.py:707
  15.5 11.4 %collective-permute-start.5 = (bf16[4,128,128]{2,1,0:T(8,128)(2,1)}, bf16[4,128,128]{2,1,0:T(8,128)(2,1)S(1)}, u32[]{:S(2)}, u32[]{:S(2)}) collective-permute-start(bf16[4,128,128]{2,1,0:T(8,128)(2,1)} %get-tuple-element.32), channel_id=1, source_target_pairs={{0,28},{4,24},{8,20},{12,16},{16,12},{20,8},{24,4},{28,0},{1,29},{... | collective-permute-start | bytes 393224 | tf_op jit(solution)/shard_map/ppermute | solution.py:707
  18.3 8.8 %collective-permute-start.6 = (bf16[4,128,128]{2,1,0:T(8,128)(2,1)}, bf16[4,128,128]{2,1,0:T(8,128)(2,1)S(1)}, u32[]{:S(2)}, u32[]{:S(2)}) collective-permute-start(bf16[4,128,128]{2,1,0:T(8,128)(2,1)} %get-tuple-element.33), channel_id=1, source_target_pairs={{0,4},{4,0},{8,12},{12,8},{16,20},{20,16},{24,28},{28,24},{1,5},{5... | collective-permute-start | bytes 393224 | tf_op jit(solution)/shard_map/ppermute | solution.py:707
  19.0 0.9 %copy-start.3 = (bf16[4,128,128]{2,1,0:T(8,128)(2,1)S(1)}, bf16[4,128,128]{2,1,0:T(8,128)(2,1)}, u32[]{:S(2)}) copy-start(bf16[4,128,128]{2,1,0:T(8,128)(2,1)} %get-tuple-element.26.own_ref) | copy-start | bytes 393220
  29.3 2.5 %collective-permute-start.7 = (bf16[256,128]{1,0:T(8,128)(2,1)S(1)}, bf16[256,128]{1,0:T(8,128)(2,1)S(1)}, u32[]{:S(2)}, u32[]{:S(2)}) collective-permute-start(bf16[256,128]{1,0:T(8,128)(2,1)S(1)} %get-tuple-element.36), channel_id=1, source_target_pairs={{0,1},{1,0},{2,3},{3,2},{4,5},{5,4},{6,7},{7,6},{8,9},{9,8},{10,11... | collective-permute-start | bytes 196616 | tf_op jit(solution)/shard_map/ppermute | solution.py:707
  31.8 11.1 %collective-permute-start.10 = (bf16[256,128]{1,0:T(8,128)(2,1)S(1)}, bf16[256,128]{1,0:T(8,128)(2,1)S(1)}, u32[]{:S(2)}, u32[]{:S(2)}) collective-permute-start(bf16[256,128]{1,0:T(8,128)(2,1)S(1)} %add_convert_fusion.1), channel_id=1, source_target_pairs={{0,24},{4,28},{8,16},{12,20},{16,8},{20,12},{24,0},{28,4},{1,25},{... | collective-permute-start | bytes 196616 | tf_op jit(solution)/shard_map/ppermute | solution.py:707
  35.3 8.4 %collective-permute-start.9 = (bf16[256,128]{1,0:T(8,128)(2,1)S(1)}, bf16[256,128]{1,0:T(8,128)(2,1)S(1)}, u32[]{:S(2)}, u32[]{:S(2)}) collective-permute-start(bf16[256,128]{1,0:T(8,128)(2,1)S(1)} %add_convert_fusion.1), channel_id=1, source_target_pairs={{0,16},{4,20},{8,24},{12,28},{16,0},{20,4},{24,8},{28,12},{1,17},{... | collective-permute-start | bytes 196616 | tf_op jit(solution)/shard_map/ppermute | solution.py:707
  38.6 5.2 %collective-permute-start.8 = (bf16[256,128]{1,0:T(8,128)(2,1)S(1)}, bf16[256,128]{1,0:T(8,128)(2,1)S(1)}, u32[]{:S(2)}, u32[]{:S(2)}) collective-permute-start(bf16[256,128]{1,0:T(8,128)(2,1)S(1)} %add_convert_fusion.1), channel_id=1, source_target_pairs={{0,8},{4,12},{8,0},{12,4},{16,24},{20,28},{24,16},{28,20},{1,9},{5... | collective-permute-start | bytes 196616 | tf_op jit(solution)/shard_map/ppermute | solution.py:707
  38.7 24.3 %all-to-all-start = ((bf16[8,3,128,128]{3,2,1,0:T(8,128)(2,1)}), bf16[8,3,128,128]{3,2,1,0:T(8,128)(2,1)S(1)}, u32[]{:S(2)}, u32[]{:S(2)}) async-start(bf16[8,3,128,128]{3,2,1,0:T(8,128)(2,1)} %grads.1), calls=%async_computation | async-start | bytes 1572864 | tf_op jit(solution)/shard_map/all_to_all | solution.py:725
  43.8 7.6 %collective-permute-start.11 = (bf16[4,256,128]{2,1,0:T(8,128)(2,1)S(1)}, bf16[4,256,128]{2,1,0:T(8,128)(2,1)S(1)}, u32[]{:S(2)}, u32[]{:S(2)}) collective-permute-start(bf16[4,256,128]{2,1,0:T(8,128)(2,1)S(1)} %pad_maximum_fusion), channel_id=1, source_target_pairs={{0,2},{1,3},{2,0},{3,1},{4,6},{5,7},{6,4},{7,5},{8,10},{9,11},{10,... | collective-permute-start | bytes 786440 | tf_op jit(solution)/shard_map/ppermute | solution.py:707
  51.4 9.6 %collective-permute-start.12 = (bf16[4,256,128]{2,1,0:T(8,128)(2,1)S(1)}, bf16[4,256,128]{2,1,0:T(8,128)(2,1)S(1)}, u32[]{:S(2)}, u32[]{:S(2)}) collective-permute-start(bf16[4,256,128]{2,1,0:T(8,128)(2,1)S(1)} %add_convert_fusion.refs_0_), channel_id=1, source_target_pairs={{0,4},{4,0},{8,12},{12,8},{16,20},{20,16},{24,28},{28,24},{1,5},{5... | collective-permute-start | bytes 786440 | tf_op jit(solution)/shard_map/ppermute | solution.py:707
  52.5 8.5 %collective-permute-start.14 = (bf16[4,256,128]{2,1,0:T(8,128)(2,1)S(1)}, bf16[4,256,128]{2,1,0:T(8,128)(2,1)S(1)}, u32[]{:S(2)}, u32[]{:S(2)}) collective-permute-start(bf16[4,256,128]{2,1,0:T(8,128)(2,1)S(1)} %add_convert_fusion.refs_0_), channel_id=1, source_target_pairs={{0,1},{1,0},{2,3},{3,2},{4,5},{5,4},{6,7},{7,6},{8,9},{9,8},{10,11... | collective-permute-start | bytes 786440 | tf_op jit(solution)/shard_map/ppermute | solution.py:707
  61.0 1.5 %collective-permute-start.13 = (bf16[4,256,128]{2,1,0:T(8,128)(2,1)S(1)}, bf16[4,256,128]{2,1,0:T(8,128)(2,1)S(1)}, u32[]{:S(2)}, u32[]{:S(2)}) collective-permute-start(bf16[4,256,128]{2,1,0:T(8,128)(2,1)S(1)} %collective-permute-done.12.refs_0_), channel_id=1, source_target_pairs={{0,1},{1,0},{2,3},{3,2},{4,5},{5,4},{6,7},{7,6},{8,9},{9,8},{10,11... | collective-permute-start | bytes 786440 | tf_op jit(solution)/shard_map/ppermute | solution.py:707
